TPU v7x, 256 devices: a whole 4x4x8 slice. The times are simulated.
256 devices in a mesh: grp: 2 (over y_lo), row: 16 (over z, core), col: 8 (over y_hi, x).
Axes of the slice: x: 4, y: 4 (y_hi: 2, y_lo: 2; y = y_hi * 2 + y_lo), z: 8, core: 2. Of those that a mesh axis runs over, the one named last changes fastest.
Arguments:
- pair: float32 [2, 512, 512, 128], P('grp', 'row', 'col'), may hold values from -6 to 6
- pair_mask: int32 [2, 512], P('grp'), may hold values from 0 to 1, as said below
- prev_pair: float32 [2, 512, 512, 128], P('grp', 'row', 'col'), may hold values from -70 to 70
- diff_tokens: float32 [2, 32, 512, 768], P('grp', 'row', 'col'), may hold values from -6 to 6
- diff_mask: int32 [2, 512], P('grp'), may hold values from 0 to 1, as said below
- atom_feats: bfloat16 [2, 32, 2048, 128], P('grp', 'row', 'col'), may hold values from -6 to 6
- atom_token: int32 [2, 2048], P('grp', 'col'), may hold values from 0 to 511, as said below
- trunk_in: bfloat16 [2, 128, 640], replicated, may hold values from -0.5 to 0.5
- trunk_out: bfloat16 [2, 128, 128], replicated, may hold values from -0.5 to 0.5
- bias_weight: bfloat16 [128, 16], replicated, may hold values from -1000 to 1000
- atom_weight: bfloat16 [128, 768], replicated, may hold values from -0.5 to 0.5
- attn_in: bfloat16 [768, 3072], replicated, may hold values from -0.21875 to 0.21875
- attn_out: bfloat16 [768, 768], replicated, may hold values from -0.21875 to 0.21875
Outputs:
- pair_next: float32 [2, 512, 512, 128], P('grp', 'row', 'col')
- tokens_next: float32 [2, 32, 512, 768], P('grp', 'row', 'col')
Inputs may be any that keep to these rules, and one draw needn't show every extreme that they name: `pair_mask`: each complex's first tokens are 1 and the rest 0; the first token is always 1 and the last always 0. `diff_mask`: each complex's first tokens are 1 and the rest 0; the first token is always 1 and the last always 0. `atom_token`: atoms b * 256 to (b + 1) * 256 - 1 belong to tokens b * 64 to (b + 1) * 64 - 1, and every token has at least one atom.
All inputs are finite; a program needn't handle non-finite values.
Results may differ from a plain program's by a relative error of at most 0.015.
Values may be sent and summed in bfloat16 or wider, within the bound.
No kernel may reach another device: no remote copies, remote signals or barrier semaphores. Data moves between devices by JAX's collectives and lax.ppermute only.
A program may use at most 128 MiB of HBM per device.

v0:
```python
import jax
import jax.numpy as jnp
from jax import lax
from jax.sharding import PartitionSpec as P

EPSILON = 1e-05


def partner(value, axis, bit):
    mask = 2**bit
    pairs = [(source, source ^ mask) for source in range(lax.axis_size(axis))]
    return lax.ppermute(value, axis, pairs)


def layer_norm(values):
    centred = values - jnp.mean(values, axis=-1, keepdims=True)
    spread = jnp.mean(centred * centred, axis=-1, keepdims=True)
    return centred * lax.rsqrt(spread + EPSILON)


def project_pair(pair_in, pair_live, weight_in):
    width = pair_in.shape[-1]
    normed = layer_norm(pair_in).astype(jnp.bfloat16)
    projected = jnp.dot(normed, weight_in, preferred_element_type=jnp.float32)
    left_side = (
        pair_live * jax.nn.sigmoid(projected[..., :width]) * projected[..., width : 2 * width]
    ).astype(jnp.bfloat16)
    right_side = (
        pair_live
        * jax.nn.sigmoid(projected[..., 2 * width : 3 * width])
        * projected[..., 3 * width : 4 * width]
    ).astype(jnp.bfloat16)
    gate_vals = jax.nn.sigmoid(projected[..., 4 * width :])
    return (left_side, right_side, gate_vals)


def finish_pair(pair_in, summed, gate_vals, weight_out):
    summed_norm = layer_norm(summed).astype(jnp.bfloat16)
    return pair_in + gate_vals * jnp.dot(
        summed_norm, weight_out, preferred_element_type=jnp.float32
    )


def outgoing_update(pair_in, pair_live, weight_in, weight_out):
    left_side, right_side, gate_vals = project_pair(pair_in, pair_live, weight_in)
    right_all = lax.all_gather(right_side, "row", axis=0, tiled=True)
    term = jnp.einsum("ikc,jkc->jic", left_side, right_all, preferred_element_type=jnp.float32)
    summed = lax.psum_scatter(
        term.astype(jnp.bfloat16).astype(jnp.float32).astype(jnp.bfloat16),
        "col",
        scatter_dimension=0,
        tiled=True,
    ).astype(jnp.float32)
    return finish_pair(pair_in, jnp.transpose(summed, (1, 0, 2)), gate_vals, weight_out)


def incoming_update(pair_in, pair_live, weight_in, weight_out):
    left_side, right_side, gate_vals = project_pair(pair_in, pair_live, weight_in)
    left_all = lax.all_gather(left_side, "col", axis=1, tiled=True)
    term = jnp.einsum("kic,kjc->ijc", left_all, right_side, preferred_element_type=jnp.float32)
    summed = lax.psum_scatter(
        term.astype(jnp.bfloat16).astype(jnp.float32).astype(jnp.bfloat16),
        "row",
        scatter_dimension=0,
        tiled=True,
    ).astype(jnp.float32)
    return finish_pair(pair_in, summed, gate_vals, weight_out)


def bias_tile(pair_in, bias_weight):
    projected = jnp.dot(
        layer_norm(pair_in).astype(jnp.bfloat16), bias_weight, preferred_element_type=jnp.float32
    )
    return jnp.transpose(projected.astype(jnp.bfloat16), (2, 1, 0))


def on_device(
    pair,
    pair_mask,
    prev_pair,
    diff_tokens,
    diff_mask,
    atom_feats,
    atom_token,
    trunk_in,
    trunk_out,
    bias_weight,
    atom_weight,
    attn_in,
    attn_out,
):
    row_index = lax.axis_index("row")
    col_index = lax.axis_index("col")
    pair_here = pair[0]
    rows_here = pair_here.shape[0]
    cols_here = pair_here.shape[1]
    live_all = pair_mask[0].astype(jnp.float32)
    live_rows = lax.dynamic_slice_in_dim(live_all, row_index * rows_here, rows_here, 0)
    live_cols = lax.dynamic_slice_in_dim(live_all, col_index * cols_here, cols_here, 0)
    pair_live = (live_rows[:, None] * live_cols[None, :])[..., None]
    first_pass = outgoing_update(pair_here, pair_live, trunk_in[0], trunk_out[0])
    pair_done = incoming_update(first_pass, pair_live, trunk_in[1], trunk_out[1])
    tokens_here = diff_tokens[0]
    samples_here, tok_here, width = tokens_here.shape
    heads = bias_weight.shape[1]
    head_size = width // heads
    local_ids = atom_token[0] - col_index * tok_here
    onehot_f = (local_ids[None, :] == jnp.arange(tok_here, dtype=jnp.int32)[:, None]).astype(
        jnp.float32
    )
    atom_count = jnp.sum(onehot_f, axis=1)
    pooled_sum = jnp.einsum(
        "ta,sac->stc",
        onehot_f.astype(jnp.bfloat16),
        atom_feats[0],
        preferred_element_type=jnp.float32,
    )
    pooled = (pooled_sum / atom_count[None, :, None]).astype(jnp.bfloat16)
    start = tokens_here + jnp.dot(pooled, atom_weight, preferred_element_type=jnp.float32)
    normed = layer_norm(start).astype(jnp.bfloat16)
    projected = jnp.dot(normed, attn_in, preferred_element_type=jnp.float32)
    queries = projected[..., :width].astype(jnp.bfloat16)
    keys_here = (
        projected[..., width : 2 * width]
        .astype(jnp.bfloat16)
        .reshape(samples_here, tok_here, heads, head_size)
    )
    values_here = (
        projected[..., 2 * width : 3 * width]
        .astype(jnp.bfloat16)
        .reshape(samples_here, tok_here, heads, head_size)
    )
    gate_vals = jax.nn.sigmoid(projected[..., 3 * width :])
    prev_here = prev_pair[0]
    other_pair = partner(prev_here, "grp", 0)
    tile_other = bias_tile(other_pair, bias_weight)
    bias_full = lax.all_gather(tile_other, "row", axis=2, tiled=True)
    queries_all = lax.all_gather(queries, "col", axis=1, tiled=True)
    tok_total = queries_all.shape[1]
    query_heads = queries_all.reshape(samples_here, tok_total, heads, head_size)
    scale = head_size ** (-0.5)
    scores = (
        jnp.einsum("sihd,sjhd->shji", query_heads, keys_here, preferred_element_type=jnp.float32)
        * scale
    )
    scores = scores + bias_full[None].astype(jnp.float32)
    key_live = lax.dynamic_slice_in_dim(diff_mask[0], col_index * tok_here, tok_here, 0) > 0
    masked = jnp.where(key_live[None, None, :, None], scores, -1e30)
    local_top = jnp.max(masked, axis=2)
    global_top = lax.pmax(local_top.astype(jnp.bfloat16), "col").astype(local_top.dtype)
    weights = jnp.exp(masked - global_top[:, :, None, :])
    total_part = jnp.transpose(jnp.sum(weights, axis=2), (0, 2, 1))
    mixed_part = jnp.einsum(
        "shji,sjhd->sihd",
        weights.astype(jnp.bfloat16),
        values_here,
        preferred_element_type=jnp.float32,
    )
    mixed_part = mixed_part.reshape(samples_here, tok_total, width)
    mixed_sum, total_sum = (
        lax.psum_scatter(
            mixed_part.astype(jnp.bfloat16), "col", scatter_dimension=1, tiled=True
        ).astype(jnp.float32),
        lax.psum_scatter(
            total_part.astype(jnp.bfloat16), "col", scatter_dimension=1, tiled=True
        ).astype(jnp.float32),
    )
    attended = mixed_sum.reshape(samples_here, tok_here, heads, head_size) / total_sum[..., None]
    blended = (gate_vals * attended.reshape(samples_here, tok_here, width)).astype(jnp.bfloat16)
    tokens_done = start + jnp.dot(blended, attn_out, preferred_element_type=jnp.float32)
    return (pair_done[None], tokens_done[None])


def solution(mesh):
    placed = (
        P("grp", "row", "col", None),
        P("grp", None),
        P("grp", "row", "col", None),
        P("grp", "row", "col", None),
        P("grp", None),
        P("grp", "row", "col", None),
        P("grp", "col"),
        P(),
        P(),
        P(),
        P(),
        P(),
        P(),
    )
    return jax.shard_map(
        on_device,
        mesh=mesh,
        in_specs=placed,
        out_specs=(P("grp", "row", "col", None), P("grp", "row", "col", None)),
        check_vma=False,
    )
```

profile of v0, /device:TPU:1, one launch (start us, length us, event | category | flops | bytes accessed | tf_op | source)
XLA Modules:
  0.0 637.9 jit_solution(3344913613290112755)
XLA Ops:
  7.2 1.7 reduce_sum.126
  8.9 1.9 fusion.58
  10.8 0.7 convert_element_type.118
  11.6 2.3 fusion.60
  14.0 2.3 copy-done.2
  16.3 1.4 fusion.40
  17.8 1.6 copy.106
  19.4 58.6 %all-gather.5.cloned.1.call-done = bf16[512,64,128]{2,1,0:T(8,128)(2,1)} async-done(((bf16[32,64,128]{2,1,0:T(8,128)(2,1)}), bf16[512,64,128]{2,1,0:T(8,128)(2,1)}) %all-gather.5.cloned.1.call-update) | async-done | bytes 8388624 | tf_op jit(solution)/shard_map/all_gather | solution.py:46
  78.0 23.7 %copy.105 = bf16[512,64,128]{1,0,2:T(8,128)(2,1)} copy(bf16[512,64,128]{2,1,0:T(8,128)(2,1)} %all-gather.5.cloned.1.call-done) | data formatting | bytes 16777216 | tf_op jit(solution)/shard_map/all_gather | solution.py:46
  101.8 10.7 %convert_bitcast_fusion.1 = bf16[512,32,128]{0,1,2:T(8,128)(2,1)} fusion(bf16[512,64,128]{1,0,2:T(8,128)(2,1)} %copy.105, bf16[32,64,128]{1,0,2:T(8,128)(2,1)S(1)} %copy.106), kind=kOutput, calls=%fused_computation.5 | convolution fusion | flops 270532608 | bytes 13107200 | tf_op jit(solution)/shard_map/ikc,jkc->jic/dot_general | solution.py:47
  112.5 9.1 %copy.107 = bf16[512,32,128]{2,1,0:T(8,128)(2,1)} copy(bf16[512,32,128]{0,1,2:T(8,128)(2,1)} %convert_bitcast_fusion.1) | data formatting | bytes 8388608 | tf_op jit(solution)/shard_map/convert_element_type | solution.py:49
  121.7 0.6 copy-done.16
  122.4 0.2 copy-done.11
  122.7 0.4 fusion.107
  123.4 0.5 copy-done.7
  123.9 4.3 fusion.112
  128.3 0.8 fusion.105
  129.1 1.3 collective-permute-start
  130.4 34.2 %collective-permute-done = f32[32,64,128]{2,1,0:T(8,128)S(1)} collective-permute-done((f32[32,64,128]{2,1,0:T(8,128)}, f32[32,64,128]{2,1,0:T(8,128)S(1)}, u32[]{:S(2)}, u32[]{:S(2)}) %collective-permute-start) | collective-permute-done | bytes 1048608 | tf_op jit(solution)/shard_map/ppermute | solution.py:12
  164.6 0.3 reduce_sum.137
  164.9 0.6 multiply_reduce_fusion
  165.6 1.4 fusion.22
  167.0 0.2 all-gather.7.cloned.1.call-start
  167.3 52.5 %reduce-scatter.7.cloned.1.call-done = bf16[64,32,128]{2,1,0:T(8,128)(2,1)} async-done(((bf16[512,32,128]{2,1,0:T(8,128)(2,1)}), bf16[64,32,128]{2,1,0:T(8,128)(2,1)}) %reduce-scatter.7.cloned.1.call-update) | async-done | bytes 524304 | tf_op jit(solution)/shard_map/reduce_scatter | solution.py:48
  219.8 1.4 bitcast_reduce_fusion
  221.3 1.7 fusion.55
  223.2 1.7 fusion.56
  224.9 1.8 fusion.106
  226.7 0.6 multiply_reduce_fusion.1
  227.3 0.3 copy-done.5
  227.6 1.0 fusion.62
  228.7 2.3 copy-done.1
  231.0 1.6 fusion.27
  232.7 0.9 copy.127
  233.6 0.9 copy.126
  234.5 0.7 compare_bitcast_fusion
  235.2 41.9 %all-gather.9.cloned.1.call-done = bf16[2,512,768]{2,1,0:T(8,128)(2,1)} async-done(((bf16[2,64,768]{2,1,0:T(8,128)(2,1)}), bf16[2,512,768]{2,1,0:T(8,128)(2,1)}) %all-gather.9.cloned.1.call-update) | async-done | bytes 1572880 | tf_op jit(solution)/shard_map/all_gather | solution.py:138
  277.2 2.7 copy.120
  279.8 39.6 %all-gather.11.cloned.1.call-done = bf16[16,64,512]{1,0,2:T(8,128)(2,1)} async-done(((bf16[16,64,32]{1,0,2:T(8,128)(2,1)}), bf16[16,64,512]{1,0,2:T(8,128)(2,1)}) %all-gather.11.cloned.1.call-update) | async-done | bytes 1048592 | tf_op jit(solution)/shard_map/all_gather | solution.py:137
  319.4 3.3 copy.122
  322.7 1.6 convert_element_type.139
  324.5 4.1 fusion.4
  328.6 34.8 %pmax.7 = bf16[2,16,512]{2,1,0:T(8,128)(2,1)S(1)} all-reduce(bf16[2,16,512]{2,1,0:T(8,128)(2,1)S(1)} %get-tuple-element.15), channel_id=1, replica_groups=mesh['grp'=2,'row'=16,'col'=8] {'col'}, use_global_device_ids=true, to_apply=%region_16.17 | all-reduce | flops 16384 | bytes 65536 | tf_op jit(solution)/shard_map/pmax | solution.py:150
  363.4 4.0 fusion.2
  367.4 0.9 copy.128
  368.4 0.8 reshape.146
  369.2 4.9 fusion.12
  374.2 2.7 copy.124
  376.9 0.3 reduce-scatter.9.cloned.1.call-start
  377.2 1.6 copy.113
  378.8 17.4 %all-gather.7.cloned.1.call-done = bf16[32,512,128]{2,1,0:T(8,128)(2,1)} async-done(((bf16[32,64,128]{2,1,0:T(8,128)(2,1)}), bf16[32,512,128]{2,1,0:T(8,128)(2,1)}) %all-gather.7.cloned.1.call-update) | async-done | bytes 4194320 | tf_op jit(solution)/shard_map/all_gather | solution.py:59
  396.2 7.9 %copy.114 = bf16[32,512,128]{1,0,2:T(8,128)(2,1)} copy(bf16[32,512,128]{2,1,0:T(8,128)(2,1)} %all-gather.7.cloned.1.call-done) | data formatting | bytes 8388608 | tf_op jit(solution)/shard_map/all_gather | solution.py:59
  404.1 7.8 %convert_bitcast_fusion = bf16[512,64,128]{0,1,2:T(8,128)(2,1)} fusion(bf16[32,64,128]{1,0,2:T(8,128)(2,1)S(1)} %copy.113, bf16[32,512,128]{1,0,2:T(8,128)(2,1)} %copy.114), kind=kOutput, calls=%fused_computation | convolution fusion | flops 272629760 | bytes 13107200 | tf_op jit(solution)/shard_map/kic,kjc->ijc/dot_general | solution.py:60
  411.9 13.6 %copy.115 = bf16[512,64,128]{2,1,0:T(8,128)(2,1)} copy(bf16[512,64,128]{0,1,2:T(8,128)(2,1)} %convert_bitcast_fusion) | data formatting | bytes 16777216 | tf_op jit(solution)/shard_map/convert_element_type | solution.py:62
  425.6 45.5 %reduce-scatter.13.cloned.1.call-done = bf16[64,32]{1,0:T(8,128)(2,1)} async-done(((bf16[512,32]{1,0:T(8,128)(2,1)}), bf16[64,32]{1,0:T(8,128)(2,1)}) %reduce-scatter.13.cloned.1.call-update) | async-done | bytes 4112
  471.1 0.8 reshape.147
  472.1 0.3 div.98
  472.5 1.2 div.99
  473.7 80.9 %reduce-scatter.11.cloned.1.call-done = bf16[2,64,768]{2,1,0:T(8,128)(2,1)} async-done(((bf16[2,512,768]{2,1,0:T(8,128)(2,1)}), bf16[2,64,768]{2,1,0:T(8,128)(2,1)}) %reduce-scatter.11.cloned.1.call-update) | async-done | bytes 196624 | tf_op jit(solution)/shard_map/reduce_scatter | solution.py:161
  554.5 2.5 fusion.20
  557.0 67.8 %reduce-scatter.9.cloned.1.call-done = bf16[32,64,128]{2,1,0:T(8,128)(2,1)} async-done(((bf16[512,64,128]{2,1,0:T(8,128)(2,1)}), bf16[32,64,128]{2,1,0:T(8,128)(2,1)}) %reduce-scatter.9.cloned.1.call-update) | async-done | bytes 524304 | tf_op jit(solution)/shard_map/reduce_scatter | solution.py:61
  624.8 1.4 convert_reduce_fusion
  626.2 1.7 fusion.25
  628.0 3.1 fusion.16
  (69 shorter events, 1.7 us)
Async XLA Ops:
  7.2 547.4 %copy-start = (bf16[768,768]{1,0:T(8,128)(2,1)S(1)}, bf16[768,768]{1,0:T(8,128)(2,1)}, u32[]{:S(2)}) copy-start(bf16[768,768]{1,0:T(8,128)(2,1)} %param.25) | copy-start | bytes 3538948
  7.2 70.9 %all-gather.5.cloned.1.call-start = ((), (), s32[]{:S(2)}) async-start(), calls=%async_computation.4 | async-start | bytes 8912896 | tf_op jit(solution)/shard_map/all_gather | solution.py:46
  14.0 2.4 copy-start.2
  17.8 202.0 %reduce-scatter.7.cloned.1.call-start = ((), (), s32[]{:S(2)}) async-start(), calls=%async_computation.5 | async-start | bytes 4718592 | tf_op jit(solution)/shard_map/reduce_scatter | solution.py:48
  121.6 0.7 copy-start.16
  121.6 1.0 copy-start.11
  121.6 1.1 copy-start.13
  121.6 1.1 copy-start.14
  121.6 155.5 %all-gather.9.cloned.1.call-start = ((), (), s32[]{:S(2)}) async-start(), calls=%async_computation.8 | async-start | bytes 1769472 | tf_op jit(solution)/shard_map/all_gather | solution.py:138
  123.2 0.8 copy-start.7
  123.9 41.7 %copy-start.15 = (bf16[128,16]{0,1:T(8,128)(2,1)S(1)}, bf16[128,16]{0,1:T(8,128)(2,1)}, u32[]{:S(2)}) copy-start(bf16[128,16]{0,1:T(8,128)(2,1)} %param.22) | copy-start | bytes 12292
  128.3 96.6 %copy-start.3 = (f32[1,32,64,128]{3,2,1,0:T(8,128)S(1)}, f32[1,32,64,128]{3,2,1,0:T(8,128)}, u32[]{:S(2)}) copy-start(f32[1,32,64,128]{3,2,1,0:T(8,128)} %param.13) | copy-start | bytes 3145732
  129.1 190.4 %all-gather.11.cloned.1.call-start = ((), (), s32[]{:S(2)}) async-start(), calls=%async_computation.9 | async-start | bytes 2228224 | tf_op jit(solution)/shard_map/all_gather | solution.py:137
  129.1 35.5 %collective-permute-start = (f32[32,64,128]{2,1,0:T(8,128)}, f32[32,64,128]{2,1,0:T(8,128)S(1)}, u32[]{:S(2)}, u32[]{:S(2)}) collective-permute-start(f32[32,64,128]{2,1,0:T(8,128)} %bitcast.123), channel_id=1, source_target_pairs={{0,128},{128,0},{1,129},{129,1},{2,130},{130,2},{3,131},{131,3},{4... | collective-permute-start | bytes 3145736 | tf_op jit(solution)/shard_map/ppermute | solution.py:12
  167.0 229.2 %all-gather.7.cloned.1.call-start = ((), (), s32[]{:S(2)}) async-start(), calls=%async_computation.6 | async-start | bytes 4718592 | tf_op jit(solution)/shard_map/all_gather | solution.py:59
  223.0 4.6 copy-start.12
  226.7 1.0 copy-start.5
  228.7 2.3 copy-start.1
  231.0 1.7 copy-start.9
  232.6 238.5 %reduce-scatter.13.cloned.1.call-start = ((), (), s32[]{:S(2)}) async-start(), calls=%async_computation.11 | async-start | bytes 147456
  322.7 1.7 copy-start.4
  363.4 4.1 copy-start.10
  369.2 185.3 %reduce-scatter.11.cloned.1.call-start = ((), (), s32[]{:S(2)}) async-start(), calls=%async_computation.10 | async-start | bytes 1769472 | tf_op jit(solution)/shard_map/reduce_scatter | solution.py:161
  374.2 3.0 copy-start.8
  376.9 248.0 %reduce-scatter.9.cloned.1.call-start = ((), (), s32[]{:S(2)}) async-start(), calls=%async_computation.7 | async-start | bytes 8912896 | tf_op jit(solution)/shard_map/reduce_scatter | solution.py:61
  425.6 202.4 %copy-start.6 = (f32[32,64,128]{2,1,0:T(8,128)S(1)}, f32[32,64,128]{2,1,0:T(8,128)}, u32[]{:S(2)}) copy-start(f32[32,64,128]{2,1,0:T(8,128)} %copy-done.5) | copy-start | bytes 3145732
  425.6 202.4 %copy-start.17 = (bf16[2,128,128]{2,1,0:T(8,128)(2,1)S(1)}, bf16[2,128,128]{2,1,0:T(8,128)(2,1)}, u32[]{:S(2)}) copy-start(bf16[2,128,128]{2,1,0:T(8,128)(2,1)} %param.21) | copy-start | bytes 196612
Sparse Core Ops, SparseCore 0:
  17.9 60.1 all-gather.4
  121.8 97.9 reduce-scatter.6
  222.3 54.7 all-gather.8
  278.8 40.5 all-gather.10
  321.9 74.2 all-gather.6
  399.9 71.2 reduce-scatter.12
  475.2 79.2 reduce-scatter.10
  557.1 67.7 reduce-scatter.8
where the time goes:
time: 642 us; the launch traced here: 638 us
  waiting for transfers between devices  439 us (68%)
  local copies, waits for them, and re-layouts  80.1 us (12%)
  matrix products  44.4 us (7%)
  blocking collectives  34.8 us (5%)
  other arithmetic  23.5 us (4%)
  between operations  14.5 us (2%)
    reduce_scatter x1, waiting for transfers between devices, on_device(): lax.psum_scatter(mixed_part.astype(jnp.bfloat16), 'col', scatter_dimensio...  80.9 us
    reduce_scatter x1, waiting for transfers between devices, incoming_update(): lax.psum_scatter(term.astype(jnp.bfloat16).astype(jnp.float32).astype(jnp...  67.8 us
    all_gather x1, waiting for transfers between devices, outgoing_update(): right_all = lax.all_gather(right_side, 'row', axis=0, tiled=True)  58.6 us
    reduce_scatter x1, waiting for transfers between devices, outgoing_update(): lax.psum_scatter(term.astype(jnp.bfloat16).astype(jnp.float32).astype(jnp...  52.5 us
    unnamed x9, waiting for transfers between devices  45.7 us
    all_gather x1, waiting for transfers between devices, on_device(): queries_all = lax.all_gather(queries, 'col', axis=1, tiled=True)  41.9 us
    all_gather x1, waiting for transfers between devices, on_device(): bias_full = lax.all_gather(tile_other, 'row', axis=2, tiled=True)  39.6 us
    pmax x1, blocking collectives, on_device(): lax.pmax(local_top.astype(jnp.bfloat16), 'col').astype(local_top.dtype)  34.8 us
  transfers between devices with their start and end apart: 9, of which 9 were waited for; matrix products, arithmetic and copies ran while one was open for 13% of the time, Pallas kernels for 0%

commit v1 on v0

v1 whole, which is shorter than its diff:
```python
import functools

import jax
import jax.numpy as jnp
from jax import lax
from jax.experimental import pallas as pl
from jax.experimental.pallas import tpu as pltpu
from jax.sharding import Mesh, PartitionSpec as P

EPSILON = 1e-05
F32, BF16 = jnp.float32, jnp.bfloat16
ROWS, COLS, TOK, C = 32, 64, 512, 128
HEADS, HEAD = 16, 48
VMEM_LIMIT = 48 * 2**20
NT = (((1,), (1,)), ((), ()))
TN = (((0,), (0,)), ((), ()))


def dot(left, right, dims=(((1,), (0,)), ((), ()))):
    return lax.dot_general(left, right, dims, preferred_element_type=F32)


def layer_norm(values, axis=-1):
    centred = values - jnp.mean(values, axis=axis, keepdims=True)
    spread = jnp.mean(centred * centred, axis=axis, keepdims=True)
    return centred * lax.rsqrt(spread + EPSILON)


def low_lanes():
    return lax.broadcasted_iota(jnp.int32, (1, 128), 1) < 64


def swap_halves(first, second):
    low = low_lanes()
    axis = first.ndim - 1
    return (
        jnp.where(low, first, pltpu.roll(second, 64, axis)),
        jnp.where(low, pltpu.roll(first, 64, axis), second),
    )


def pair_step(pair_ref, step):
    return pair_ref[:, step].reshape(2 * COLS, C)


def project_step(values, step, length, row0, col0, weight_ref, spread_ref):
    normed = layer_norm(values).astype(BF16)
    lane = lax.broadcasted_iota(jnp.int32, (1, 128), 1)
    half = (lane >= 64).astype(jnp.int32)
    row = row0 + half * 16 + step
    col = col0 + lane - half * 64
    live = jnp.logical_and(row < length, col < length).astype(F32)
    projected = dot(weight_ref[...], normed, NT)
    left = live * jax.nn.sigmoid(projected[:C]) * projected[C : 2 * C]
    right = live * jax.nn.sigmoid(projected[2 * C : 3 * C]) * projected[3 * C :]
    spread_ref[pl.ds(step, C, stride=32), :] = left
    spread_ref[pl.ds(step + 16, C, stride=32), :] = right


def mask_length(mask_ref):
    return jnp.sum(mask_ref[...])


def project_kernel(place_ref, mask_ref, pair_ref, weight_ref, out_ref, spread_ref):
    length = mask_length(mask_ref)

    def body(step, carry):
        project_step(
            pair_step(pair_ref, step), step, length, place_ref[0], place_ref[1], weight_ref, spread_ref
        )
        return carry

    lax.fori_loop(0, 16, body, 0, unroll=4)
    out_ref[...] = spread_ref[...].astype(BF16).reshape(C, 32, 128)


def gate_kernel(pair_ref, weight_ref, out_ref):
    def body(step, carry):
        normed = layer_norm(pair_step(pair_ref, step)).astype(BF16)
        out_ref[:, step] = jax.nn.sigmoid(dot(normed, weight_ref[...])).reshape(2, COLS, C)
        return carry

    lax.fori_loop(0, 16, body, 0, unroll=4)


def product_kernel(recv_ref, out_ref, left_ref, right_ref, *, outgoing):
    for block in range(4):
        lanes = slice(block * 128, (block + 1) * 128)
        for side, dest_ref in ((0, left_ref), (1, right_ref)):
            rows = slice(side * 16, side * 16 + 16)
            first, second = swap_halves(
                recv_ref[:, 2 * block, rows, :].astype(F32),
                recv_ref[:, 2 * block + 1, rows, :].astype(F32),
            )
            dest_ref[:, 0, :, lanes] = first.astype(BF16)
            dest_ref[:, 1, :, lanes] = second.astype(BF16)
    left = left_ref[...].reshape(TOK, TOK)
    right = right_ref[...].reshape(TOK, TOK)
    for block in range(4):
        lanes = slice(block * 128, (block + 1) * 128)
        if outgoing:
            summed = dot(left, right[lanes], NT)
        else:
            summed = dot(left, right[:, lanes], TN)
        summed = summed.reshape(16, 2, 16, 128)
        first, second = swap_halves(summed[:, 0], summed[:, 1])
        out_ref[:, 2 * block] = first.astype(BF16)
        out_ref[:, 2 * block + 1] = second.astype(BF16)


def finish_step(recv_f32_ref, pair_ref, gate_ref, weight_ref, step):
    summed = recv_f32_ref[pl.ds(step, C, stride=16), :]
    normed = layer_norm(summed, 0).astype(BF16)
    update = dot(normed, weight_ref[...], TN)
    return pair_step(pair_ref, step) + pair_step(gate_ref, step) * update


def finish_project_kernel(
    place_ref, mask_ref, recv_ref, pair_ref, gate_ref, out_weight_ref, in_weight_ref,
    pair_out_ref, out_ref, recv_f32_ref, spread_ref,
):
    length = mask_length(mask_ref)
    recv_f32_ref[...] = recv_ref[...].astype(F32).reshape(C * 16, 128)

    def body(step, carry):
        values = finish_step(recv_f32_ref, pair_ref, gate_ref, out_weight_ref, step)
        pair_out_ref[:, step] = values.reshape(2, COLS, C)
        project_step(values, step, length, place_ref[0], place_ref[1], in_weight_ref, spread_ref)
        return carry

    lax.fori_loop(0, 16, body, 0, unroll=4)
    out_ref[...] = spread_ref[...].astype(BF16).reshape(C, 32, 128)


def finish_kernel(recv_ref, pair_ref, gate_ref, out_weight_ref, pair_out_ref, recv_f32_ref):
    recv_f32_ref[...] = recv_ref[...].astype(F32).reshape(C * 16, 128)

    def body(step, carry):
        values = finish_step(recv_f32_ref, pair_ref, gate_ref, out_weight_ref, step)
        pair_out_ref[:, step] = values.reshape(2, COLS, C)
        return carry

    lax.fori_loop(0, 16, body, 0, unroll=4)


def bias_kernel(prev_ref, weight_ref, out_ref, spread_ref):
    def body(step, carry):
        normed = layer_norm(pair_step(prev_ref, step)).astype(BF16)
        spread_ref[pl.ds(step, HEADS, stride=16), :] = dot(weight_ref[...], normed, NT)
        return carry

    lax.fori_loop(0, 16, body, 0, unroll=4)
    out_ref[...] = spread_ref[...].astype(BF16).reshape(HEADS, 16, 128)


def tokens_kernel(
    place_ref, tokens_ref, atoms_ref, ids_ref, atom_weight_ref, weight_ref, bias_ref,
    start_ref, gate_ref, out_ref,
):
    tokens, atoms = 64, 256
    local = ids_ref[...] - place_ref[1]
    onehot = (lax.broadcasted_iota(jnp.int32, (tokens, atoms), 0) == local).astype(F32)
    count = jnp.sum(onehot, axis=1, keepdims=True)
    onehot = onehot.astype(BF16)
    pooled = [(dot(onehot, atoms_ref[sample]) / count).astype(BF16) for sample in range(2)]
    width = HEADS * HEAD
    start = tokens_ref[...].reshape(128, width) + dot(
        jnp.concatenate(pooled, axis=0), atom_weight_ref[...]
    )
    start_ref[...] = start
    normed = layer_norm(start).astype(BF16)
    for part in range(3):
        projected = dot(normed, weight_ref[:, part * width : (part + 1) * width])
        turned = jnp.transpose(projected, (1, 0)).astype(BF16)
        out_ref[:, part * HEAD : (part + 1) * HEAD, :] = turned.reshape(HEADS, HEAD, 128)
    out_ref[:, 3 * HEAD :, :] = bias_ref[...]
    gate_ref[...] = jax.nn.sigmoid(dot(normed, weight_ref[:, 3 * width :]))


def attention_kernel(mask_ref, recv_ref, bias_ref, out_ref, parts_ref, full_bias_ref, mixed_ref):
    live = lax.broadcasted_iota(jnp.int32, (1, TOK), 1) < mask_length(mask_ref)
    for block in range(4):
        lanes = slice(block * 128, (block + 1) * 128)
        first, second = swap_halves(
            bias_ref[:, 2 * block].astype(F32), bias_ref[:, 2 * block + 1].astype(F32)
        )
        full_bias_ref[:, 0, :, lanes] = first
        full_bias_ref[:, 1, :, lanes] = second
        for core in range(2):
            halves = swap_halves(
                recv_ref[core, 2 * block, : 3 * HEAD, :].astype(F32),
                recv_ref[core, 2 * block + 1, : 3 * HEAD, :].astype(F32),
            )
            for sample in range(2):
                parts_ref[2 * core + sample, : 3 * HEAD, lanes] = halves[sample].astype(BF16)
    parts_ref[:, 3 * HEAD :, :] = jnp.ones((4, 16, TOK), BF16)
    bias = full_bias_ref.reshape(TOK, TOK)

    def body(index, carry):
        query = parts_ref[index, :HEAD, :]
        key = parts_ref[index, HEAD : 2 * HEAD, :]
        value = parts_ref[index, 2 * HEAD :, :]
        scores = dot(query, key, TN) * (HEAD**-0.5) + bias[...]
        scores = jnp.where(live, scores, -1e30)
        top = jnp.max(scores, axis=1, keepdims=True)
        weights = jnp.exp(scores - top).astype(BF16)
        mixed = dot(value, weights, NT)
        mixed_ref[index] = mixed[:HEAD] / mixed[HEAD : HEAD + 1]
        return carry

    lax.fori_loop(0, 4, body, 0)
    for core in range(2):
        for block in range(4):
            lanes = slice(block * 128, (block + 1) * 128)
            first, second = swap_halves(mixed_ref[2 * core, :, lanes], mixed_ref[2 * core + 1, :, lanes])
            out_ref[core, 2 * block] = first.astype(BF16)
            out_ref[core, 2 * block + 1] = second.astype(BF16)


def tokens_out_kernel(recv_ref, gate_ref, start_ref, weight_ref, out_ref):
    width = HEADS * HEAD
    mixed = jnp.transpose(recv_ref[...].reshape(width, 128).astype(F32), (1, 0))
    blended = (gate_ref[...] * mixed).astype(BF16)
    out_ref[...] = (start_ref[...] + dot(blended, weight_ref[...])).reshape(2, 64, width)


def call(kernel, name, out_shape, scratch, *operands, smem=0, flops=10**8):
    shapes = jax.tree.leaves(out_shape)
    nbytes = sum(v.size * v.dtype.itemsize for v in (*operands, *shapes))
    vmem = pl.BlockSpec(memory_space=pltpu.VMEM)
    return pl.pallas_call(
        kernel,
        name=name,
        out_shape=out_shape,
        in_specs=[pl.BlockSpec(memory_space=pltpu.SMEM)] * smem + [vmem] * (len(operands) - smem),
        out_specs=jax.tree.map(lambda _: vmem, out_shape),
        scratch_shapes=scratch,
        cost_estimate=pl.CostEstimate(flops=flops, bytes_accessed=nbytes, transcendentals=0),
        compiler_params=pltpu.CompilerParams(vmem_limit_bytes=VMEM_LIMIT),
    )(*operands)


def shape(*dims, dtype=F32):
    return jax.ShapeDtypeStruct(dims, dtype)


ALL = ("z", "core", "col")
NEAR = ("core", "col")


def exchange(value, axes):
    return lax.all_to_all(value, axes, 0, 0, tiled=True)


def on_device(
    pair, pair_mask, prev_pair, diff_tokens, diff_mask, atom_feats, atom_token,
    trunk_in, trunk_out, bias_weight, atom_weight, attn_in, attn_out,
):
    row = lax.axis_index("z") * 2 + lax.axis_index("core")
    place = jnp.stack([row * ROWS, lax.axis_index("col") * COLS]).astype(jnp.int32)
    tile = (2, 16, COLS, C)
    send = shape(C, 32, 128, dtype=BF16)
    spread = pltpu.VMEM((C * 32, 128), F32)
    received = pltpu.VMEM((C * 16, 128), F32)
    square = pltpu.VMEM((16, 2, 16, TOK), BF16)
    weights = jnp.swapaxes(trunk_in, 1, 2)

    def product(operands, outgoing):
        gathered = exchange(operands, ALL).reshape(16, 8, 32, 128)
        result = call(
            functools.partial(product_kernel, outgoing=outgoing), "product",
            shape(16, 8, 16, 128, dtype=BF16), [square, square], gathered, flops=2 * TOK**3,
        )
        return exchange(result.reshape(C, 16, 128), ALL)

    pair0 = pair.reshape(tile)
    operands = call(
        project_kernel, "project", send, [spread],
        place, pair_mask, pair0, weights[0, : 4 * C], smem=1,
    )
    bias_here = call(
        bias_kernel, "bias", shape(HEADS, 16, 128, dtype=BF16), [pltpu.VMEM((HEADS * 16, 128), F32)],
        prev_pair.reshape(tile), jnp.swapaxes(bias_weight, 0, 1),
    )
    bias_other = lax.ppermute(bias_here, "grp", [(0, 1), (1, 0)])
    gate0 = call(gate_kernel, "gate", shape(*tile), [], pair0, trunk_in[0, :, 4 * C :])
    summed0 = product(operands, True)

    start, gate2, parts = call(
        tokens_kernel, "tokens_in",
        (shape(128, 768), shape(128, 768), shape(HEADS, 160, 128, dtype=BF16)), [],
        place, diff_tokens[0], atom_feats[0], atom_token, atom_weight, attn_in, bias_other, smem=1,
    )
    parts = exchange(parts, NEAR)
    bias_all = lax.all_gather(parts[:, 3 * HEAD :], "z", axis=0, tiled=True)

    pair1, operands = call(
        finish_project_kernel, "finish_project", (shape(*tile), send), [received, spread],
        place, pair_mask, summed0, pair0, gate0, trunk_out[0], weights[1, : 4 * C], smem=1,
    )
    gate1 = call(gate_kernel, "gate", shape(*tile), [], pair1, trunk_in[1, :, 4 * C :])
    summed1 = product(operands, False)

    mixed = call(
        attention_kernel, "attention", shape(2, 8, HEAD, 128, dtype=BF16),
        [
            pltpu.VMEM((4, 160, TOK), BF16),
            pltpu.VMEM((16, 2, 16, TOK), F32),
            pltpu.VMEM((4, HEAD, TOK), F32),
        ],
        diff_mask, parts.reshape(2, 8, 160, 128), bias_all.reshape(16, 8, 16, 128),
    )
    mixed = exchange(mixed.reshape(HEADS, HEAD, 128), NEAR)
    tokens_done = call(
        tokens_out_kernel, "tokens_out", shape(2, 64, 768), [], mixed, gate2, start, attn_out
    )

    pair2 = call(
        finish_kernel, "finish", shape(*tile), [received], summed1, pair1, gate1, trunk_out[1]
    )
    return (pair2.reshape(1, ROWS, COLS, C), tokens_done[None])


def solution(mesh):
    split = Mesh(mesh.devices.reshape(2, 8, 2, 8), ("grp", "z", "core", "col"))
    row = ("z", "core")
    placed = (
        P("grp", row, "col", None),
        P("grp", None),
        P("grp", row, "col", None),
        P("grp", row, "col", None),
        P("grp", None),
        P("grp", row, "col", None),
        P("grp", "col"),
        P(),
        P(),
        P(),
        P(),
        P(),
        P(),
    )
    return jax.shard_map(
        on_device,
        mesh=split,
        in_specs=placed,
        out_specs=(P("grp", row, "col", None), P("grp", row, "col", None)),
        check_vma=False,
    )
```

time: 642 us -> 206 us (0.32)
  waiting for transfers between devices: 439 us -> 38.7 us
  local copies, waits for them, and re-layouts: 80.1 us -> 9.76 us
  blocking collectives: 34.8 us -> 88.7 us
  matrix products: 44.4 us -> 0 us
  starting transfers between devices: 2.04 us -> 36.1 us
  Pallas kernels: 0 us -> 31.3 us
  other arithmetic: 23.5 us -> 0.08 us
  between operations: 14.5 us -> 0.87 us
    reduce_scatter x3 -> x0, waiting for transfers between devices: 201 us -> none  [the longest x1 80.9 us: on_device(): lax.psum_scatter(mixed_part.astype(jnp.bfloat16), 'col', scatter_dimensio...]
    all_gather x4 -> x0, waiting for transfers between devices: 158 us -> none  [the longest x1 58.6 us: outgoing_update(): right_all = lax.all_gather(right_side, 'row', axis=0, tiled=True)]
    all_to_all x0 -> x1, blocking collectives: none -> 47.8 us  [exchange(): return lax.all_to_all(value, axes, 0, 0, tiled=True)]
    unnamed x9 -> x0, waiting for transfers between devices: 45.7 us -> none
    dot_general x12 -> x0, matrix products: 44.4 us -> none  [the longest x1 10.7 us: outgoing_update(): jnp.einsum('ikc,jkc->jic', left_side, right_all, preferred_element_type=j...]
    all_gather x0 -> x1, blocking collectives: none -> 41 us  [on_device(): bias_all = lax.all_gather(parts[:, 3 * HEAD:], 'z', axis=0, tiled=True)]
    all_gather x4 -> x0, local copies, waits for them, and re-layouts: 37.6 us -> none  [the longest x1 23.7 us: outgoing_update(): right_all = lax.all_gather(right_side, 'row', axis=0, tiled=True)]
    all_to_all x0 -> x5, starting transfers between devices: none -> 35.6 us  [exchange(): return lax.all_to_all(value, axes, 0, 0, tiled=True)]
  transfers between devices with their start and end apart: 9 -> 6, of which waited for: 9 -> 5; matrix products, arithmetic and copies ran while one was open for 13% -> 0% of each run, Pallas kernels for 0% -> 11%
where the time goes in v1:
time: 206 us
  blocking collectives  88.7 us (43%)
  waiting for transfers between devices  38.7 us (19%)
  starting transfers between devices  36.1 us (18%)
  Pallas kernels  31.3 us (15%)
  local copies, waits for them, and re-layouts  9.76 us (5%)
    all_to_all x1, blocking collectives, exchange(): return lax.all_to_all(value, axes, 0, 0, tiled=True)  47.8 us
    all_gather x1, blocking collectives, on_device(): bias_all = lax.all_gather(parts[:, 3 * HEAD:], 'z', axis=0, tiled=True)  41 us
    all_to_all x5, starting transfers between devices, exchange(): return lax.all_to_all(value, axes, 0, 0, tiled=True)  35.6 us
    all_to_all x5, waiting for transfers between devices, exchange(): return lax.all_to_all(value, axes, 0, 0, tiled=True)  35.4 us
    pallas_call x11, Pallas kernels, call(): pl.pallas_call(kernel, name=name, out_shape=out_shape, in_specs=[pl.Block...  31.3 us
    unnamed x37, local copies, waits for them, and re-layouts  8.95 us
  transfers between devices with their start and end apart: 6, of which 5 were waited for; matrix products, arithmetic and copies ran while one was open for 0% of the time, Pallas kernels for 11%

profile of v1, /device:TPU:1, one launch (start us, length us, event | category | flops | bytes accessed | tf_op | source)
XLA Modules:
  0.0 205.6 jit_solution(16279283660556919553)
XLA Ops:
  0.6 0.0 copy-start.3
  0.6 0.0 copy-start.14
  0.7 0.0 copy-start.11
  0.7 0.0 copy-start.16
  0.7 1.3 copy.16
  2.0 0.1 pad_add_fusion.place_ref
  2.1 0.0 copy-start
  2.1 1.2 copy-done
  3.3 0.0 copy-start.12
  3.3 0.7 copy-done.12
  4.0 0.0 copy-start.5
  4.0 0.0 copy-start.10
  4.0 4.4 %project.1 = bf16[128,32,128]{2,1,0:T(8,128)(2,1)S(1)} custom-call(s32[2]{0:T(128)S(1)} %pad_add_fusion.place_ref, s32[1,512]{1,0:T(1,128)S(1)} %copy-done.12, f32[2,16,64,128]{3,2,1,0:T(8,128)S(1)} %bitcast.29, bf16[512,128]{1,0:T(8,128)(2,1)S(1)} %get-tuple-element.15.weight_ref), custom_call_target="tpu_custom_call" | custom-call | flops 100000000 | bytes 2230280 | tf_op jit(solution)/shard_map/project/pallas_call | solution.py:231
  8.4 47.8 %all_to_all.30 = bf16[128,32,128]{2,1,0:T(8,128)(2,1)S(1)} all-to-all(bf16[128,32,128]{2,1,0:T(8,128)(2,1)S(1)} %project.1), channel_id=1, replica_groups=mesh['grp'=2,'z'=8,'core'=2,'col'=8] {'z','core','col'}, dimensions={0} | all-to-all | bytes 2097152 | tf_op jit(solution)/shard_map/all_to_all | solution.py:252
  56.1 1.8 product.2
  58.0 0.0 copy-start.1
  58.0 6.3 %all-to-all-start.1 = ((bf16[128,16,128]{2,1,0:T(8,128)(2,1)}), bf16[128,16,128]{2,1,0:T(8,128)(2,1)S(1)}, u32[]{:S(2)}, u32[]{:S(2)}) async-start(bf16[128,16,128]{2,1,0:T(8,128)(2,1)} %bitcast.6), calls=%async_computation.1 | async-start | bytes 1048576 | tf_op jit(solution)/shard_map/all_to_all | solution.py:252
  64.2 0.0 copy-done.3
  64.2 0.0 copy-done.14
  64.2 1.6 bias.1
  65.8 0.0 copy-start.17
  65.8 0.0 copy-start.13
  65.9 0.5 collective-permute-start
  66.3 3.4 %collective-permute-done.bias_ref = bf16[16,16,128]{2,1,0:T(8,128)(2,1)S(1)} collective-permute-done((bf16[16,16,128]{2,1,0:T(8,128)(2,1)S(1)}, bf16[16,16,128]{2,1,0:T(8,128)(2,1)S(1)}, u32[]{:S(2)}, u32[]{:S(2)}) %collective-permute-start) | collective-permute-done | bytes 65568 | tf_op jit(solution)/shard_map/ppermute | solution.py:285
  69.7 0.0 copy-done.11
  69.7 0.0 copy-done.16
  69.7 0.0 copy-done.5
  69.7 0.0 copy-done.10
  69.7 4.4 %tokens_in.1 = (f32[128,768]{1,0:T(8,128)S(1)}, f32[128,768]{1,0:T(8,128)S(1)}, bf16[16,160,128]{2,1,0:T(8,128)(2,1)}) custom-call(s32[2]{0:T(128)S(1)} %pad_add_fusion.place_ref, f32[2,64,768]{2,1,0:T(8,128)S(1)} %bitcast.37, bf16[2,256,128]{2,1,0:T(8,128)(2,1)S(1)} %bitcast.38, s32[1,256]{1,0:T(1,128)S(1)} %copy-done.16, bf16[128,768]{1,0:T(8,128)(2,1)S(1)} %copy-done.10, ...), custom_call_target="tpu_custom_call" | custom-call | flops 100000000 | bytes 6947848 | tf_op jit(solution)/shard_map/tokens_in/pallas_call | solution.py:231
  74.1 0.0 copy-start.6
  74.1 0.8 copy-done.6
  74.9 0.0 copy-start.8
  74.9 0.7 copy-done.8
  75.7 0.0 copy-start.15
  75.7 9.8 %all-to-all-done.1.recv_ref = bf16[128,16,128]{2,1,0:T(8,128)(2,1)S(1)} async-done(((bf16[128,16,128]{2,1,0:T(8,128)(2,1)}), bf16[128,16,128]{2,1,0:T(8,128)(2,1)S(1)}, u32[]{:S(2)}, u32[]{:S(2)}) %all-to-all-start.1) | async-done | bytes 524320 | tf_op jit(solution)/shard_map/all_to_all | solution.py:252
  85.4 3.7 %all-to-all-start.4 = ((bf16[16,160,128]{2,1,0:T(8,128)(2,1)}), bf16[16,160,128]{2,1,0:T(8,128)(2,1)S(1)}, u32[]{:S(2)}, u32[]{:S(2)}) async-start(bf16[16,160,128]{2,1,0:T(8,128)(2,1)} %get-tuple-element.9), calls=%async_computation.4 | async-start | bytes 1310720 | tf_op jit(solution)/shard_map/all_to_all | solution.py:252
  89.2 0.8 slice_bitcast_fusion.3
  89.9 0.0 copy-done.1
  89.9 1.4 gate.2.gate_ref
  91.4 0.0 copy-done.17
  91.4 0.0 copy-done.13
  91.4 6.6 %finish_project.1 = (f32[2,16,64,128]{3,2,1,0:T(8,128)S(1)}, bf16[128,32,128]{2,1,0:T(8,128)(2,1)S(1)}) custom-call(s32[2]{0:T(128)S(1)} %pad_add_fusion.place_ref, s32[1,512]{1,0:T(1,128)S(1)} %copy-done.13, bf16[128,16,128]{2,1,0:T(8,128)(2,1)S(1)} %all-to-all-done.1.recv_ref, f32[2,16,64,128]{3,2,1,0:T(8,128)S(1)} %bitcast.31, ...), custom_call_target="tpu_custom_call" | custom-call | flops 100000000 | bytes 4884488 | tf_op jit(solution)/shard_map/finish_project/pallas_call | solution.py:231
  98.1 0.0 copy-start.4
  98.1 1.0 copy-done.4
  99.0 3.6 %all-to-all-done.4 = bf16[16,160,128]{2,1,0:T(8,128)(2,1)S(1)} async-done(((bf16[16,160,128]{2,1,0:T(8,128)(2,1)}), bf16[16,160,128]{2,1,0:T(8,128)(2,1)S(1)}, u32[]{:S(2)}, u32[]{:S(2)}) %all-to-all-start.4) | async-done | bytes 655392 | tf_op jit(solution)/shard_map/all_to_all | solution.py:252
  102.7 6.0 %all-to-all-start.2 = ((bf16[128,32,128]{2,1,0:T(8,128)(2,1)}), bf16[128,32,128]{2,1,0:T(8,128)(2,1)S(1)}, u32[]{:S(2)}, u32[]{:S(2)}) async-start(bf16[128,32,128]{2,1,0:T(8,128)(2,1)} %copy-done.4), calls=%async_computation.2 | async-start | bytes 2097152 | tf_op jit(solution)/shard_map/all_to_all | solution.py:252
  108.7 41.0 %all_gather.3 = bf16[128,16,128]{2,1,0:T(8,128)(2,1)S(1)} all-gather(bf16[16,16,128]{2,1,0:T(8,128)(2,1)S(1)} %slice.30), channel_id=1, replica_groups=mesh['grp'=2,'z'=8,'core'=2,'col'=8] {'z'}, dimensions={0}, use_global_device_ids=true | all-gather | bytes 589824 | tf_op jit(solution)/shard_map/all_gather | solution.py:295
  149.6 0.0 copy-done.15
  149.6 4.1 %attention.1 = bf16[2,8,48,128]{3,2,1,0:T(8,128)(2,1)} custom-call(s32[1,512]{1,0:T(1,128)S(1)} %copy-done.15, bf16[2,8,160,128]{3,2,1,0:T(8,128)(2,1)S(1)} %bitcast.34, bf16[16,8,16,128]{3,2,1,0:T(8,128)(2,1)S(1)} %bitcast.35), custom_call_target="tpu_custom_call" | custom-call | flops 100000000 | bytes 1378304 | tf_op jit(solution)/shard_map/attention/pallas_call | solution.py:231
  153.7 0.0 all-to-all-done.2
  153.7 12.3 %all-to-all-start.5 = ((bf16[16,48,128]{2,1,0:T(8,128)(2,1)}), bf16[16,48,128]{2,1,0:T(8,128)(2,1)S(1)}, u32[]{:S(2)}, u32[]{:S(2)}) async-start(bf16[16,48,128]{2,1,0:T(8,128)(2,1)} %bitcast.21), calls=%async_computation.5 | async-start | bytes 393216 | tf_op jit(solution)/shard_map/all_to_all | solution.py:252
  166.0 2.0 product.3
  168.0 6.6 %all-to-all-done.5.recv_ref = bf16[16,48,128]{2,1,0:T(8,128)(2,1)S(1)} async-done(((bf16[16,48,128]{2,1,0:T(8,128)(2,1)}), bf16[16,48,128]{2,1,0:T(8,128)(2,1)S(1)}, u32[]{:S(2)}, u32[]{:S(2)}) %all-to-all-start.5) | async-done | bytes 196640 | tf_op jit(solution)/shard_map/all_to_all | solution.py:252
  174.5 7.4 %all-to-all-start.3 = ((bf16[128,16,128]{2,1,0:T(8,128)(2,1)}), bf16[128,16,128]{2,1,0:T(8,128)(2,1)S(1)}, u32[]{:S(2)}, u32[]{:S(2)}) async-start(bf16[128,16,128]{2,1,0:T(8,128)(2,1)} %bitcast.11), calls=%async_computation.3 | async-start | bytes 1048576 | tf_op jit(solution)/shard_map/all_to_all | solution.py:252
  181.9 0.0 copy-start.2
  181.9 1.3 copy-done.2
  183.2 0.0 copy-start.7
  183.2 1.0 copy-done.7
  184.2 0.0 copy-start.9
  184.2 1.0 copy-done.9
  185.2 1.1 tokens_out.1
  186.3 1.4 gate.3.gate_ref
  187.8 15.4 %all-to-all-done.3.recv_ref = bf16[128,16,128]{2,1,0:T(8,128)(2,1)S(1)} async-done(((bf16[128,16,128]{2,1,0:T(8,128)(2,1)}), bf16[128,16,128]{2,1,0:T(8,128)(2,1)S(1)}, u32[]{:S(2)}, u32[]{:S(2)}) %all-to-all-start.3) | async-done | bytes 524320 | tf_op jit(solution)/shard_map/all_to_all | solution.py:252
  203.1 2.4 %finish.1 = f32[2,16,64,128]{3,2,1,0:T(8,128)} custom-call(bf16[128,16,128]{2,1,0:T(8,128)(2,1)S(1)} %all-to-all-done.3.recv_ref, f32[2,16,64,128]{3,2,1,0:T(8,128)S(1)} %get-tuple-element.8.pair_ref, f32[2,16,64,128]{3,2,1,0:T(8,128)S(1)} %gate.3.gate_ref, bf16[128,128]{1,0:T(8,128)(2,1)S(1)} %get-tuple-element.16.out_weight_ref), custom_call_target="tpu_custom_call" | custom-call | flops 100000000 | bytes 3702784 | tf_op jit(solution)/shard_map/finish/pallas_call | solution.py:231
  (3 shorter events, 0.0 us)
Async XLA Ops:
  0.6 63.6 %copy-start.3 = (f32[1,32,64,128]{3,2,1,0:T(8,128)S(1)}, f32[1,32,64,128]{3,2,1,0:T(8,128)}, u32[]{:S(2)}) copy-start(f32[1,32,64,128]{3,2,1,0:T(8,128)} %param.15) | copy-start | bytes 3145732
  0.6 63.6 %copy-start.14 = (bf16[128,16]{0,1:T(8,128)(2,1)S(1)}, bf16[128,16]{0,1:T(8,128)(2,1)}, u32[]{:S(2)}) copy-start(bf16[128,16]{0,1:T(8,128)(2,1)} %param.22) | copy-start | bytes 12292
  0.7 69.1 %copy-start.11 = (bf16[1,2,256,128]{3,2,1,0:T(8,128)(2,1)S(1)}, bf16[1,2,256,128]{3,2,1,0:T(8,128)(2,1)}, u32[]{:S(2)}) copy-start(bf16[1,2,256,128]{3,2,1,0:T(8,128)(2,1)} %param.18) | copy-start | bytes 393220
  0.7 69.1 %copy-start.16 = (s32[1,256]{1,0:T(1,128)S(1)}, s32[1,256]{1,0:T(1,128)}, u32[]{:S(2)}) copy-start(s32[1,256]{1,0:T(1,128)} %ids_ref.1) | copy-start | bytes 3076
  2.1 1.2 copy-start
  3.3 0.7 copy-start.12
  4.0 65.7 %copy-start.5 = (f32[1,2,64,768]{3,2,1,0:T(8,128)S(1)}, f32[1,2,64,768]{3,2,1,0:T(8,128)}, u32[]{:S(2)}) copy-start(f32[1,2,64,768]{3,2,1,0:T(8,128)} %param.16) | copy-start | bytes 1179652
  4.0 65.7 %copy-start.10 = (bf16[128,768]{1,0:T(8,128)(2,1)S(1)}, bf16[128,768]{1,0:T(8,128)(2,1)}, u32[]{:S(2)}) copy-start(bf16[128,768]{1,0:T(8,128)(2,1)} %atom_weight_ref.1) | copy-start | bytes 589828
  58.0 32.0 %copy-start.1 = (f32[1,32,64,128]{3,2,1,0:T(8,128)S(1)}, f32[1,32,64,128]{3,2,1,0:T(8,128)}, u32[]{:S(2)}) copy-start(f32[1,32,64,128]{3,2,1,0:T(8,128)} %param.13) | copy-start | bytes 3145732
  58.0 27.5 %all-to-all-start.1 = ((bf16[128,16,128]{2,1,0:T(8,128)(2,1)}), bf16[128,16,128]{2,1,0:T(8,128)(2,1)S(1)}, u32[]{:S(2)}, u32[]{:S(2)}) async-start(bf16[128,16,128]{2,1,0:T(8,128)(2,1)} %bitcast.6), calls=%async_computation.1 | async-start | bytes 1048576 | tf_op jit(solution)/shard_map/all_to_all | solution.py:252
  65.8 25.5 %copy-start.17 = (bf16[2,128,128]{2,1,0:T(8,128)(2,1)S(1)}, bf16[2,128,128]{2,1,0:T(8,128)(2,1)}, u32[]{:S(2)}) copy-start(bf16[2,128,128]{2,1,0:T(8,128)(2,1)} %param.21) | copy-start | bytes 196612
  65.8 25.6 %copy-start.13 = (s32[1,512]{1,0:T(1,128)S(1)}, s32[1,512]{1,0:T(1,128)}, u32[]{:S(2)}) copy-start(s32[1,512]{1,0:T(1,128)} %mask_ref.4) | copy-start | bytes 6148
  65.9 3.9 %collective-permute-start = (bf16[16,16,128]{2,1,0:T(8,128)(2,1)S(1)}, bf16[16,16,128]{2,1,0:T(8,128)(2,1)S(1)}, u32[]{:S(2)}, u32[]{:S(2)}) collective-permute-start(bf16[16,16,128]{2,1,0:T(8,128)(2,1)S(1)} %bias.1), channel_id=1, source_target_pairs={{0,128},{128,0},{1,129},{129,1},{2,130},{130,2},{3,131},{131,3},{4... | collective-permute-start | bytes 196616 | tf_op jit(solution)/shard_map/ppermute | solution.py:285
  74.1 0.8 copy-start.6
  74.9 0.7 copy-start.8
  75.7 74.0 %copy-start.15 = (s32[1,512]{1,0:T(1,128)S(1)}, s32[1,512]{1,0:T(1,128)}, u32[]{:S(2)}) copy-start(s32[1,512]{1,0:T(1,128)} %mask_ref.5) | copy-start | bytes 6148
  85.4 17.2 %all-to-all-start.4 = ((bf16[16,160,128]{2,1,0:T(8,128)(2,1)}), bf16[16,160,128]{2,1,0:T(8,128)(2,1)S(1)}, u32[]{:S(2)}, u32[]{:S(2)}) async-start(bf16[16,160,128]{2,1,0:T(8,128)(2,1)} %get-tuple-element.9), calls=%async_computation.4 | async-start | bytes 1310720 | tf_op jit(solution)/shard_map/all_to_all | solution.py:252
  98.1 1.0 copy-start.4
  102.7 51.0 %all-to-all-start.2 = ((bf16[128,32,128]{2,1,0:T(8,128)(2,1)}), bf16[128,32,128]{2,1,0:T(8,128)(2,1)S(1)}, u32[]{:S(2)}, u32[]{:S(2)}) async-start(bf16[128,32,128]{2,1,0:T(8,128)(2,1)} %copy-done.4), calls=%async_computation.2 | async-start | bytes 2097152 | tf_op jit(solution)/shard_map/all_to_all | solution.py:252
  153.7 20.8 %all-to-all-start.5 = ((bf16[16,48,128]{2,1,0:T(8,128)(2,1)}), bf16[16,48,128]{2,1,0:T(8,128)(2,1)S(1)}, u32[]{:S(2)}, u32[]{:S(2)}) async-start(bf16[16,48,128]{2,1,0:T(8,128)(2,1)} %bitcast.21), calls=%async_computation.5 | async-start | bytes 393216 | tf_op jit(solution)/shard_map/all_to_all | solution.py:252
  174.5 28.6 %all-to-all-start.3 = ((bf16[128,16,128]{2,1,0:T(8,128)(2,1)}), bf16[128,16,128]{2,1,0:T(8,128)(2,1)S(1)}, u32[]{:S(2)}, u32[]{:S(2)}) async-start(bf16[128,16,128]{2,1,0:T(8,128)(2,1)} %bitcast.11), calls=%async_computation.3 | async-start | bytes 1048576 | tf_op jit(solution)/shard_map/all_to_all | solution.py:252
  181.9 1.3 copy-start.2
  183.2 1.0 copy-start.7
  184.2 1.0 copy-start.9

commit v2 on v1

v2 whole, which is shorter than its diff:
```python
import functools

import jax
import jax.numpy as jnp
from jax import lax
from jax.experimental import pallas as pl
from jax.experimental.pallas import tpu as pltpu
from jax.sharding import Mesh, PartitionSpec as P

EPSILON = 1e-05
F32, BF16 = jnp.float32, jnp.bfloat16
ROWS, COLS, TOK, C = 32, 64, 512, 128
HEADS, HEAD = 16, 48
WIDTH, PAIR = HEADS * HEAD, 2 * HEAD
VMEM_LIMIT = 48 * 2**20
NT = (((1,), (1,)), ((), ()))
TN = (((0,), (0,)), ((), ()))


def dot(left, right, dims=(((1,), (0,)), ((), ()))):
    return lax.dot_general(left, right, dims, preferred_element_type=F32)


def layer_norm(values, axis=-1):
    centred = values - jnp.mean(values, axis=axis, keepdims=True)
    spread = jnp.mean(centred * centred, axis=axis, keepdims=True)
    return centred * lax.rsqrt(spread + EPSILON)


def low_lanes():
    return lax.broadcasted_iota(jnp.int32, (1, 128), 1) < 64


def swap_halves(first, second):
    low = low_lanes()
    axis = first.ndim - 1
    return (
        jnp.where(low, first, pltpu.roll(second, 64, axis)),
        jnp.where(low, pltpu.roll(first, 64, axis), second),
    )


def pair_step(pair_ref, step):
    return pair_ref[:, step].reshape(2 * COLS, C)


def turned_weight(weight_ref, update):
    return jnp.transpose(weight_ref[update, :, : 4 * C].astype(F32), (1, 0)).astype(BF16)


def project_step(values, step, length, row0, col0, weight, spread_ref):
    normed = layer_norm(values).astype(BF16)
    lane = lax.broadcasted_iota(jnp.int32, (1, 128), 1)
    half = (lane >= 64).astype(jnp.int32)
    row = row0 + half * 16 + step
    col = col0 + lane - half * 64
    live = jnp.logical_and(row < length, col < length).astype(F32)
    projected = dot(weight, normed, NT)
    left = live * jax.nn.sigmoid(projected[:C]) * projected[C : 2 * C]
    right = live * jax.nn.sigmoid(projected[2 * C : 3 * C]) * projected[3 * C :]
    spread_ref[pl.ds(step, C, stride=32), :] = left
    spread_ref[pl.ds(step + 16, C, stride=32), :] = right


def mask_length(mask_ref):
    return jnp.sum(mask_ref[...])


def project_kernel(place_ref, mask_ref, pair_ref, weight_ref, out_ref, spread_ref):
    length = mask_length(mask_ref)
    weight = turned_weight(weight_ref, 0)

    def body(step, carry):
        project_step(
            pair_step(pair_ref, step), step, length, place_ref[0], place_ref[1], weight, spread_ref
        )
        return carry

    lax.fori_loop(0, 16, body, 0, unroll=4)
    out_ref[...] = spread_ref[...].astype(BF16).reshape(C, 32, 128)


def gate_kernel(pair_ref, weight_ref, out_ref, *, update):
    weight = weight_ref[update, :, 4 * C :]

    def body(step, carry):
        normed = layer_norm(pair_step(pair_ref, step)).astype(BF16)
        out_ref[:, step] = jax.nn.sigmoid(dot(normed, weight)).reshape(2, COLS, C)
        return carry

    lax.fori_loop(0, 16, body, 0, unroll=4)


def product_kernel(recv_ref, *refs, outgoing):
    out_ref, left_ref, right_ref = refs[-3:]
    if outgoing:
        bias_ref = refs[0]
        for core in range(2):
            for col in range(8):
                tile = bias_ref[2 * col + core]
                out_ref[core, col, :, 16:, :] = jnp.broadcast_to(tile[None], (8, 16, 128))
    for block in range(4):
        lanes = slice(block * 128, (block + 1) * 128)
        for side, dest_ref in ((0, left_ref), (1, right_ref)):
            rows = slice(side * 16, side * 16 + 16)
            for core in range(2):
                first, second = swap_halves(
                    recv_ref[core, 2 * block, :, rows, :].astype(F32),
                    recv_ref[core, 2 * block + 1, :, rows, :].astype(F32),
                )
                dest_ref[:, core, 0, :, lanes] = first.astype(BF16)
                dest_ref[:, core, 1, :, lanes] = second.astype(BF16)
    left = left_ref[...].reshape(TOK, TOK)
    right = right_ref[...].reshape(TOK, TOK)
    for block in range(4):
        lanes = slice(block * 128, (block + 1) * 128)
        if outgoing:
            summed = dot(left, right[lanes], NT)
        else:
            summed = dot(left, right[:, lanes], TN)
        summed = summed.reshape(8, 2, 2, 16, 128)
        for core in range(2):
            first, second = swap_halves(summed[:, core, 0], summed[:, core, 1])
            out_ref[core, 2 * block, :, :16, :] = first.astype(BF16)
            out_ref[core, 2 * block + 1, :, :16, :] = second.astype(BF16)


def finish_step(recv_f32_ref, pair_ref, gate_ref, weight, step):
    summed = recv_f32_ref[pl.ds(step, C, stride=16), :]
    normed = layer_norm(summed, 0).astype(BF16)
    update = dot(normed, weight, TN)
    return pair_step(pair_ref, step) + pair_step(gate_ref, step) * update


def finish_project_kernel(
    place_ref, mask_ref, recv_ref, pair_ref, gate_ref, out_weight_ref, in_weight_ref,
    pair_out_ref, out_ref, recv_f32_ref, spread_ref,
):
    length = mask_length(mask_ref)
    weight = turned_weight(in_weight_ref, 1)
    recv_f32_ref[...] = recv_ref[:, :16, :].astype(F32).reshape(C * 16, 128)

    def body(step, carry):
        values = finish_step(recv_f32_ref, pair_ref, gate_ref, out_weight_ref[0], step)
        pair_out_ref[:, step] = values.reshape(2, COLS, C)
        project_step(values, step, length, place_ref[0], place_ref[1], weight, spread_ref)
        return carry

    lax.fori_loop(0, 16, body, 0, unroll=4)
    out_ref[...] = spread_ref[...].astype(BF16).reshape(C, 32, 128)


def finish_kernel(recv_ref, pair_ref, gate_ref, out_weight_ref, *refs):
    pair_out_ref, recv_f32_ref = refs[-2:]
    recv_f32_ref[...] = recv_ref[:, :16, :].astype(F32).reshape(C * 16, 128)

    def body(step, carry):
        values = finish_step(recv_f32_ref, pair_ref, gate_ref, out_weight_ref[1], step)
        pair_out_ref[:, step] = values.reshape(2, COLS, C)
        return carry

    lax.fori_loop(0, 16, body, 0, unroll=4)


def bias_kernel(prev_ref, weight_ref, *refs):
    out_ref, spread_ref = refs[-2:]

    def body(step, carry):
        normed = layer_norm(pair_step(prev_ref, step)).astype(BF16)
        spread_ref[pl.ds(step, HEADS, stride=16), :] = dot(weight_ref[...], normed, NT)
        return carry

    lax.fori_loop(0, 16, body, 0, unroll=4)
    out_ref[...] = spread_ref[...].astype(BF16).reshape(HEADS, 16, 128)


def tokens_kernel(
    place_ref, tokens_ref, atoms_ref, ids_ref, atom_weight_ref, weight_ref, *refs,
):
    start_ref, gate_ref, parts_ref = refs[-3:]
    tokens, atoms = 64, 256
    local = ids_ref[...] - place_ref[1]
    onehot = (lax.broadcasted_iota(jnp.int32, (tokens, atoms), 0) == local).astype(F32)
    count = jnp.sum(onehot, axis=1, keepdims=True)
    onehot = onehot.astype(BF16)
    pooled = [(dot(onehot, atoms_ref[sample]) / count).astype(BF16) for sample in range(2)]
    start = tokens_ref[...].reshape(128, WIDTH) + dot(
        jnp.concatenate(pooled, axis=0), atom_weight_ref[...]
    )
    start_ref[...] = start
    normed = layer_norm(start).astype(BF16)
    for part in range(3):
        projected = dot(normed, weight_ref[:, part * WIDTH : (part + 1) * WIDTH])
        turned = jnp.transpose(projected, (1, 0)).astype(BF16)
        parts_ref[:, part * PAIR : (part + 1) * PAIR, :] = turned.reshape(8, PAIR, 128)
    gate_ref[...] = jax.nn.sigmoid(dot(normed, weight_ref[:, 3 * WIDTH :]))


def attention_kernel(place_ref, mask_ref, recv_ref, bias_ref, other_bias_ref, *refs):
    sends = refs[:8]
    query_key_ref, value_ref, full_bias_ref, mixed_ref, out_ref = refs[8:]
    live = lax.broadcasted_iota(jnp.int32, (1, TOK), 1) < mask_length(mask_ref)
    own = place_ref[2]
    for block in range(4):
        lanes = slice(block * 128, (block + 1) * 128)
        for head, source_ref in ((own, bias_ref), (1 - own, other_bias_ref)):
            for core in range(2):
                first, second = swap_halves(
                    source_ref[core, 2 * block].astype(F32), source_ref[core, 2 * block + 1].astype(F32)
                )
                full_bias_ref[head, :, core, 0, :, lanes] = first.astype(BF16)
                full_bias_ref[head, :, core, 1, :, lanes] = second.astype(BF16)
        halves = swap_halves(recv_ref[2 * block].astype(F32), recv_ref[2 * block + 1].astype(F32))
        for sample in range(2):
            half = halves[sample].astype(BF16)
            query_key_ref[sample, :, lanes] = half[: 2 * PAIR]
            for head in range(2):
                at = 2 * PAIR + head * HEAD
                value_ref[sample, head, :HEAD, lanes] = half[at : at + HEAD]
    value_ref[:, :, HEAD:, :] = jnp.ones((2, 2, 16, TOK), BF16)
    for head in range(2):
        bias = full_bias_ref[head].reshape(TOK, TOK)
        for sample in range(2):
            query = query_key_ref[sample, head * HEAD : (head + 1) * HEAD, :]
            key = query_key_ref[sample, PAIR + head * HEAD : PAIR + (head + 1) * HEAD, :]
            scores = dot(query, key, TN) * (HEAD**-0.5) + bias.astype(F32)
            scores = jnp.where(live, scores, -1e30)
            top = jnp.max(scores, axis=1, keepdims=True)
            weights = jnp.exp(scores - top).astype(BF16)
            mixed = dot(value_ref[sample, head], weights, NT)
            mixed_ref[sample, head * HEAD : (head + 1) * HEAD] = mixed[:HEAD] / mixed[HEAD : HEAD + 1]
    for block in range(4):
        lanes = slice(block * 128, (block + 1) * 128)
        first, second = swap_halves(mixed_ref[0, :, lanes], mixed_ref[1, :, lanes])
        out_ref[2 * block] = first.astype(BF16)
        out_ref[2 * block + 1] = second.astype(BF16)
    for slot in range(8):
        sends[slot][...] = out_ref[place_ref[3] ^ slot]


def tokens_out_kernel(place_ref, gate_ref, start_ref, weight_ref, *refs):
    out_ref, recv_ref = refs[8:]
    for slot in range(8):
        recv_ref[place_ref[3] ^ slot] = refs[slot][...]
    mixed = jnp.transpose(recv_ref[...].reshape(WIDTH, 128).astype(F32), (1, 0))
    blended = (gate_ref[...] * mixed).astype(BF16)
    out_ref[...] = (start_ref[...] + dot(blended, weight_ref[...])).reshape(2, 64, WIDTH)


def call(kernel, name, out_shape, scratch, *operands, smem=0, after=(), flops=10**8):
    shapes = jax.tree.leaves(out_shape)
    nbytes = sum(v.size * v.dtype.itemsize for v in (*operands, *shapes))
    vmem = pl.BlockSpec(memory_space=pltpu.VMEM)
    return pl.pallas_call(
        kernel,
        name=name,
        out_shape=out_shape,
        in_specs=[pl.BlockSpec(memory_space=pltpu.SMEM)] * smem
        + [vmem] * (len(operands) - smem)
        + [pl.BlockSpec(memory_space=pl.ANY)] * len(after),
        out_specs=jax.tree.map(lambda _: vmem, out_shape),
        scratch_shapes=scratch,
        cost_estimate=pl.CostEstimate(flops=flops, bytes_accessed=nbytes, transcendentals=0),
        compiler_params=pltpu.CompilerParams(vmem_limit_bytes=VMEM_LIMIT),
    )(*operands, *after)


def shape(*dims, dtype=F32):
    return jax.ShapeDtypeStruct(dims, dtype)


ALL = ("core", "col", "z")


def exchange(value, axes=ALL):
    return lax.all_to_all(value, axes, 0, 0, tiled=True)


def on_device(
    pair, pair_mask, prev_pair, diff_tokens, diff_mask, atom_feats, atom_token,
    trunk_in, trunk_out, bias_weight, atom_weight, attn_in, attn_out,
):
    z, core, col = lax.axis_index("z"), lax.axis_index("core"), lax.axis_index("col")
    place = jnp.stack([(z * 2 + core) * ROWS, col * COLS, core, col]).astype(jnp.int32)
    tile = (2, 16, COLS, C)
    send = shape(C, 32, 128, dtype=BF16)
    spread = pltpu.VMEM((C * 32, 128), F32)
    received = pltpu.VMEM((C * 16, 128), F32)
    square = pltpu.VMEM((8, 2, 2, 16, TOK), BF16)

    def product(gathered, outgoing, *bias, after):
        rows = 32 if bias else 16
        result = call(
            functools.partial(product_kernel, outgoing=outgoing), "product",
            shape(2, 8, 8, rows, 128, dtype=BF16), [square, square],
            gathered.reshape(2, 8, 8, 32, 128), *bias, after=after, flops=2 * TOK**3,
        )
        return exchange(result.reshape(C, rows, 128))

    def gate(values, update):
        return call(
            functools.partial(gate_kernel, update=update), "gate", shape(*tile), [], values, trunk_in
        )

    pair0 = pair.reshape(tile)
    operands = call(
        project_kernel, "project", send, [spread], place, pair_mask, pair0, trunk_in, smem=1
    )
    gathered = exchange(operands)

    bias_here = call(
        bias_kernel, "bias", shape(HEADS, 16, 128, dtype=BF16), [pltpu.VMEM((HEADS * 16, 128), F32)],
        prev_pair.reshape(tile), jnp.swapaxes(bias_weight, 0, 1), after=(operands,),
    )
    bias_other = lax.ppermute(bias_here, "grp", [(0, 1), (1, 0)])
    start, gate2, parts = call(
        tokens_kernel, "tokens_in",
        [shape(128, WIDTH), shape(128, WIDTH), shape(8, 3 * PAIR, 128, dtype=BF16)], [],
        place, diff_tokens[0], atom_feats[0], atom_token, atom_weight, attn_in, smem=1, after=(operands,),
    )

    summed0 = product(gathered, True, bias_other, after=(start,))
    gate0 = gate(pair0, 0)
    parts = exchange(parts, "col")

    pair1, operands = call(
        finish_project_kernel, "finish_project", (shape(*tile), send), [received, spread],
        place, pair_mask, summed0, pair0, gate0, trunk_out, trunk_in, smem=1,
    )
    gathered = exchange(operands)
    biases = summed0[:, 16:, :]
    other_biases = lax.ppermute(biases, "core", [(0, 1), (1, 0)])
    mixed = call(
        attention_kernel, "attention", [shape(PAIR, 128, dtype=BF16)] * 8,
        [
            pltpu.VMEM((2, 2 * PAIR, TOK), BF16),
            pltpu.VMEM((2, 2, HEAD + 16, TOK), BF16),
            pltpu.VMEM((2, 8, 2, 2, 16, TOK), BF16),
            pltpu.VMEM((2, PAIR, TOK), F32),
            pltpu.VMEM((8, PAIR, 128), BF16),
        ],
        place, diff_mask, parts, biases.reshape(2, 8, 8, 16, 128),
        other_biases.reshape(2, 8, 8, 16, 128), smem=1,
    )
    summed1 = product(gathered, False, after=(mixed[0],))
    mixed = [mixed[0]] + [
        lax.ppermute(mixed[slot], "col", [(at, at ^ slot) for at in range(8)]) for slot in range(1, 8)
    ]
    tokens_done = call(
        tokens_out_kernel, "tokens_out", shape(2, 64, WIDTH), [pltpu.VMEM((8, PAIR, 128), BF16)],
        place, gate2, start, attn_out, *mixed, smem=1,
    )
    gate1 = gate(pair1, 1)
    pair2 = call(
        finish_kernel, "finish", shape(*tile), [received],
        summed1, pair1, gate1, trunk_out, after=(tokens_done,),
    )
    return (pair2.reshape(1, ROWS, COLS, C), tokens_done[None])


def solution(mesh):
    split = Mesh(mesh.devices.reshape(2, 8, 2, 8), ("grp", "z", "core", "col"))
    row = ("z", "core")
    placed = (
        P("grp", row, "col", None),
        P("grp", None),
        P("grp", row, "col", None),
        P("grp", row, "col", None),
        P("grp", None),
        P("grp", row, "col", None),
        P("grp", "col"),
        P(),
        P(),
        P(),
        P(),
        P(),
        P(),
    )
    return jax.shard_map(
        on_device,
        mesh=split,
        in_specs=placed,
        out_specs=(P("grp", row, "col", None), P("grp", row, "col", None)),
        check_vma=False,
    )
```

time: 206 us -> 192 us (0.932)
  blocking collectives: 88.7 us -> 38.2 us
  waiting for transfers between devices: 38.7 us -> 59 us
  starting transfers between devices: 36.1 us -> 47.7 us
  local copies, waits for them, and re-layouts: 9.76 us -> 12.6 us
    all_gather x1 -> x0, blocking collectives: 41 us -> none  [on_device(): bias_all = lax.all_gather(parts[:, 3 * HEAD:], 'z', axis=0, tiled=True)]
    all_to_all x5 -> x4, waiting for transfers between devices: 35.4 us -> 52.3 us  [exchange(): return lax.all_to_all(value, axes, 0, 0, tiled=True)]
    ppermute x0 -> x8, starting transfers between devices: none -> 14 us  [the longest x7 13.2 us: on_device(): lax.ppermute(mixed[slot], 'col', [(at, at ^ slot) for at in range(8)])]
    all_to_all x1, blocking collectives: 47.8 us -> 38.2 us  [exchange(): return lax.all_to_all(value, axes, 0, 0, tiled=True)]
    ppermute x0 -> x8, waiting for transfers between devices: none -> 6.7 us  [the longest x7 5.16 us: on_device(): lax.ppermute(mixed[slot], 'col', [(at, at ^ slot) for at in range(8)])]
    unnamed x37 -> x56, local copies, waits for them, and re-layouts: 8.95 us -> 12.6 us
    ppermute x1, waiting for transfers between devices: 3.37 us -> 0.01 us  [on_device(): bias_other = lax.ppermute(bias_here, 'grp', [(0, 1), (1, 0)])]
    all_to_all x5 -> x4, starting transfers between devices: 35.6 us -> 33.2 us  [exchange(): return lax.all_to_all(value, axes, 0, 0, tiled=True)]
  transfers between devices with their start and end apart: 6 -> 13, of which waited for: 5 -> 6; matrix products, arithmetic and copies ran while one was open for 0% -> 0% of each run, Pallas kernels for 11% -> 11%
where the time goes in v2:
time: 192 us; the launch traced here: 191 us
  waiting for transfers between devices  59 us (31%)
  starting transfers between devices  47.7 us (25%)
  blocking collectives  38.2 us (20%)
  Pallas kernels  32.2 us (17%)
  local copies, waits for them, and re-layouts  12.6 us (7%)
    all_to_all x4, waiting for transfers between devices, exchange(): return lax.all_to_all(value, axes, 0, 0, tiled=True)  52.3 us
    all_to_all x1, blocking collectives, exchange(): return lax.all_to_all(value, axes, 0, 0, tiled=True)  38.2 us
    all_to_all x4, starting transfers between devices, exchange(): return lax.all_to_all(value, axes, 0, 0, tiled=True)  33.2 us
    pallas_call x11, Pallas kernels, call(): pl.pallas_call(kernel, name=name, out_shape=out_shape, in_specs=[pl.Block...  32.2 us
    ppermute x7, starting transfers between devices, on_device(): lax.ppermute(mixed[slot], 'col', [(at, at ^ slot) for at in range(8)])  13.2 us
    unnamed x56, local copies, waits for them, and re-layouts  12.6 us
    ppermute x7, waiting for transfers between devices, on_device(): lax.ppermute(mixed[slot], 'col', [(at, at ^ slot) for at in range(8)])  5.16 us
  transfers between devices with their start and end apart: 13, of which 6 were waited for; matrix products, arithmetic and copies ran while one was open for 0% of the time, Pallas kernels for 11%

profile of v2, /device:TPU:1, one launch (start us, length us, event | category | flops | bytes accessed | tf_op | source)
XLA Modules:
  0.0 190.7 jit_solution(5424399235441459266)
XLA Ops:
  0.6 0.0 copy-start.24
  0.6 0.1 pad_add_fusion.place_ref
  0.7 1.2 copy-done
  2.0 1.0 copy-done.2
  2.9 0.7 copy-done.20
  3.6 5.4 %project.1.refs_0_ = bf16[128,32,128]{2,1,0:T(8,128)(2,1)} custom-call(s32[4]{0:T(128)S(1)} %pad_add_fusion.place_ref, s32[1,512]{1,0:T(1,128)S(1)} %copy-done.20, f32[2,16,64,128]{3,2,1,0:T(8,128)S(1)} %bitcast.17, bf16[2,128,640]{2,1,0:T(8,128)(2,1)S(1)} %copy-done.2), custom_call_target="tpu_custom_call" | custom-call | flops 100000000 | bytes 2426896 | tf_op jit(solution)/shard_map/project/pallas_call | solution.py:254
  9.0 16.7 %all-to-all-start = ((bf16[128,32,128]{2,1,0:T(8,128)(2,1)}), bf16[128,32,128]{2,1,0:T(8,128)(2,1)S(1)}, u32[]{:S(2)}, u32[]{:S(2)}) async-start(bf16[128,32,128]{2,1,0:T(8,128)(2,1)} %project.1.refs_0_), calls=%async_computation | async-start | bytes 2097152 | tf_op jit(solution)/shard_map/all_to_all | solution.py:276
  25.8 0.0 copy-done.8
  25.8 0.0 copy-start.22
  25.8 0.7 copy-done.22
  26.5 1.6 bias.1
  28.0 0.5 collective-permute-start
  28.5 0.0 copy-done.24
  28.5 0.0 copy-start.1
  28.6 0.0 copy-start.3
  28.6 0.0 copy-start.21
  28.6 4.5 %tokens_in.1 = (f32[128,768]{1,0:T(8,128)S(1)}, f32[128,768]{1,0:T(8,128)S(1)}, bf16[8,288,128]{2,1,0:T(8,128)(2,1)}) custom-call(s32[4]{0:T(128)S(1)} %pad_add_fusion.place_ref, f32[2,64,768]{2,1,0:T(8,128)S(1)} %bitcast.27, bf16[2,256,128]{2,1,0:T(8,128)(2,1)S(1)} %bitcast.28, s32[1,256]{1,0:T(1,128)S(1)} %copy-done.24, bf16[128,768]{1,0:T(8,128)(2,1)S(1)} %copy-done.14, ...), custom_call_target="tpu_custom_call" | custom-call | flops 100000000 | bytes 6816784 | tf_op jit(solution)/shard_map/tokens_in/pallas_call | solution.py:254
  33.1 0.7 copy-done.11
  33.8 0.0 collective-permute-done.refs_0_
  33.8 0.6 copy-done.18
  34.4 24.3 %all-to-all-done = bf16[128,32,128]{2,1,0:T(8,128)(2,1)S(1)} async-done(((bf16[128,32,128]{2,1,0:T(8,128)(2,1)}), bf16[128,32,128]{2,1,0:T(8,128)(2,1)S(1)}, u32[]{:S(2)}, u32[]{:S(2)}) %all-to-all-start) | async-done | bytes 1048608 | tf_op jit(solution)/shard_map/all_to_all | solution.py:276
  58.7 0.8 copy-done.19
  59.5 1.1 product.2
  60.6 38.2 %all_to_all.25.recv_ref = bf16[128,32,128]{2,1,0:T(8,128)(2,1)S(1)} all-to-all(bf16[128,32,128]{2,1,0:T(8,128)(2,1)S(1)} %bitcast.22), channel_id=1, replica_groups=mesh['grp'=2,'z'=8,'core'=2,'col'=8] {'core','col','z'}, dimensions={0} | all-to-all | bytes 2097152 | tf_op jit(solution)/shard_map/all_to_all | solution.py:276
  98.9 4.2 %all-to-all-start.3 = ((bf16[8,288,128]{2,1,0:T(8,128)(2,1)}), bf16[8,288,128]{2,1,0:T(8,128)(2,1)}, u32[]{:S(2)}, u32[]{:S(2)}) async-start(bf16[8,288,128]{2,1,0:T(8,128)(2,1)} %get-tuple-element.17), calls=%async_computation.3 | async-start | bytes 1179648 | tf_op jit(solution)/shard_map/all_to_all | solution.py:276
  103.1 0.0 copy-start.23
  103.1 1.4 gate.2.gate_ref
  104.6 6.7 %finish_project.1 = (f32[2,16,64,128]{3,2,1,0:T(8,128)S(1)}, bf16[128,32,128]{2,1,0:T(8,128)(2,1)S(1)}) custom-call(s32[4]{0:T(128)S(1)} %pad_add_fusion.place_ref, s32[1,512]{1,0:T(1,128)S(1)} %copy-done.21, bf16[128,32,128]{2,1,0:T(8,128)(2,1)S(1)} %all_to_all.25.recv_ref, f32[2,16,64,128]{3,2,1,0:T(8,128)S(1)} %bitcast.19, ...), custom_call_target="tpu_custom_call" | custom-call | flops 100000000 | bytes 5638160 | tf_op jit(solution)/shard_map/finish_project/pallas_call | solution.py:254
  111.2 0.0 copy-start.9
  111.3 1.0 copy-done.9
  112.2 3.3 %all-to-all-done.3.recv_ref = bf16[8,288,128]{2,1,0:T(8,128)(2,1)} async-done(((bf16[8,288,128]{2,1,0:T(8,128)(2,1)}), bf16[8,288,128]{2,1,0:T(8,128)(2,1)}, u32[]{:S(2)}, u32[]{:S(2)}) %all-to-all-start.3) | async-done | bytes 589856 | tf_op jit(solution)/shard_map/all_to_all | solution.py:276
  115.6 6.4 %all-to-all-start.2 = ((bf16[128,32,128]{2,1,0:T(8,128)(2,1)}), bf16[128,32,128]{2,1,0:T(8,128)(2,1)S(1)}, u32[]{:S(2)}, u32[]{:S(2)}) async-start(bf16[128,32,128]{2,1,0:T(8,128)(2,1)} %copy-done.9), calls=%async_computation.2 | async-start | bytes 2097152 | tf_op jit(solution)/shard_map/all_to_all | solution.py:276
  122.0 0.8 collective-permute-start.1
  122.8 1.5 collective-permute-done.1
  124.4 4.0 %attention.1 = (bf16[96,128]{1,0:T(8,128)(2,1)S(1)}, bf16[96,128]{1,0:T(8,128)(2,1)S(1)}, bf16[96,128]{1,0:T(8,128)(2,1)S(1)}, bf16[96,128]{1,0:T(8,128)(2,1)S(1...) custom-call(s32[4]{0:T(128)S(1)} %pad_add_fusion.place_ref, ...), custom_call_target="tpu_custom_call" | custom-call | flops 100000000 | bytes 1837072 | tf_op jit(solution)/shard_map/attention/pallas_call | solution.py:254
  128.4 0.6 copy-done.25
  129.0 0.6 copy-done.26
  129.6 0.6 copy-done.27
  130.2 24.7 %all-to-all-done.2 = bf16[128,32,128]{2,1,0:T(8,128)(2,1)S(1)} async-done(((bf16[128,32,128]{2,1,0:T(8,128)(2,1)}), bf16[128,32,128]{2,1,0:T(8,128)(2,1)S(1)}, u32[]{:S(2)}, u32[]{:S(2)}) %all-to-all-start.2) | async-done | bytes 1048608 | tf_op jit(solution)/shard_map/all_to_all | solution.py:276
  154.9 2.0 %product.3 = bf16[2,8,8,16,128]{4,3,2,1,0:T(8,128)(2,1)} custom-call(bf16[2,8,8,32,128]{4,3,2,1,0:T(8,128)(2,1)S(1)} %bitcast.20, bf16[96,128]{1,0:T(8,128)(2,1)S(1)} %get-tuple-element.18.refs_0_), custom_call_target="tpu_custom_call" | custom-call | flops 268435456 | bytes 1572864 | tf_op jit(solution)/shard_map/product/pallas_call | solution.py:254
  156.9 5.9 %all-to-all-start.4 = ((bf16[128,16,128]{2,1,0:T(8,128)(2,1)}), bf16[128,16,128]{2,1,0:T(8,128)(2,1)S(1)}, u32[]{:S(2)}, u32[]{:S(2)}) async-start(bf16[128,16,128]{2,1,0:T(8,128)(2,1)} %bitcast.14), calls=%async_computation.4 | async-start | bytes 1048576 | tf_op jit(solution)/shard_map/all_to_all | solution.py:276
  162.8 1.5 collective-permute-start.2
  164.3 2.5 %collective-permute-start.3 = (bf16[96,128]{1,0:T(8,128)(2,1)}, bf16[96,128]{1,0:T(8,128)(2,1)S(1)}, u32[]{:S(2)}, u32[]{:S(2)}) collective-permute-start(bf16[96,128]{1,0:T(8,128)(2,1)} %copy-done.26), channel_id=1, source_target_pairs={{0,2},{1,3},{2,0},{3,1},{4,6},{5,7},{6,4},{7,5},{8,10},{9,11},{10,... | collective-permute-start | bytes 73736 | tf_op jit(solution)/shard_map/ppermute | solution.py:347
  166.8 0.0 collective-permute-start.4
  166.8 3.0 %collective-permute-start.5 = (bf16[96,128]{1,0:T(8,128)(2,1)S(1)}, bf16[96,128]{1,0:T(8,128)(2,1)S(1)}, u32[]{:S(2)}, u32[]{:S(2)}) collective-permute-start(bf16[96,128]{1,0:T(8,128)(2,1)S(1)} %get-tuple-element.24), channel_id=1, source_target_pairs={{0,4},{1,5},{2,6},{3,7},{4,0},{5,1},{6,2},{7,3},{8,12},{9,13},{10,... | collective-permute-start | bytes 73736 | tf_op jit(solution)/shard_map/ppermute | solution.py:347
  169.8 0.0 collective-permute-start.6
  169.8 0.0 collective-permute-done.2.refs_1_
  169.8 6.1 %collective-permute-start.7 = (bf16[96,128]{1,0:T(8,128)(2,1)S(1)}, bf16[96,128]{1,0:T(8,128)(2,1)S(1)}, u32[]{:S(2)}, u32[]{:S(2)}) collective-permute-start(bf16[96,128]{1,0:T(8,128)(2,1)S(1)} %get-tuple-element.26), channel_id=1, source_target_pairs={{0,6},{1,7},{2,4},{3,5},{4,2},{5,3},{6,0},{7,1},{8,14},{9,15},{10,... | collective-permute-start | bytes 73736 | tf_op jit(solution)/shard_map/ppermute | solution.py:347
  176.0 0.0 collective-permute-done.3.refs_2_
  176.0 0.0 collective-permute-start.8
  176.0 1.4 gate.3.gate_ref
  177.4 0.0 collective-permute-done.4.refs_3_
  177.4 0.0 collective-permute-done.5.refs_4_
  177.4 0.0 collective-permute-done.6.refs_5_
  177.5 0.7 collective-permute-done.7.refs_6_
  178.1 4.5 %collective-permute-done.8.refs_7_ = bf16[96,128]{1,0:T(8,128)(2,1)S(1)} collective-permute-done((bf16[96,128]{1,0:T(8,128)(2,1)S(1)}, bf16[96,128]{1,0:T(8,128)(2,1)S(1)}, u32[]{:S(2)}, u32[]{:S(2)}) %collective-permute-start.8) | collective-permute-done | bytes 24608 | tf_op jit(solution)/shard_map/ppermute | solution.py:347
  182.6 0.0 copy-done.5
  182.6 1.3 copy-done.7
  183.9 1.0 copy-done.12
  184.9 0.7 copy-done.17
  185.6 1.7 tokens_out.1.refs_0_
  187.3 0.0 all-to-all-done.4.recv_ref
  187.3 1.0 copy-done.6
  188.3 2.4 %finish.1 = f32[2,16,64,128]{3,2,1,0:T(8,128)} custom-call(bf16[128,16,128]{2,1,0:T(8,128)(2,1)S(1)} %all-to-all-done.4.recv_ref, f32[2,16,64,128]{3,2,1,0:T(8,128)S(1)} %get-tuple-element.19.pair_ref, f32[2,16,64,128]{3,2,1,0:T(8,128)S(1)} %gate.3.gate_ref, bf16[2,128,128]{2,1,0:T(8,128)(2,1)S(1)} %copy-done.13, f32[2,64,768]{2,1,0:T(8,128)S(1)} %copy-done.6), custom_call_target="tpu_custom_call" | custom-call | flops 100000000 | bytes 3735552 | tf_op jit(solution)/shard_map/finish/pallas_call | solution.py:254
  (32 shorter events, 0.1 us)
Async XLA Ops:
  0.6 27.9 %copy-start.24 = (s32[1,256]{1,0:T(1,128)S(1)}, s32[1,256]{1,0:T(1,128)}, u32[]{:S(2)}) copy-start(s32[1,256]{1,0:T(1,128)} %ids_ref.1) | copy-start | bytes 3076
  0.7 1.2 copy-start
  2.0 1.0 copy-start.2
  2.9 0.7 copy-start.20
  3.6 22.2 %copy-start.8 = (f32[1,32,64,128]{3,2,1,0:T(8,128)S(1)}, f32[1,32,64,128]{3,2,1,0:T(8,128)}, u32[]{:S(2)}) copy-start(f32[1,32,64,128]{3,2,1,0:T(8,128)} %param.15) | copy-start | bytes 3145732
  3.6 24.9 %copy-start.10 = (f32[1,2,64,768]{3,2,1,0:T(8,128)S(1)}, f32[1,2,64,768]{3,2,1,0:T(8,128)}, u32[]{:S(2)}) copy-start(f32[1,2,64,768]{3,2,1,0:T(8,128)} %param.16) | copy-start | bytes 1179652
  3.6 24.9 %copy-start.14 = (bf16[128,768]{1,0:T(8,128)(2,1)S(1)}, bf16[128,768]{1,0:T(8,128)(2,1)}, u32[]{:S(2)}) copy-start(bf16[128,768]{1,0:T(8,128)(2,1)} %atom_weight_ref.1) | copy-start | bytes 589828
  3.6 24.9 %copy-start.15 = (bf16[1,2,256,128]{3,2,1,0:T(8,128)(2,1)S(1)}, bf16[1,2,256,128]{3,2,1,0:T(8,128)(2,1)}, u32[]{:S(2)}) copy-start(bf16[1,2,256,128]{3,2,1,0:T(8,128)(2,1)} %param.18) | copy-start | bytes 393220
  9.0 49.7 %all-to-all-start = ((bf16[128,32,128]{2,1,0:T(8,128)(2,1)}), bf16[128,32,128]{2,1,0:T(8,128)(2,1)S(1)}, u32[]{:S(2)}, u32[]{:S(2)}) async-start(bf16[128,32,128]{2,1,0:T(8,128)(2,1)} %project.1.refs_0_), calls=%async_computation | async-start | bytes 2097152 | tf_op jit(solution)/shard_map/all_to_all | solution.py:276
  25.8 0.7 copy-start.22
  28.0 5.8 %collective-permute-start = (bf16[16,16,128]{2,1,0:T(8,128)(2,1)S(1)}, bf16[16,16,128]{2,1,0:T(8,128)(2,1)S(1)}, u32[]{:S(2)}, u32[]{:S(2)}) collective-permute-start(bf16[16,16,128]{2,1,0:T(8,128)(2,1)S(1)} %bias.1), channel_id=1, source_target_pairs={{0,128},{128,0},{1,129},{129,1},{2,130},{130,2},{3,131},{131,3},{4... | collective-permute-start | bytes 196616 | tf_op jit(solution)/shard_map/ppermute | solution.py:315
  28.5 74.5 %copy-start.1 = (f32[1,32,64,128]{3,2,1,0:T(8,128)S(1)}, f32[1,32,64,128]{3,2,1,0:T(8,128)}, u32[]{:S(2)}) copy-start(f32[1,32,64,128]{3,2,1,0:T(8,128)} %param.13) | copy-start | bytes 3145732
  28.6 74.5 %copy-start.3 = (bf16[2,128,640]{2,1,0:T(8,128)(2,1)S(1)}, bf16[2,128,640]{2,1,0:T(8,128)(2,1)}, u32[]{:S(2)}) copy-start(bf16[2,128,640]{2,1,0:T(8,128)(2,1)} %weight_ref.8) | copy-start | bytes 983044
  28.6 76.0 %copy-start.21 = (s32[1,512]{1,0:T(1,128)S(1)}, s32[1,512]{1,0:T(1,128)}, u32[]{:S(2)}) copy-start(s32[1,512]{1,0:T(1,128)} %mask_ref.4) | copy-start | bytes 6148
  33.1 0.7 copy-start.11
  33.8 69.2 %copy-start.4 = (f32[128,768]{1,0:T(8,128)}, f32[128,768]{1,0:T(8,128)S(1)}, u32[]{:S(2)}) copy-start(f32[128,768]{1,0:T(8,128)S(1)} %get-tuple-element.15.refs_1_.start_ref) | copy-start | bytes 1179652
  33.8 70.7 %copy-start.13 = (bf16[2,128,128]{2,1,0:T(8,128)(2,1)S(1)}, bf16[2,128,128]{2,1,0:T(8,128)(2,1)}, u32[]{:S(2)}) copy-start(bf16[2,128,128]{2,1,0:T(8,128)(2,1)} %out_weight_ref.3) | copy-start | bytes 196612
  33.8 0.6 copy-start.18
  58.7 0.8 copy-start.19
  98.9 16.7 %all-to-all-start.3 = ((bf16[8,288,128]{2,1,0:T(8,128)(2,1)}), bf16[8,288,128]{2,1,0:T(8,128)(2,1)}, u32[]{:S(2)}, u32[]{:S(2)}) async-start(bf16[8,288,128]{2,1,0:T(8,128)(2,1)} %get-tuple-element.17), calls=%async_computation.3 | async-start | bytes 1179648 | tf_op jit(solution)/shard_map/all_to_all | solution.py:276
  103.1 21.3 %copy-start.23 = (s32[1,512]{1,0:T(1,128)S(1)}, s32[1,512]{1,0:T(1,128)}, u32[]{:S(2)}) copy-start(s32[1,512]{1,0:T(1,128)} %mask_ref.5) | copy-start | bytes 6148
  111.2 1.0 copy-start.9
  115.6 39.3 %all-to-all-start.2 = ((bf16[128,32,128]{2,1,0:T(8,128)(2,1)}), bf16[128,32,128]{2,1,0:T(8,128)(2,1)S(1)}, u32[]{:S(2)}, u32[]{:S(2)}) async-start(bf16[128,32,128]{2,1,0:T(8,128)(2,1)} %copy-done.9), calls=%async_computation.2 | async-start | bytes 2097152 | tf_op jit(solution)/shard_map/all_to_all | solution.py:276
  122.0 60.6 %copy-start.5 = (f32[128,768]{1,0:T(8,128)S(1)}, f32[128,768]{1,0:T(8,128)}, u32[]{:S(2)}) copy-start(f32[128,768]{1,0:T(8,128)} %copy-done.4) | copy-start | bytes 1179652
  122.0 2.4 %collective-permute-start.1 = (bf16[128,16,128]{2,1,0:T(8,128)(2,1)S(1)}, bf16[128,16,128]{2,1,0:T(8,128)(2,1)S(1)}, u32[]{:S(2)}, u32[]{:S(2)}) collective-permute-start(bf16[128,16,128]{2,1,0:T(8,128)(2,1)S(1)} %slice.4), channel_id=1, source_target_pairs={{0,8},{8,0},{1,9},{9,1},{2,10},{10,2},{3,11},{11,3},{4,12},{12,4},... | collective-permute-start | bytes 1572872 | tf_op jit(solution)/shard_map/ppermute | solution.py:332
  128.4 0.6 copy-start.25
  129.0 0.6 copy-start.26
  129.6 0.6 copy-start.27
  130.2 52.5 %copy-start.16 = (bf16[96,128]{1,0:T(8,128)(2,1)}, bf16[96,128]{1,0:T(8,128)(2,1)S(1)}, u32[]{:S(2)}) copy-start(bf16[96,128]{1,0:T(8,128)(2,1)S(1)} %get-tuple-element.18.refs_0_) | copy-start | bytes 73732
  156.9 30.5 %all-to-all-start.4 = ((bf16[128,16,128]{2,1,0:T(8,128)(2,1)}), bf16[128,16,128]{2,1,0:T(8,128)(2,1)S(1)}, u32[]{:S(2)}, u32[]{:S(2)}) async-start(bf16[128,16,128]{2,1,0:T(8,128)(2,1)} %bitcast.14), calls=%async_computation.4 | async-start | bytes 1048576 | tf_op jit(solution)/shard_map/all_to_all | solution.py:276
  162.8 7.0 %collective-permute-start.2 = (bf16[96,128]{1,0:T(8,128)(2,1)}, bf16[96,128]{1,0:T(8,128)(2,1)S(1)}, u32[]{:S(2)}, u32[]{:S(2)}) collective-permute-start(bf16[96,128]{1,0:T(8,128)(2,1)} %copy-done.27), channel_id=1, source_target_pairs={{0,1},{1,0},{2,3},{3,2},{4,5},{5,4},{6,7},{7,6},{8,9},{9,8},{10,11... | collective-permute-start | bytes 73736 | tf_op jit(solution)/shard_map/ppermute | solution.py:347
  164.3 11.7 %collective-permute-start.3 = (bf16[96,128]{1,0:T(8,128)(2,1)}, bf16[96,128]{1,0:T(8,128)(2,1)S(1)}, u32[]{:S(2)}, u32[]{:S(2)}) collective-permute-start(bf16[96,128]{1,0:T(8,128)(2,1)} %copy-done.26), channel_id=1, source_target_pairs={{0,2},{1,3},{2,0},{3,1},{4,6},{5,7},{6,4},{7,5},{8,10},{9,11},{10,... | collective-permute-start | bytes 73736 | tf_op jit(solution)/shard_map/ppermute | solution.py:347
  166.8 10.6 %collective-permute-start.4 = (bf16[96,128]{1,0:T(8,128)(2,1)}, bf16[96,128]{1,0:T(8,128)(2,1)S(1)}, u32[]{:S(2)}, u32[]{:S(2)}) collective-permute-start(bf16[96,128]{1,0:T(8,128)(2,1)} %copy-done.25), channel_id=1, source_target_pairs={{0,3},{1,2},{2,1},{3,0},{4,7},{5,6},{6,5},{7,4},{8,11},{9,10},{10,... | collective-permute-start | bytes 73736 | tf_op jit(solution)/shard_map/ppermute | solution.py:347
  166.8 10.6 %collective-permute-start.5 = (bf16[96,128]{1,0:T(8,128)(2,1)S(1)}, bf16[96,128]{1,0:T(8,128)(2,1)S(1)}, u32[]{:S(2)}, u32[]{:S(2)}) collective-permute-start(bf16[96,128]{1,0:T(8,128)(2,1)S(1)} %get-tuple-element.24), channel_id=1, source_target_pairs={{0,4},{1,5},{2,6},{3,7},{4,0},{5,1},{6,2},{7,3},{8,12},{9,13},{10,... | collective-permute-start | bytes 73736 | tf_op jit(solution)/shard_map/ppermute | solution.py:347
  169.8 7.6 %collective-permute-start.6 = (bf16[96,128]{1,0:T(8,128)(2,1)S(1)}, bf16[96,128]{1,0:T(8,128)(2,1)S(1)}, u32[]{:S(2)}, u32[]{:S(2)}) collective-permute-start(bf16[96,128]{1,0:T(8,128)(2,1)S(1)} %get-tuple-element.25), channel_id=1, source_target_pairs={{0,5},{1,4},{2,7},{3,6},{4,1},{5,0},{6,3},{7,2},{8,13},{9,12},{10,... | collective-permute-start | bytes 73736 | tf_op jit(solution)/shard_map/ppermute | solution.py:347
  169.8 8.3 %collective-permute-start.7 = (bf16[96,128]{1,0:T(8,128)(2,1)S(1)}, bf16[96,128]{1,0:T(8,128)(2,1)S(1)}, u32[]{:S(2)}, u32[]{:S(2)}) collective-permute-start(bf16[96,128]{1,0:T(8,128)(2,1)S(1)} %get-tuple-element.26), channel_id=1, source_target_pairs={{0,6},{1,7},{2,4},{3,5},{4,2},{5,3},{6,0},{7,1},{8,14},{9,15},{10,... | collective-permute-start | bytes 73736 | tf_op jit(solution)/shard_map/ppermute | solution.py:347
  176.0 6.6 %collective-permute-start.8 = (bf16[96,128]{1,0:T(8,128)(2,1)S(1)}, bf16[96,128]{1,0:T(8,128)(2,1)S(1)}, u32[]{:S(2)}, u32[]{:S(2)}) collective-permute-start(bf16[96,128]{1,0:T(8,128)(2,1)S(1)} %get-tuple-element.27), channel_id=1, source_target_pairs={{0,7},{1,6},{2,5},{3,4},{4,3},{5,2},{6,1},{7,0},{8,15},{9,14},{10,... | collective-permute-start | bytes 73736 | tf_op jit(solution)/shard_map/ppermute | solution.py:347
  182.6 1.3 copy-start.7
  183.9 1.0 copy-start.12
  184.9 0.7 copy-start.17
  187.3 1.0 copy-start.6

commit v3 on v2

v3 whole, which is shorter than its diff:
```python
import functools

import jax
import jax.numpy as jnp
from jax import lax
from jax.experimental import pallas as pl
from jax.experimental.pallas import tpu as pltpu
from jax.sharding import Mesh, PartitionSpec as P

EPSILON = 1e-05
F32, BF16 = jnp.float32, jnp.bfloat16
ROWS, COLS, TOK, C = 32, 64, 512, 128
HEADS, HEAD = 16, 48
WIDTH, PAIR = HEADS * HEAD, 2 * HEAD
WIDE, MIDDLE, NARROW = 63_000_000, 40_000_000, 24 * 2**20
PITCH, RECV_PITCH = 40, 24
NT = (((1,), (1,)), ((), ()))
TN = (((0,), (0,)), ((), ()))


def dot(left, right, dims=(((1,), (0,)), ((), ()))):
    return lax.dot_general(left, right, dims, preferred_element_type=F32)


def layer_norm(values, axis=-1):
    centred = values - jnp.mean(values, axis=axis, keepdims=True)
    spread = jnp.mean(centred * centred, axis=axis, keepdims=True)
    return centred * lax.rsqrt(spread + EPSILON)


def low_lanes():
    return lax.broadcasted_iota(jnp.int32, (1, 128), 1) < 64


def swap_halves(first, second):
    low = low_lanes()
    axis = first.ndim - 1
    return (
        jnp.where(low, first, pltpu.roll(second, 64, axis)),
        jnp.where(low, pltpu.roll(first, 64, axis), second),
    )


def pair_step(pair_ref, step):
    return pair_ref[:, step].reshape(2 * COLS, C)


def turned(weight):
    return jnp.transpose(weight.astype(F32), (1, 0)).astype(BF16)


def project_step(values, step, length, row0, col0, weight, spread_ref):
    normed = layer_norm(values, 0).astype(BF16)
    lane = lax.broadcasted_iota(jnp.int32, (1, 128), 1)
    half = (lane >= 64).astype(jnp.int32)
    row = row0 + half * 16 + step
    col = col0 + lane - half * 64
    live = jnp.logical_and(row < length, col < length).astype(F32)
    projected = dot(weight, normed)
    left = live * jax.nn.sigmoid(projected[:C]) * projected[C : 2 * C]
    right = live * jax.nn.sigmoid(projected[2 * C : 3 * C]) * projected[3 * C :]
    spread_ref[pl.ds(step, C, stride=PITCH), :] = left
    spread_ref[pl.ds(step + 16, C, stride=PITCH), :] = right


def mask_length(mask_ref):
    return jnp.sum(mask_ref[...])


def send_out(spread_ref, stage_ref, out_ref, sems):
    copies = []
    for part in range(4):
        chunk = pl.ds(part * 32, 32)
        values = spread_ref[pl.ds(part * 32 * PITCH, 32 * PITCH), :].reshape(32, PITCH, 128)
        stage_ref[chunk] = values[:, :32].astype(BF16)
        copies.append(pltpu.make_async_copy(stage_ref.at[chunk], out_ref.at[chunk], sems.at[part]))
        copies[-1].start()
    for copy in copies:
        copy.wait()


def project_kernel(
    place_ref, mask_in, pair_in, weight_in, out_ref,
    mask_ref, pair_ref, weight_ref, spread_ref, stage_ref, in_sems, out_sems,
):
    copies = [
        pltpu.make_async_copy(mask_in, mask_ref, in_sems.at[4]),
        pltpu.make_async_copy(weight_in, weight_ref, in_sems.at[5]),
    ]
    for part in range(4):
        steps = pl.ds(part * 4, 4)
        copies.append(
            pltpu.make_async_copy(pair_in.at[:, steps], pair_ref.at[:, steps], in_sems.at[part])
        )
    for copy in copies:
        copy.start()
    copies[0].wait()
    copies[1].wait()
    length = mask_length(mask_ref)
    weight = turned(weight_ref[0, :, : 4 * C])
    for part in range(4):
        copies[2 + part].wait()
        for step in range(part * 4, part * 4 + 4):
            values = jnp.transpose(pair_step(pair_ref, step), (1, 0))
            project_step(values, step, length, place_ref[0], place_ref[1], weight, spread_ref)
    send_out(spread_ref, stage_ref, out_ref, out_sems)


def gate_kernel(pair_ref, weight_ref, *refs):
    pair_out_ref, gate_ref = refs[-2:]
    weight = turned(weight_ref[0, :, 4 * C :])
    for step in range(16):
        values = jnp.transpose(pair_step(pair_ref, step), (1, 0))
        pair_out_ref[step] = values
        gate_ref[step] = jax.nn.sigmoid(dot(weight, layer_norm(values, 0).astype(BF16)))


def gate_back_kernel(pair_ref, weight_ref, *refs):
    pair_out_ref, gate_ref = refs[-2:]
    weight = turned(weight_ref[1, :, 4 * C :])
    for step in range(16):
        values = pair_ref[step]
        gate = jax.nn.sigmoid(dot(weight, layer_norm(values, 0).astype(BF16)))
        pair_out_ref[:, step] = jnp.transpose(values, (1, 0)).reshape(2, COLS, C)
        gate_ref[:, step] = jnp.transpose(gate, (1, 0)).reshape(2, COLS, C)


def product_kernel(recv_ref, *refs, outgoing):
    out_ref, left_ref, right_ref = refs[-3:]
    if outgoing:
        bias_ref = refs[0]
        for core in range(2):
            for col in range(8):
                tile = bias_ref[2 * col + core]
                out_ref[core, col, :, 16:, :] = jnp.broadcast_to(tile[None], (8, 16, 128))
    for block in range(4):
        lanes = slice(block * 128, (block + 1) * 128)
        for side, dest_ref in ((0, left_ref), (1, right_ref)):
            rows = slice(side * 16, side * 16 + 16)
            for core in range(2):
                first, second = swap_halves(
                    recv_ref[core, 2 * block, :, rows, :].astype(F32),
                    recv_ref[core, 2 * block + 1, :, rows, :].astype(F32),
                )
                dest_ref[:, core, 0, :, lanes] = first.astype(BF16)
                dest_ref[:, core, 1, :, lanes] = second.astype(BF16)
    left = left_ref[...].reshape(TOK, TOK)
    right = right_ref[...].reshape(TOK, TOK)
    for block in range(4):
        lanes = slice(block * 128, (block + 1) * 128)
        if outgoing:
            summed = dot(left, right[lanes], NT)
        else:
            summed = dot(left, right[:, lanes], TN)
        summed = summed.reshape(8, 2, 2, 16, 128)
        for core in range(2):
            first, second = swap_halves(summed[:, core, 0], summed[:, core, 1])
            out_ref[core, 2 * block, :, :16, :] = first.astype(BF16)
            out_ref[core, 2 * block + 1, :, :16, :] = second.astype(BF16)


def load_summed(recv_ref, recv_f32_ref):
    recv_f32_ref.reshape(C, RECV_PITCH, 128)[:, :16] = recv_ref[:, :16, :].astype(F32)


def normed_sum(recv_f32_ref, step):
    return layer_norm(recv_f32_ref[pl.ds(step, C, stride=RECV_PITCH), :], 0).astype(BF16)


def finish_project_kernel(
    place_ref, mask_ref, recv_ref, pair_ref, gate_ref, out_weight_ref, in_weight_ref,
    pair_out_ref, out_ref, recv_f32_ref, spread_ref, stage_ref, out_sems,
):
    length = mask_length(mask_ref)
    weight = turned(in_weight_ref[1, :, : 4 * C])
    out_weight = turned(out_weight_ref[0])
    load_summed(recv_ref, recv_f32_ref)
    for step in range(16):
        update = dot(out_weight, normed_sum(recv_f32_ref, step))
        values = pair_ref[step] + gate_ref[step] * update
        pair_out_ref[step] = values
        project_step(values, step, length, place_ref[0], place_ref[1], weight, spread_ref)
    send_out(spread_ref, stage_ref, out_ref, out_sems)


def finish_kernel(recv_ref, pair_ref, gate_ref, out_weight_ref, out_ref, recv_f32_ref, stage_ref, sems):
    load_summed(recv_ref, recv_f32_ref)
    copies = []
    for part in range(4):
        for step in range(part * 4, part * 4 + 4):
            normed = normed_sum(recv_f32_ref, step).astype(F32)
            update = dot(jnp.transpose(normed, (1, 0)).astype(BF16), out_weight_ref[1])
            values = pair_step(pair_ref, step) + pair_step(gate_ref, step) * update
            stage_ref[:, step] = values.reshape(2, COLS, C)
        steps = pl.ds(part * 4, 4)
        copies.append(
            pltpu.make_async_copy(stage_ref.at[:, steps], out_ref.at[:, steps], sems.at[part])
        )
        copies[-1].start()
    for copy in copies:
        copy.wait()


def fence_kernel(*refs):
    refs[-1][...] = jnp.zeros_like(refs[-1])


def bias_kernel(prev_ref, weight_ref, *refs):
    out_ref, spread_ref = refs[-2:]

    def body(step, carry):
        normed = layer_norm(pair_step(prev_ref, step)).astype(BF16)
        spread_ref[pl.ds(step, HEADS, stride=16), :] = dot(weight_ref[...], normed, NT)
        return carry

    lax.fori_loop(0, 16, body, 0, unroll=4)
    out_ref[...] = spread_ref[...].astype(BF16).reshape(HEADS, 16, 128)


def copy_all(pairs, sems):
    copies = [
        pltpu.make_async_copy(source, dest, sems.at[index]) for index, (source, dest) in enumerate(pairs)
    ]
    for copy in copies:
        copy.start()
    return copies


def wait_all(copies):
    for copy in copies:
        copy.wait()


def tokens_kernel(
    place_ref, tokens_ref, atoms_ref, ids_ref, atom_weight_ref, weight_ref, *refs,
):
    start_out, gate_out, *sends = refs[-14:-4]
    start_ref, gate_ref, parts_ref, sems = refs[-4:]
    tokens, atoms = 64, 256
    local = ids_ref[...] - place_ref[1]
    onehot = (lax.broadcasted_iota(jnp.int32, (tokens, atoms), 0) == local).astype(F32)
    count = jnp.sum(onehot, axis=1, keepdims=True)
    onehot = onehot.astype(BF16)
    pooled = [(dot(onehot, atoms_ref[sample]) / count).astype(BF16) for sample in range(2)]
    start = tokens_ref[...].reshape(128, WIDTH) + dot(
        jnp.concatenate(pooled, axis=0), atom_weight_ref[...]
    )
    start_ref[...] = start
    normed = layer_norm(start).astype(BF16)
    for part in range(3):
        projected = dot(normed, weight_ref[:, part * WIDTH : (part + 1) * WIDTH])
        turned = jnp.transpose(projected, (1, 0)).astype(BF16)
        parts_ref[:, part * PAIR : (part + 1) * PAIR, :] = turned.reshape(8, PAIR, 128)
    copies = copy_all(
        [(parts_ref.at[place_ref[3] ^ slot], sends[slot]) for slot in range(8)] + [(start_ref, start_out)],
        sems,
    )
    gate_ref[...] = jax.nn.sigmoid(dot(normed, weight_ref[:, 3 * WIDTH :]))
    copies.append(pltpu.make_async_copy(gate_ref, gate_out, sems.at[9]))
    copies[-1].start()
    wait_all(copies)


def attention_kernel(place_ref, mask_ref, bias_ref, other_bias_ref, *refs):
    received, sends = refs[:8], refs[8:16]
    recv_ref, query_key_ref, value_ref, full_bias_ref, mixed_ref, out_ref, sems = refs[16:]
    own = place_ref[2]
    copies = copy_all(
        [(received[slot], recv_ref.at[place_ref[3] ^ slot]) for slot in range(8)], sems
    )
    live = lax.broadcasted_iota(jnp.int32, (1, TOK), 1) < mask_length(mask_ref)
    for block in range(4):
        lanes = slice(block * 128, (block + 1) * 128)
        for head, source_ref, rows in ((own, bias_ref, slice(16, 32)), (1 - own, other_bias_ref, slice(16))):
            for core in range(2):
                first, second = swap_halves(
                    source_ref[core, 2 * block, :, rows, :].astype(F32),
                    source_ref[core, 2 * block + 1, :, rows, :].astype(F32),
                )
                full_bias_ref[head, :, core, 0, :, lanes] = first.astype(BF16)
                full_bias_ref[head, :, core, 1, :, lanes] = second.astype(BF16)
    wait_all(copies)
    for block in range(4):
        lanes = slice(block * 128, (block + 1) * 128)
        halves = swap_halves(recv_ref[2 * block].astype(F32), recv_ref[2 * block + 1].astype(F32))
        for sample in range(2):
            half = halves[sample].astype(BF16)
            query_key_ref[sample, :, lanes] = half[: 2 * PAIR]
            for head in range(2):
                at = 2 * PAIR + head * HEAD
                value_ref[sample, head, :HEAD, lanes] = half[at : at + HEAD]
    value_ref[:, :, HEAD:, :] = jnp.ones((2, 2, 16, TOK), BF16)
    for head in range(2):
        bias = full_bias_ref[head].reshape(TOK, TOK)
        for sample in range(2):
            query = query_key_ref[sample, head * HEAD : (head + 1) * HEAD, :]
            key = query_key_ref[sample, PAIR + head * HEAD : PAIR + (head + 1) * HEAD, :]
            scores = dot(query, key, TN) * (HEAD**-0.5) + bias.astype(F32)
            scores = jnp.where(live, scores, -1e30)
            top = jnp.max(scores, axis=1, keepdims=True)
            weights = jnp.exp(scores - top).astype(BF16)
            mixed = dot(value_ref[sample, head], weights, NT)
            mixed_ref[sample, head * HEAD : (head + 1) * HEAD] = mixed[:HEAD] / mixed[HEAD : HEAD + 1]
    for block in range(4):
        lanes = slice(block * 128, (block + 1) * 128)
        first, second = swap_halves(mixed_ref[0, :, lanes], mixed_ref[1, :, lanes])
        out_ref[2 * block] = first.astype(BF16)
        out_ref[2 * block + 1] = second.astype(BF16)
    wait_all(copy_all([(out_ref.at[place_ref[3] ^ slot], sends[slot]) for slot in range(8)], sems))


def tokens_out_kernel(place_ref, gate_in, start_in, weight_in, *refs):
    received = refs[:8]
    out_ref, gate_ref, start_ref, weight_ref, recv_ref, sems = refs[8:]
    wait_all(
        copy_all(
            [(received[slot], recv_ref.at[place_ref[3] ^ slot]) for slot in range(8)]
            + [(gate_in, gate_ref), (start_in, start_ref), (weight_in, weight_ref)],
            sems,
        )
    )
    mixed = jnp.transpose(recv_ref[...].reshape(WIDTH, 128).astype(F32), (1, 0))
    blended = (gate_ref[...] * mixed).astype(BF16)
    out_ref[...] = (start_ref[...] + dot(blended, weight_ref[...])).reshape(2, 64, WIDTH)


def call(
    kernel, name, out_shape, scratch, *operands, smem=0, after=(), far=(), far_out=(), flops=10**8, limit=WIDE
):
    shapes = jax.tree.leaves(out_shape)
    nbytes = sum(v.size * v.dtype.itemsize for v in (*operands, *shapes))
    near = pl.BlockSpec(memory_space=pltpu.VMEM)
    anywhere = pl.BlockSpec(memory_space=pltpu.HBM)
    scalar = pl.BlockSpec(memory_space=pltpu.SMEM)
    outs = [anywhere if index in far_out else near for index in range(len(shapes))]
    return pl.pallas_call(
        kernel,
        name=name,
        out_shape=out_shape,
        in_specs=[
            scalar if index < smem else anywhere if index in far else near
            for index in range(len(operands))
        ]
        + [anywhere] * len(after),
        out_specs=outs if isinstance(out_shape, (list, tuple)) else outs[0],
        scratch_shapes=scratch,
        cost_estimate=pl.CostEstimate(flops=flops, bytes_accessed=nbytes, transcendentals=0),
        compiler_params=pltpu.CompilerParams(vmem_limit_bytes=limit),
    )(*operands, *after)


def shape(*dims, dtype=F32):
    return jax.ShapeDtypeStruct(dims, dtype)


ALL = ("core", "col", "z")


def exchange(value):
    return lax.all_to_all(value, ALL, 0, 0, tiled=True)


def swap(values, axis):
    return [values[0]] + [
        lax.ppermute(values[slot], axis, [(at, at ^ slot) for at in range(8)]) for slot in range(1, 8)
    ]


def on_device(
    pair, pair_mask, prev_pair, diff_tokens, diff_mask, atom_feats, atom_token,
    trunk_in, trunk_out, bias_weight, atom_weight, attn_in, attn_out,
):
    z, core, col = lax.axis_index("z"), lax.axis_index("core"), lax.axis_index("col")
    place = jnp.stack([(z * 2 + core) * ROWS, col * COLS, core, col, z]).astype(jnp.int32)
    tile = (2, 16, COLS, C)
    send = shape(C, 32, 128, dtype=BF16)
    spread = pltpu.VMEM((C * PITCH, 128), F32)
    stage = pltpu.VMEM((C, 32, 128), BF16)
    received = pltpu.VMEM((C * RECV_PITCH, 128), F32)
    square = pltpu.VMEM((8, 2, 2, 16, TOK), BF16)
    sems = pltpu.SemaphoreType.DMA((4,))

    def product(gathered, outgoing, extra):
        rows = 32 if outgoing else 16
        result = call(
            functools.partial(product_kernel, outgoing=outgoing), "product",
            shape(2, 8, 8, rows, 128, dtype=BF16), [square, square],
            gathered.reshape(2, 8, 8, 32, 128), extra, flops=2 * TOK**3, limit=NARROW,
        )
        return exchange(result.reshape(C, rows, 128))

    turned_tile = shape(16, C, 128)
    token_shape = shape(8, 128)

    pair0 = pair.reshape(tile)
    operands = call(
        project_kernel, "project", send,
        [
            pltpu.VMEM((1, TOK), jnp.int32), pltpu.VMEM(tile, F32), pltpu.VMEM((2, C, 5 * C), BF16),
            spread, stage, pltpu.SemaphoreType.DMA((6,)), sems,
        ],
        place, pair_mask, pair0, trunk_in, smem=1, far=(1, 2, 3), far_out=(0,),
    )
    gathered = exchange(operands)

    start, gate2, *parts = call(
        tokens_kernel, "tokens_in",
        [shape(128, WIDTH), shape(128, WIDTH)] + [shape(3 * PAIR, 128, dtype=BF16)] * 8,
        [
            pltpu.VMEM((128, WIDTH), F32), pltpu.VMEM((128, WIDTH), F32),
            pltpu.VMEM((8, 3 * PAIR, 128), BF16), pltpu.SemaphoreType.DMA((10,)),
        ],
        place, diff_tokens[0], atom_feats[0], atom_token, atom_weight, attn_in,
        smem=1, far_out=range(10), after=(operands,),
    )
    bias_here = call(
        bias_kernel, "bias", shape(HEADS, 16, 128, dtype=BF16), [pltpu.VMEM((HEADS * 16, 128), F32)],
        prev_pair.reshape(tile), jnp.swapaxes(bias_weight, 0, 1), after=(parts[0],),
    )
    bias_other = lax.ppermute(bias_here, "grp", [(0, 1), (1, 0)])

    summed0 = product(gathered, True, bias_other)
    parts = swap(parts, "col")
    pair0, gate0 = call(
        gate_kernel, "gate", [turned_tile, turned_tile], [], pair0, trunk_in, after=tuple(parts[1:]),
        limit=MIDDLE,
    )

    pair1, operands = call(
        finish_project_kernel, "finish_project", (turned_tile, send), [received, spread, stage, sems],
        place, pair_mask, summed0, pair0, gate0, trunk_out, trunk_in,
        smem=1, far_out=(1,), limit=NARROW,
    )
    gathered = exchange(operands)
    bias_far = lax.ppermute(summed0[:, 16:, :], "core", [(0, 1), (1, 0)])
    mixed = call(
        attention_kernel, "attention", [shape(PAIR, 128, dtype=BF16)] * 8,
        [
            pltpu.VMEM((8, 3 * PAIR, 128), BF16),
            pltpu.VMEM((2, 2 * PAIR, TOK), BF16),
            pltpu.VMEM((2, 2, HEAD + 16, TOK), BF16),
            pltpu.VMEM((2, 8, 2, 2, 16, TOK), BF16),
            pltpu.VMEM((2, PAIR, TOK), F32),
            pltpu.VMEM((8, PAIR, 128), BF16),
            pltpu.SemaphoreType.DMA((8,)),
        ],
        place, diff_mask, summed0.reshape(2, 8, 8, 32, 128), bias_far.reshape(2, 8, 8, 16, 128), *parts,
        smem=1, far=range(4, 12), far_out=range(8),
    )
    mixed = swap(mixed, "col")
    token = call(fence_kernel, "fence", token_shape, [], after=tuple(mixed[1:]))
    summed1 = product(gathered, False, token)
    tokens_done = call(
        tokens_out_kernel, "tokens_out", shape(2, 64, WIDTH),
        [
            pltpu.VMEM((128, WIDTH), F32), pltpu.VMEM((128, WIDTH), F32), pltpu.VMEM((WIDTH, WIDTH), BF16),
            pltpu.VMEM((8, PAIR, 128), BF16), pltpu.SemaphoreType.DMA((11,)),
        ],
        place, gate2, start, attn_out, *mixed, smem=1, far=range(1, 12),
    )
    pair1, gate1 = call(
        gate_back_kernel, "gate_back", [shape(*tile), shape(*tile)], [], pair1, trunk_in,
        after=(tokens_done,), limit=MIDDLE,
    )
    pair2 = call(
        finish_kernel, "finish", shape(*tile), [received, pltpu.VMEM(tile, F32), sems],
        summed1, pair1, gate1, trunk_out, far_out=(0,), limit=NARROW,
    )
    return (pair2.reshape(1, ROWS, COLS, C), tokens_done[None])


def solution(mesh):
    split = Mesh(mesh.devices.reshape(2, 8, 2, 8), ("grp", "z", "core", "col"))
    row = ("z", "core")
    placed = (
        P("grp", row, "col", None),
        P("grp", None),
        P("grp", row, "col", None),
        P("grp", row, "col", None),
        P("grp", None),
        P("grp", row, "col", None),
        P("grp", "col"),
        P(),
        P(),
        P(),
        P(),
        P(),
        P(),
    )
    return jax.shard_map(
        on_device,
        mesh=split,
        in_specs=placed,
        out_specs=(P("grp", row, "col", None), P("grp", row, "col", None)),
        check_vma=False,
    )
```

time: 192 us -> 180 us (0.938)
  blocking collectives: 38.2 us -> 0 us
  starting transfers between devices: 47.7 us -> 66.2 us
  waiting for transfers between devices: 59 us -> 64.3 us
    all_to_all x1 -> x0, blocking collectives: 38.2 us -> none  [exchange(): return lax.all_to_all(value, axes, 0, 0, tiled=True)]
    ppermute x8 -> x15, starting transfers between devices: 14 us -> 26.9 us  [the longest x14 26.2 us: swap(): lax.ppermute(values[slot], axis, [(at, at ^ slot) for at in range(8)])]
    ppermute x8 -> x15, waiting for transfers between devices: 6.7 us -> 15.9 us  [the longest x14 14.4 us: swap(): lax.ppermute(values[slot], axis, [(at, at ^ slot) for at in range(8)])]
    all_to_all x4, waiting for transfers between devices: 52.3 us -> 44.6 us  [exchange(): return lax.all_to_all(value, ALL, 0, 0, tiled=True)]
    all_to_all x4, starting transfers between devices: 33.2 us -> 38.9 us  [exchange(): return lax.all_to_all(value, ALL, 0, 0, tiled=True)]
    ppermute x1, waiting for transfers between devices: 0.01 us -> 3.81 us  [on_device(): bias_other = lax.ppermute(bias_here, 'grp', [(0, 1), (1, 0)])]
    pallas_call x11 -> x12, Pallas kernels: 32.2 us -> 33.7 us  [call(): pl.pallas_call(kernel, name=name, out_shape=out_shape, in_specs=[scalar i...]
    unnamed x56 -> x72, local copies, waits for them, and re-layouts: 12.6 us -> 13.6 us
  transfers between devices with their start and end apart: 13 -> 20, of which waited for: 6 -> 12; matrix products, arithmetic and copies ran while one was open for 0% -> 0% of each run, Pallas kernels for 11% -> 11%
where the time goes in v3:
time: 180 us
  starting transfers between devices  66.2 us (37%)
  waiting for transfers between devices  64.3 us (36%)
  Pallas kernels  33.7 us (19%)
  local copies, waits for them, and re-layouts  14.3 us (8%)
    all_to_all x4, waiting for transfers between devices, exchange(): return lax.all_to_all(value, ALL, 0, 0, tiled=True)  44.6 us
    all_to_all x4, starting transfers between devices, exchange(): return lax.all_to_all(value, ALL, 0, 0, tiled=True)  38.9 us
    pallas_call x12, Pallas kernels, call(): pl.pallas_call(kernel, name=name, out_shape=out_shape, in_specs=[scalar i...  33.7 us
    ppermute x14, starting transfers between devices, swap(): lax.ppermute(values[slot], axis, [(at, at ^ slot) for at in range(8)])  26.2 us
    ppermute x14, waiting for transfers between devices, swap(): lax.ppermute(values[slot], axis, [(at, at ^ slot) for at in range(8)])  14.4 us
    unnamed x72, local copies, waits for them, and re-layouts  13.6 us
    ppermute x1, waiting for transfers between devices, on_device(): bias_other = lax.ppermute(bias_here, 'grp', [(0, 1), (1, 0)])  3.81 us
  transfers between devices with their start and end apart: 20, of which 12 were waited for; matrix products, arithmetic and copies ran while one was open for 0% of the time, Pallas kernels for 11%

profile of v3, /device:TPU:1, one launch (start us, length us, event | category | flops | bytes accessed | tf_op | source)
XLA Modules:
  0.0 179.6 jit_solution(12218132640329933155)
XLA Ops:
  0.6 0.6 stack.23.place_ref
  1.3 4.7 %project.1.refs_0_ = bf16[128,32,128]{2,1,0:T(8,128)(2,1)} custom-call(s32[5]{0:T(128)} %stack.23.place_ref, s32[1,512]{1,0:T(1,128)} %mask_ref.2, f32[2,16,64,128]{3,2,1,0:T(8,128)} %bitcast.21, bf16[2,128,640]{2,1,0:T(8,128)(2,1)} %weight_ref.5), custom_call_target="tpu_custom_call" | custom-call | flops 100000000 | bytes 2426900 | tf_op jit(solution)/shard_map/project/pallas_call | solution.py:336
  5.9 16.7 %all-to-all-start = ((bf16[128,32,128]{2,1,0:T(8,128)(2,1)}), bf16[128,32,128]{2,1,0:T(8,128)(2,1)S(1)}, u32[]{:S(2)}, u32[]{:S(2)}) async-start(bf16[128,32,128]{2,1,0:T(8,128)(2,1)} %project.1.refs_0_), calls=%async_computation | async-start | bytes 2097152 | tf_op jit(solution)/shard_map/all_to_all | solution.py:360
  22.7 0.0 copy-start.1
  22.7 0.0 copy-start.2
  22.7 5.1 %tokens_in.1 = (f32[128,768]{1,0:T(8,128)}, f32[128,768]{1,0:T(8,128)}, bf16[288,128]{1,0:T(8,128)(2,1)}, bf16[288,128]{1,0:T(8,128)(2,1)}, bf16[288,128]{1,0:T(...) custom-call(s32[5]{0:T(128)} %stack.23.place_ref, ...), custom_call_target="tpu_custom_call" | custom-call | flops 100000000 | bytes 6816788 | tf_op jit(solution)/shard_map/tokens_in/pallas_call | solution.py:336
  27.9 0.0 copy-start.19
  27.9 3.6 %bias.1 = bf16[16,16,128]{2,1,0:T(8,128)(2,1)} custom-call(f32[2,16,64,128]{3,2,1,0:T(8,128)} %bitcast.25, bf16[16,128]{1,0:T(8,128)(2,1)} %bitcast.29, bf16[288,128]{1,0:T(8,128)(2,1)} %get-tuple-element.26.refs_0_), custom_call_target="tpu_custom_call" | custom-call | flops 100000000 | bytes 1118208 | tf_op jit(solution)/shard_map/bias/pallas_call | solution.py:336
  31.5 0.4 collective-permute-start
  31.9 3.8 %collective-permute-done.refs_0_ = bf16[16,16,128]{2,1,0:T(8,128)(2,1)S(1)} collective-permute-done((bf16[16,16,128]{2,1,0:T(8,128)(2,1)}, bf16[16,16,128]{2,1,0:T(8,128)(2,1)S(1)}, u32[]{:S(2)}, u32[]{:S(2)}) %collective-permute-start) | collective-permute-done | bytes 65568 | tf_op jit(solution)/shard_map/ppermute | solution.py:420
  35.7 19.9 %all-to-all-done = bf16[128,32,128]{2,1,0:T(8,128)(2,1)S(1)} async-done(((bf16[128,32,128]{2,1,0:T(8,128)(2,1)}), bf16[128,32,128]{2,1,0:T(8,128)(2,1)S(1)}, u32[]{:S(2)}, u32[]{:S(2)}) %all-to-all-start) | async-done | bytes 1048608 | tf_op jit(solution)/shard_map/all_to_all | solution.py:360
  55.6 2.0 %product.2 = bf16[2,8,8,32,128]{4,3,2,1,0:T(8,128)(2,1)} custom-call(bf16[2,8,8,32,128]{4,3,2,1,0:T(8,128)(2,1)S(1)} %bitcast.20, bf16[16,16,128]{2,1,0:T(8,128)(2,1)S(1)} %collective-permute-done.refs_0_), custom_call_target="tpu_custom_call" | custom-call | flops 268435456 | bytes 2162688 | tf_op jit(solution)/shard_map/product/pallas_call | solution.py:336
  57.6 5.9 %all-to-all-start.1 = ((bf16[128,32,128]{2,1,0:T(8,128)(2,1)}), bf16[128,32,128]{2,1,0:T(8,128)(2,1)S(1)}, u32[]{:S(2)}, u32[]{:S(2)}) async-start(bf16[128,32,128]{2,1,0:T(8,128)(2,1)} %bitcast.11), calls=%async_computation.1 | async-start | bytes 2097152 | tf_op jit(solution)/shard_map/all_to_all | solution.py:360
  63.6 1.5 collective-permute-start.1
  65.1 2.5 %collective-permute-start.2 = (bf16[288,128]{1,0:T(8,128)(2,1)S(1)}, bf16[288,128]{1,0:T(8,128)(2,1)S(1)}, u32[]{:S(2)}, u32[]{:S(2)}) collective-permute-start(bf16[288,128]{1,0:T(8,128)(2,1)S(1)} %copy-done.34), channel_id=1, source_target_pairs={{0,2},{1,3},{2,0},{3,1},{4,6},{5,7},{6,4},{7,5},{8,10},{9,11},{10,... | collective-permute-start | bytes 221192 | tf_op jit(solution)/shard_map/ppermute | solution.py:365
  67.6 3.0 %collective-permute-start.4 = (bf16[288,128]{1,0:T(8,128)(2,1)S(1)}, bf16[288,128]{1,0:T(8,128)(2,1)S(1)}, u32[]{:S(2)}, u32[]{:S(2)}) collective-permute-start(bf16[288,128]{1,0:T(8,128)(2,1)S(1)} %copy-done.32), channel_id=1, source_target_pairs={{0,4},{1,5},{2,6},{3,7},{4,0},{5,1},{6,2},{7,3},{8,12},{9,13},{10,... | collective-permute-start | bytes 221192 | tf_op jit(solution)/shard_map/ppermute | solution.py:365
  70.6 0.0 collective-permute-start.5
  70.6 6.2 %collective-permute-start.6 = (bf16[288,128]{1,0:T(8,128)(2,1)S(1)}, bf16[288,128]{1,0:T(8,128)(2,1)S(1)}, u32[]{:S(2)}, u32[]{:S(2)}) collective-permute-start(bf16[288,128]{1,0:T(8,128)(2,1)S(1)} %copy-done.30), channel_id=1, source_target_pairs={{0,6},{1,7},{2,4},{3,5},{4,2},{5,3},{6,0},{7,1},{8,14},{9,15},{10,... | collective-permute-start | bytes 221192 | tf_op jit(solution)/shard_map/ppermute | solution.py:365
  76.8 0.0 collective-permute-start.7
  76.9 0.2 collective-permute-done.3.refs_2_.refs_3_
  77.1 1.0 collective-permute-done.5.refs_4_.refs_5_
  78.1 3.6 %collective-permute-done.6.refs_5_.refs_6_ = bf16[288,128]{1,0:T(8,128)(2,1)S(1)} collective-permute-done((bf16[288,128]{1,0:T(8,128)(2,1)S(1)}, bf16[288,128]{1,0:T(8,128)(2,1)S(1)}, u32[]{:S(2)}, u32[]{:S(2)}) %collective-permute-start.6) | collective-permute-done | bytes 73760 | tf_op jit(solution)/shard_map/ppermute | solution.py:365
  81.6 2.8 %collective-permute-done.7.refs_6_.refs_7_ = bf16[288,128]{1,0:T(8,128)(2,1)S(1)} collective-permute-done((bf16[288,128]{1,0:T(8,128)(2,1)S(1)}, bf16[288,128]{1,0:T(8,128)(2,1)S(1)}, u32[]{:S(2)}, u32[]{:S(2)}) %collective-permute-start.7) | collective-permute-done | bytes 73760 | tf_op jit(solution)/shard_map/ppermute | solution.py:365
  84.4 0.6 gate.1
  85.0 1.0 copy-done.4
  86.1 0.6 copy-done.10
  86.7 0.6 copy-done.11
  87.3 0.6 copy-done.12
  88.0 0.6 copy-done.13
  88.6 0.6 copy-done.14
  89.2 0.6 copy-done.15
  89.8 6.7 %all-to-all-done.1.recv_ref = bf16[128,32,128]{2,1,0:T(8,128)(2,1)S(1)} async-done(((bf16[128,32,128]{2,1,0:T(8,128)(2,1)}), bf16[128,32,128]{2,1,0:T(8,128)(2,1)S(1)}, u32[]{:S(2)}, u32[]{:S(2)}) %all-to-all-start.1) | async-done | bytes 1048608 | tf_op jit(solution)/shard_map/all_to_all | solution.py:360
  96.5 1.6 copy-done.5
  98.1 0.8 copy-done.16
  99.0 3.4 %finish_project.1 = (f32[16,128,128]{2,1,0:T(8,128)S(1)}, bf16[128,32,128]{2,1,0:T(8,128)(2,1)S(1)}) custom-call(s32[5]{0:T(128)S(1)} %copy-done.18, s32[1,512]{1,0:T(1,128)S(1)} %copy-done.19, bf16[128,32,128]{2,1,0:T(8,128)(2,1)S(1)} %all-to-all-done.1.recv_ref, f32[16,128,128]{2,1,0:T(8,128)S(1)} %get-tuple-element.34.pair_ref, ...), custom_call_target="tpu_custom_call" | custom-call | flops 100000000 | bytes 5638164 | tf_op jit(solution)/shard_map/finish_project/pallas_call | solution.py:336
  102.3 1.0 copy-done.6
  103.4 1.0 copy-done.8
  104.3 8.0 %all-to-all-start.2 = ((bf16[128,32,128]{2,1,0:T(8,128)(2,1)}), bf16[128,32,128]{2,1,0:T(8,128)(2,1)S(1)}, u32[]{:S(2)}, u32[]{:S(2)}) async-start(bf16[128,32,128]{2,1,0:T(8,128)(2,1)} %copy-done.8), calls=%async_computation.2 | async-start | bytes 2097152 | tf_op jit(solution)/shard_map/all_to_all | solution.py:360
  112.4 0.7 collective-permute-start.8
  113.0 1.5 collective-permute-done.8
  114.6 0.8 copy-done.21
  115.3 5.8 %attention.1 = (bf16[96,128]{1,0:T(8,128)(2,1)}, bf16[96,128]{1,0:T(8,128)(2,1)}, bf16[96,128]{1,0:T(8,128)(2,1)}, bf16[96,128]{1,0:T(8,128)(2,1)}, bf16[96,128]...) custom-call(s32[5]{0:T(128)} %stack.23.place_ref, ...), custom_call_target="tpu_custom_call" | custom-call | flops 100000000 | bytes 2361364 | tf_op jit(solution)/shard_map/attention/pallas_call | solution.py:336
  121.1 1.3 collective-permute-start.9
  122.4 2.5 %collective-permute-start.10 = (bf16[96,128]{1,0:T(8,128)(2,1)}, bf16[96,128]{1,0:T(8,128)(2,1)S(1)}, u32[]{:S(2)}, u32[]{:S(2)}) collective-permute-start(bf16[96,128]{1,0:T(8,128)(2,1)} %get-tuple-element.38), channel_id=1, source_target_pairs={{0,2},{1,3},{2,0},{3,1},{4,6},{5,7},{6,4},{7,5},{8,10},{9,11},{10,... | collective-permute-start | bytes 73736 | tf_op jit(solution)/shard_map/ppermute | solution.py:365
  124.9 0.2 collective-permute-start.11
  125.1 2.9 %collective-permute-start.12 = (bf16[96,128]{1,0:T(8,128)(2,1)}, bf16[96,128]{1,0:T(8,128)(2,1)S(1)}, u32[]{:S(2)}, u32[]{:S(2)}) collective-permute-start(bf16[96,128]{1,0:T(8,128)(2,1)} %get-tuple-element.40), channel_id=1, source_target_pairs={{0,4},{1,5},{2,6},{3,7},{4,0},{5,1},{6,2},{7,3},{8,12},{9,13},{10,... | collective-permute-start | bytes 73736 | tf_op jit(solution)/shard_map/ppermute | solution.py:365
  128.0 6.1 %collective-permute-start.14 = (bf16[96,128]{1,0:T(8,128)(2,1)}, bf16[96,128]{1,0:T(8,128)(2,1)S(1)}, u32[]{:S(2)}, u32[]{:S(2)}) collective-permute-start(bf16[96,128]{1,0:T(8,128)(2,1)} %get-tuple-element.42), channel_id=1, source_target_pairs={{0,6},{1,7},{2,4},{3,5},{4,2},{5,3},{6,0},{7,1},{8,14},{9,15},{10,... | collective-permute-start | bytes 73736 | tf_op jit(solution)/shard_map/ppermute | solution.py:365
  134.1 0.0 collective-permute-done.10.refs_1_.refs_2_
  134.1 0.0 collective-permute-start.15
  134.2 2.8 %collective-permute-done.14.refs_5_.refs_6_ = bf16[96,128]{1,0:T(8,128)(2,1)S(1)} collective-permute-done((bf16[96,128]{1,0:T(8,128)(2,1)}, bf16[96,128]{1,0:T(8,128)(2,1)S(1)}, u32[]{:S(2)}, u32[]{:S(2)}) %collective-permute-start.14) | collective-permute-done | bytes 24608 | tf_op jit(solution)/shard_map/ppermute | solution.py:365
  137.0 4.1 %collective-permute-done.15.refs_6_.refs_7_ = bf16[96,128]{1,0:T(8,128)(2,1)S(1)} collective-permute-done((bf16[96,128]{1,0:T(8,128)(2,1)}, bf16[96,128]{1,0:T(8,128)(2,1)S(1)}, u32[]{:S(2)}, u32[]{:S(2)}) %collective-permute-start.15) | collective-permute-done | bytes 24608 | tf_op jit(solution)/shard_map/ppermute | solution.py:365
  141.1 0.6 copy-done.28
  141.7 0.6 fence.1.refs_0_
  142.3 3.0 %all-to-all-done.2 = bf16[128,32,128]{2,1,0:T(8,128)(2,1)S(1)} async-done(((bf16[128,32,128]{2,1,0:T(8,128)(2,1)}), bf16[128,32,128]{2,1,0:T(8,128)(2,1)S(1)}, u32[]{:S(2)}, u32[]{:S(2)}) %all-to-all-start.2) | async-done | bytes 1048608 | tf_op jit(solution)/shard_map/all_to_all | solution.py:360
  145.2 0.7 copy-done.20
  145.9 2.0 %product.3 = bf16[2,8,8,16,128]{4,3,2,1,0:T(8,128)(2,1)} custom-call(bf16[2,8,8,32,128]{4,3,2,1,0:T(8,128)(2,1)S(1)} %bitcast.19, f32[8,128]{1,0:T(8,128)S(1)} %copy-done.20), custom_call_target="tpu_custom_call" | custom-call | flops 268435456 | bytes 1576960 | tf_op jit(solution)/shard_map/product/pallas_call | solution.py:336
  147.9 8.2 %all-to-all-start.3 = ((bf16[128,16,128]{2,1,0:T(8,128)(2,1)}), bf16[128,16,128]{2,1,0:T(8,128)(2,1)S(1)}, u32[]{:S(2)}, u32[]{:S(2)}) async-start(bf16[128,16,128]{2,1,0:T(8,128)(2,1)} %bitcast.15), calls=%async_computation.3 | async-start | bytes 1048576 | tf_op jit(solution)/shard_map/all_to_all | solution.py:360
  156.2 3.5 %tokens_out.1.refs_0_ = f32[2,64,768]{2,1,0:T(8,128)} custom-call(s32[5]{0:T(128)} %stack.23.place_ref, f32[128,768]{1,0:T(8,128)} %get-tuple-element.45.gate_in, f32[128,768]{1,0:T(8,128)} %get-tuple-element.46.start_in, bf16[768,768]{1,0:T(8,128)(2,1)} %weight_in.3, bf16[96,128]{1,0:T(8,128)(2,1)} %get-tuple-element.47.refs_0_, ...), custom_call_target="tpu_custom_call" | custom-call | flops 100000000 | bytes 2555924 | tf_op jit(solution)/shard_map/tokens_out/pallas_call | solution.py:336
  159.7 0.0 copy-start.3
  159.7 1.0 copy-done.3
  160.7 1.2 copy-done.7
  161.9 0.9 gate_back.1
  162.8 15.1 %all-to-all-done.3.recv_ref = bf16[128,16,128]{2,1,0:T(8,128)(2,1)S(1)} async-done(((bf16[128,16,128]{2,1,0:T(8,128)(2,1)}), bf16[128,16,128]{2,1,0:T(8,128)(2,1)S(1)}, u32[]{:S(2)}, u32[]{:S(2)}) %all-to-all-start.3) | async-done | bytes 524320 | tf_op jit(solution)/shard_map/all_to_all | solution.py:360
  177.9 1.5 finish.1
  (62 shorter events, 0.2 us)
Async XLA Ops:
  5.9 49.7 %all-to-all-start = ((bf16[128,32,128]{2,1,0:T(8,128)(2,1)}), bf16[128,32,128]{2,1,0:T(8,128)(2,1)S(1)}, u32[]{:S(2)}, u32[]{:S(2)}) async-start(bf16[128,32,128]{2,1,0:T(8,128)(2,1)} %project.1.refs_0_), calls=%async_computation | async-start | bytes 2097152 | tf_op jit(solution)/shard_map/all_to_all | solution.py:360
  22.7 61.7 %copy-start.1 = (bf16[2,128,640]{2,1,0:T(8,128)(2,1)S(1)}, bf16[2,128,640]{2,1,0:T(8,128)(2,1)}, u32[]{:S(2)}) copy-start(bf16[2,128,640]{2,1,0:T(8,128)(2,1)} %weight_ref.5) | copy-start | bytes 983044
  22.7 61.7 %copy-start.2 = (f32[1,32,64,128]{3,2,1,0:T(8,128)S(1)}, f32[1,32,64,128]{3,2,1,0:T(8,128)}, u32[]{:S(2)}) copy-start(f32[1,32,64,128]{3,2,1,0:T(8,128)} %param.13) | copy-start | bytes 3145732
  27.8 35.7 %copy-start.35 = (bf16[288,128]{1,0:T(8,128)(2,1)S(1)}, bf16[288,128]{1,0:T(8,128)(2,1)}, u32[]{:S(2)}) copy-start(bf16[288,128]{1,0:T(8,128)(2,1)} %get-tuple-element.27) | copy-start | bytes 221188
  27.8 37.2 %copy-start.34 = (bf16[288,128]{1,0:T(8,128)(2,1)S(1)}, bf16[288,128]{1,0:T(8,128)(2,1)}, u32[]{:S(2)}) copy-start(bf16[288,128]{1,0:T(8,128)(2,1)} %get-tuple-element.28) | copy-start | bytes 221188
  27.9 39.7 %copy-start.33 = (bf16[288,128]{1,0:T(8,128)(2,1)S(1)}, bf16[288,128]{1,0:T(8,128)(2,1)}, u32[]{:S(2)}) copy-start(bf16[288,128]{1,0:T(8,128)(2,1)} %get-tuple-element.29) | copy-start | bytes 221188
  27.9 39.7 %copy-start.32 = (bf16[288,128]{1,0:T(8,128)(2,1)S(1)}, bf16[288,128]{1,0:T(8,128)(2,1)}, u32[]{:S(2)}) copy-start(bf16[288,128]{1,0:T(8,128)(2,1)} %get-tuple-element.30) | copy-start | bytes 221188
  27.9 42.7 %copy-start.31 = (bf16[288,128]{1,0:T(8,128)(2,1)S(1)}, bf16[288,128]{1,0:T(8,128)(2,1)}, u32[]{:S(2)}) copy-start(bf16[288,128]{1,0:T(8,128)(2,1)} %get-tuple-element.31) | copy-start | bytes 221188
  27.9 42.7 %copy-start.30 = (bf16[288,128]{1,0:T(8,128)(2,1)S(1)}, bf16[288,128]{1,0:T(8,128)(2,1)}, u32[]{:S(2)}) copy-start(bf16[288,128]{1,0:T(8,128)(2,1)} %get-tuple-element.32) | copy-start | bytes 221188
  27.9 49.0 %copy-start.29 = (bf16[288,128]{1,0:T(8,128)(2,1)S(1)}, bf16[288,128]{1,0:T(8,128)(2,1)}, u32[]{:S(2)}) copy-start(bf16[288,128]{1,0:T(8,128)(2,1)} %get-tuple-element.33) | copy-start | bytes 221188
  27.9 68.6 %copy-start.18 = (s32[5]{0:T(128)S(1)}, s32[5]{0:T(128)}, u32[]{:S(2)}) copy-start(s32[5]{0:T(128)} %stack.23.place_ref) | copy-start | bytes 64
  27.9 68.6 %copy-start.19 = (s32[1,512]{1,0:T(1,128)S(1)}, s32[1,512]{1,0:T(1,128)}, u32[]{:S(2)}) copy-start(s32[1,512]{1,0:T(1,128)} %mask_ref.2) | copy-start | bytes 6148
  31.5 4.2 %collective-permute-start = (bf16[16,16,128]{2,1,0:T(8,128)(2,1)}, bf16[16,16,128]{2,1,0:T(8,128)(2,1)S(1)}, u32[]{:S(2)}, u32[]{:S(2)}) collective-permute-start(bf16[16,16,128]{2,1,0:T(8,128)(2,1)} %bias.1), channel_id=1, source_target_pairs={{0,128},{128,0},{1,129},{129,1},{2,130},{130,2},{3,131},{131,3},{4... | collective-permute-start | bytes 196616 | tf_op jit(solution)/shard_map/ppermute | solution.py:420
  57.6 38.9 %all-to-all-start.1 = ((bf16[128,32,128]{2,1,0:T(8,128)(2,1)}), bf16[128,32,128]{2,1,0:T(8,128)(2,1)S(1)}, u32[]{:S(2)}, u32[]{:S(2)}) async-start(bf16[128,32,128]{2,1,0:T(8,128)(2,1)} %bitcast.11), calls=%async_computation.1 | async-start | bytes 2097152 | tf_op jit(solution)/shard_map/all_to_all | solution.py:360
  63.6 7.0 %collective-permute-start.1 = (bf16[288,128]{1,0:T(8,128)(2,1)S(1)}, bf16[288,128]{1,0:T(8,128)(2,1)S(1)}, u32[]{:S(2)}, u32[]{:S(2)}) collective-permute-start(bf16[288,128]{1,0:T(8,128)(2,1)S(1)} %copy-done.35), channel_id=1, source_target_pairs={{0,1},{1,0},{2,3},{3,2},{4,5},{5,4},{6,7},{7,6},{8,9},{9,8},{10,11... | collective-permute-start | bytes 221192 | tf_op jit(solution)/shard_map/ppermute | solution.py:365
  65.1 11.8 %collective-permute-start.2 = (bf16[288,128]{1,0:T(8,128)(2,1)S(1)}, bf16[288,128]{1,0:T(8,128)(2,1)S(1)}, u32[]{:S(2)}, u32[]{:S(2)}) collective-permute-start(bf16[288,128]{1,0:T(8,128)(2,1)S(1)} %copy-done.34), channel_id=1, source_target_pairs={{0,2},{1,3},{2,0},{3,1},{4,6},{5,7},{6,4},{7,5},{8,10},{9,11},{10,... | collective-permute-start | bytes 221192 | tf_op jit(solution)/shard_map/ppermute | solution.py:365
  67.6 9.5 %collective-permute-start.3 = (bf16[288,128]{1,0:T(8,128)(2,1)S(1)}, bf16[288,128]{1,0:T(8,128)(2,1)S(1)}, u32[]{:S(2)}, u32[]{:S(2)}) collective-permute-start(bf16[288,128]{1,0:T(8,128)(2,1)S(1)} %copy-done.33), channel_id=1, source_target_pairs={{0,3},{1,2},{2,1},{3,0},{4,7},{5,6},{6,5},{7,4},{8,11},{9,10},{10,... | collective-permute-start | bytes 221192 | tf_op jit(solution)/shard_map/ppermute | solution.py:365
  67.6 9.5 %collective-permute-start.4 = (bf16[288,128]{1,0:T(8,128)(2,1)S(1)}, bf16[288,128]{1,0:T(8,128)(2,1)S(1)}, u32[]{:S(2)}, u32[]{:S(2)}) collective-permute-start(bf16[288,128]{1,0:T(8,128)(2,1)S(1)} %copy-done.32), channel_id=1, source_target_pairs={{0,4},{1,5},{2,6},{3,7},{4,0},{5,1},{6,2},{7,3},{8,12},{9,13},{10,... | collective-permute-start | bytes 221192 | tf_op jit(solution)/shard_map/ppermute | solution.py:365
  70.6 7.4 %collective-permute-start.5 = (bf16[288,128]{1,0:T(8,128)(2,1)S(1)}, bf16[288,128]{1,0:T(8,128)(2,1)S(1)}, u32[]{:S(2)}, u32[]{:S(2)}) collective-permute-start(bf16[288,128]{1,0:T(8,128)(2,1)S(1)} %copy-done.31), channel_id=1, source_target_pairs={{0,5},{1,4},{2,7},{3,6},{4,1},{5,0},{6,3},{7,2},{8,13},{9,12},{10,... | collective-permute-start | bytes 221192 | tf_op jit(solution)/shard_map/ppermute | solution.py:365
  70.6 44.7 %copy-start.9 = (bf16[288,128]{1,0:T(8,128)(2,1)}, bf16[288,128]{1,0:T(8,128)(2,1)S(1)}, u32[]{:S(2)}) copy-start(bf16[288,128]{1,0:T(8,128)(2,1)S(1)} %collective-permute-done.1.refs_0_.refs_1_) | copy-start | bytes 221188
  70.6 11.0 %collective-permute-start.6 = (bf16[288,128]{1,0:T(8,128)(2,1)S(1)}, bf16[288,128]{1,0:T(8,128)(2,1)S(1)}, u32[]{:S(2)}, u32[]{:S(2)}) collective-permute-start(bf16[288,128]{1,0:T(8,128)(2,1)S(1)} %copy-done.30), channel_id=1, source_target_pairs={{0,6},{1,7},{2,4},{3,5},{4,2},{5,3},{6,0},{7,1},{8,14},{9,15},{10,... | collective-permute-start | bytes 221192 | tf_op jit(solution)/shard_map/ppermute | solution.py:365
  76.8 7.5 %collective-permute-start.7 = (bf16[288,128]{1,0:T(8,128)(2,1)S(1)}, bf16[288,128]{1,0:T(8,128)(2,1)S(1)}, u32[]{:S(2)}, u32[]{:S(2)}) collective-permute-start(bf16[288,128]{1,0:T(8,128)(2,1)S(1)} %copy-done.29), channel_id=1, source_target_pairs={{0,7},{1,6},{2,5},{3,4},{4,3},{5,2},{6,1},{7,0},{8,15},{9,14},{10,... | collective-permute-start | bytes 221192 | tf_op jit(solution)/shard_map/ppermute | solution.py:365
  85.0 1.0 copy-start.4
  86.1 0.6 copy-start.10
  86.7 0.6 copy-start.11
  87.3 0.6 copy-start.12
  88.0 0.6 copy-start.13
  88.6 0.6 copy-start.14
  89.2 0.6 copy-start.15
  96.5 18.8 %copy-start = (bf16[128,32,128]{2,1,0:T(8,128)(2,1)}, bf16[128,32,128]{2,1,0:T(8,128)(2,1)S(1)}, u32[]{:S(2)}) copy-start(bf16[128,32,128]{2,1,0:T(8,128)(2,1)S(1)} %all-to-all-done.1.recv_ref) | copy-start | bytes 3145732
  96.5 1.6 copy-start.5
  98.1 0.8 copy-start.16
  102.3 1.0 copy-start.6
  103.3 1.0 copy-start.8
  104.3 40.9 %all-to-all-start.2 = ((bf16[128,32,128]{2,1,0:T(8,128)(2,1)}), bf16[128,32,128]{2,1,0:T(8,128)(2,1)S(1)}, u32[]{:S(2)}, u32[]{:S(2)}) async-start(bf16[128,32,128]{2,1,0:T(8,128)(2,1)} %copy-done.8), calls=%async_computation.2 | async-start | bytes 2097152 | tf_op jit(solution)/shard_map/all_to_all | solution.py:360
  112.4 2.2 %collective-permute-start.8 = (bf16[128,16,128]{2,1,0:T(8,128)(2,1)S(1)}, bf16[128,16,128]{2,1,0:T(8,128)(2,1)S(1)}, u32[]{:S(2)}, u32[]{:S(2)}) collective-permute-start(bf16[128,16,128]{2,1,0:T(8,128)(2,1)S(1)} %slice.4), channel_id=1, source_target_pairs={{0,8},{8,0},{1,9},{9,1},{2,10},{10,2},{3,11},{11,3},{4,12},{12,4},... | collective-permute-start | bytes 1572872 | tf_op jit(solution)/shard_map/ppermute | solution.py:435
  114.6 0.8 copy-start.21
  115.3 62.5 %copy-start.17 = (bf16[2,128,128]{2,1,0:T(8,128)(2,1)S(1)}, bf16[2,128,128]{2,1,0:T(8,128)(2,1)}, u32[]{:S(2)}) copy-start(bf16[2,128,128]{2,1,0:T(8,128)(2,1)} %out_weight_ref.3) | copy-start | bytes 196612
  121.1 6.8 %collective-permute-start.9 = (bf16[96,128]{1,0:T(8,128)(2,1)}, bf16[96,128]{1,0:T(8,128)(2,1)S(1)}, u32[]{:S(2)}, u32[]{:S(2)}) collective-permute-start(bf16[96,128]{1,0:T(8,128)(2,1)} %get-tuple-element.37), channel_id=1, source_target_pairs={{0,1},{1,0},{2,3},{3,2},{4,5},{5,4},{6,7},{7,6},{8,9},{9,8},{10,11... | collective-permute-start | bytes 73736 | tf_op jit(solution)/shard_map/ppermute | solution.py:365
  122.4 11.7 %collective-permute-start.10 = (bf16[96,128]{1,0:T(8,128)(2,1)}, bf16[96,128]{1,0:T(8,128)(2,1)S(1)}, u32[]{:S(2)}, u32[]{:S(2)}) collective-permute-start(bf16[96,128]{1,0:T(8,128)(2,1)} %get-tuple-element.38), channel_id=1, source_target_pairs={{0,2},{1,3},{2,0},{3,1},{4,6},{5,7},{6,4},{7,5},{8,10},{9,11},{10,... | collective-permute-start | bytes 73736 | tf_op jit(solution)/shard_map/ppermute | solution.py:365
  124.9 9.2 %collective-permute-start.11 = (bf16[96,128]{1,0:T(8,128)(2,1)}, bf16[96,128]{1,0:T(8,128)(2,1)S(1)}, u32[]{:S(2)}, u32[]{:S(2)}) collective-permute-start(bf16[96,128]{1,0:T(8,128)(2,1)} %get-tuple-element.39), channel_id=1, source_target_pairs={{0,3},{1,2},{2,1},{3,0},{4,7},{5,6},{6,5},{7,4},{8,11},{9,10},{10,... | collective-permute-start | bytes 73736 | tf_op jit(solution)/shard_map/ppermute | solution.py:365
  125.1 9.1 %collective-permute-start.12 = (bf16[96,128]{1,0:T(8,128)(2,1)}, bf16[96,128]{1,0:T(8,128)(2,1)S(1)}, u32[]{:S(2)}, u32[]{:S(2)}) collective-permute-start(bf16[96,128]{1,0:T(8,128)(2,1)} %get-tuple-element.40), channel_id=1, source_target_pairs={{0,4},{1,5},{2,6},{3,7},{4,0},{5,1},{6,2},{7,3},{8,12},{9,13},{10,... | collective-permute-start | bytes 73736 | tf_op jit(solution)/shard_map/ppermute | solution.py:365
  128.0 6.2 %collective-permute-start.13 = (bf16[96,128]{1,0:T(8,128)(2,1)}, bf16[96,128]{1,0:T(8,128)(2,1)S(1)}, u32[]{:S(2)}, u32[]{:S(2)}) collective-permute-start(bf16[96,128]{1,0:T(8,128)(2,1)} %get-tuple-element.41), channel_id=1, source_target_pairs={{0,5},{1,4},{2,7},{3,6},{4,1},{5,0},{6,3},{7,2},{8,13},{9,12},{10,... | collective-permute-start | bytes 73736 | tf_op jit(solution)/shard_map/ppermute | solution.py:365
  128.0 13.1 %copy-start.22 = (bf16[96,128]{1,0:T(8,128)(2,1)}, bf16[96,128]{1,0:T(8,128)(2,1)S(1)}, u32[]{:S(2)}) copy-start(bf16[96,128]{1,0:T(8,128)(2,1)S(1)} %collective-permute-done.9.refs_0_.refs_1_) | copy-start | bytes 73732
  128.0 9.0 %collective-permute-start.14 = (bf16[96,128]{1,0:T(8,128)(2,1)}, bf16[96,128]{1,0:T(8,128)(2,1)S(1)}, u32[]{:S(2)}, u32[]{:S(2)}) collective-permute-start(bf16[96,128]{1,0:T(8,128)(2,1)} %get-tuple-element.42), channel_id=1, source_target_pairs={{0,6},{1,7},{2,4},{3,5},{4,2},{5,3},{6,0},{7,1},{8,14},{9,15},{10,... | collective-permute-start | bytes 73736 | tf_op jit(solution)/shard_map/ppermute | solution.py:365
  134.1 6.9 %copy-start.23 = (bf16[96,128]{1,0:T(8,128)(2,1)}, bf16[96,128]{1,0:T(8,128)(2,1)S(1)}, u32[]{:S(2)}) copy-start(bf16[96,128]{1,0:T(8,128)(2,1)S(1)} %collective-permute-done.10.refs_1_.refs_2_) | copy-start | bytes 73732
  134.1 6.9 %collective-permute-start.15 = (bf16[96,128]{1,0:T(8,128)(2,1)}, bf16[96,128]{1,0:T(8,128)(2,1)S(1)}, u32[]{:S(2)}, u32[]{:S(2)}) collective-permute-start(bf16[96,128]{1,0:T(8,128)(2,1)} %get-tuple-element.43), channel_id=1, source_target_pairs={{0,7},{1,6},{2,5},{3,4},{4,3},{5,2},{6,1},{7,0},{8,15},{9,14},{10,... | collective-permute-start | bytes 73736 | tf_op jit(solution)/shard_map/ppermute | solution.py:365
  134.1 6.9 %copy-start.24 = (bf16[96,128]{1,0:T(8,128)(2,1)}, bf16[96,128]{1,0:T(8,128)(2,1)S(1)}, u32[]{:S(2)}) copy-start(bf16[96,128]{1,0:T(8,128)(2,1)S(1)} %collective-permute-done.11.refs_2_.refs_3_) | copy-start | bytes 73732
  134.2 6.9 %copy-start.25 = (bf16[96,128]{1,0:T(8,128)(2,1)}, bf16[96,128]{1,0:T(8,128)(2,1)S(1)}, u32[]{:S(2)}) copy-start(bf16[96,128]{1,0:T(8,128)(2,1)S(1)} %collective-permute-done.12.refs_3_.refs_4_) | copy-start | bytes 73732
  134.2 6.9 %copy-start.26 = (bf16[96,128]{1,0:T(8,128)(2,1)}, bf16[96,128]{1,0:T(8,128)(2,1)S(1)}, u32[]{:S(2)}) copy-start(bf16[96,128]{1,0:T(8,128)(2,1)S(1)} %collective-permute-done.13.refs_4_.refs_5_) | copy-start | bytes 73732
  137.0 4.1 %copy-start.27 = (bf16[96,128]{1,0:T(8,128)(2,1)}, bf16[96,128]{1,0:T(8,128)(2,1)S(1)}, u32[]{:S(2)}) copy-start(bf16[96,128]{1,0:T(8,128)(2,1)S(1)} %collective-permute-done.14.refs_5_.refs_6_) | copy-start | bytes 73732
  141.1 0.6 copy-start.28
  145.2 0.7 copy-start.20
  147.9 29.9 %all-to-all-start.3 = ((bf16[128,16,128]{2,1,0:T(8,128)(2,1)}), bf16[128,16,128]{2,1,0:T(8,128)(2,1)S(1)}, u32[]{:S(2)}, u32[]{:S(2)}) async-start(bf16[128,16,128]{2,1,0:T(8,128)(2,1)} %bitcast.15), calls=%async_computation.3 | async-start | bytes 1048576 | tf_op jit(solution)/shard_map/all_to_all | solution.py:360
  159.7 1.0 copy-start.3
  160.7 1.2 copy-start.7

commit v4 on v3

--- a/solution.py
+++ b/solution.py
@@ -13,6 +13,7 @@
 HEADS, HEAD = 16, 48
 WIDTH, PAIR = HEADS * HEAD, 2 * HEAD
 WIDE, MIDDLE, NARROW = 63_000_000, 40_000_000, 24 * 2**20
+FINISH = 24 * 2**20
 PITCH, RECV_PITCH = 40, 24
 NT = (((1,), (1,)), ((), ()))
 TN = (((0,), (0,)), ((), ()))
@@ -49,39 +50,41 @@
     return jnp.transpose(weight.astype(F32), (1, 0)).astype(BF16)
 
 
-def project_step(values, step, length, row0, col0, weight, spread_ref):
-    normed = layer_norm(values, 0).astype(BF16)
+def quarter_weight(weight):
+    return turned(weight).reshape(4, 4, 32, C)
+
+
+def project_out(normed_ref, weight, length, row0, col0, spread_ref, stage_ref, out_ref, sems):
     lane = lax.broadcasted_iota(jnp.int32, (1, 128), 1)
     half = (lane >= 64).astype(jnp.int32)
-    row = row0 + half * 16 + step
-    col = col0 + lane - half * 64
-    live = jnp.logical_and(row < length, col < length).astype(F32)
-    projected = dot(weight, normed)
-    left = live * jax.nn.sigmoid(projected[:C]) * projected[C : 2 * C]
-    right = live * jax.nn.sigmoid(projected[2 * C : 3 * C]) * projected[3 * C :]
-    spread_ref[pl.ds(step, C, stride=PITCH), :] = left
-    spread_ref[pl.ds(step + 16, C, stride=PITCH), :] = right
-
-
-def mask_length(mask_ref):
-    return jnp.sum(mask_ref[...])
-
-
-def send_out(spread_ref, stage_ref, out_ref, sems):
+    col_live = col0 + lane - half * 64 < length
     copies = []
-    for part in range(4):
-        chunk = pl.ds(part * 32, 32)
-        values = spread_ref[pl.ds(part * 32 * PITCH, 32 * PITCH), :].reshape(32, PITCH, 128)
+    for quarter in range(4):
+        part_weight = jnp.concatenate([weight[part, quarter] for part in range(4)], axis=0)
+        base = quarter * 32 * PITCH
+        for step in range(16):
+            live = jnp.logical_and(row0 + half * 16 + step < length, col_live).astype(F32)
+            projected = dot(part_weight, normed_ref[step])
+            left = live * jax.nn.sigmoid(projected[:32]) * projected[32:64]
+            right = live * jax.nn.sigmoid(projected[64:96]) * projected[96:]
+            spread_ref[pl.ds(base + step, 32, stride=PITCH), :] = left
+            spread_ref[pl.ds(base + step + 16, 32, stride=PITCH), :] = right
+        chunk = pl.ds(quarter * 32, 32)
+        values = spread_ref[pl.ds(base, 32 * PITCH), :].reshape(32, PITCH, 128)
         stage_ref[chunk] = values[:, :32].astype(BF16)
-        copies.append(pltpu.make_async_copy(stage_ref.at[chunk], out_ref.at[chunk], sems.at[part]))
+        copies.append(pltpu.make_async_copy(stage_ref.at[chunk], out_ref.at[chunk], sems.at[quarter]))
         copies[-1].start()
     for copy in copies:
         copy.wait()
 
 
+def mask_length(mask_ref):
+    return jnp.sum(mask_ref[...])
+
+
 def project_kernel(
     place_ref, mask_in, pair_in, weight_in, out_ref,
-    mask_ref, pair_ref, weight_ref, spread_ref, stage_ref, in_sems, out_sems,
+    mask_ref, pair_ref, weight_ref, normed_ref, spread_ref, stage_ref, in_sems, out_sems,
 ):
     copies = [
         pltpu.make_async_copy(mask_in, mask_ref, in_sems.at[4]),
@@ -97,22 +100,20 @@
     copies[0].wait()
     copies[1].wait()
     length = mask_length(mask_ref)
-    weight = turned(weight_ref[0, :, : 4 * C])
+    weight = quarter_weight(weight_ref[0, :, : 4 * C])
     for part in range(4):
         copies[2 + part].wait()
         for step in range(part * 4, part * 4 + 4):
             values = jnp.transpose(pair_step(pair_ref, step), (1, 0))
-            project_step(values, step, length, place_ref[0], place_ref[1], weight, spread_ref)
-    send_out(spread_ref, stage_ref, out_ref, out_sems)
-
-
-def gate_kernel(pair_ref, weight_ref, *refs):
-    pair_out_ref, gate_ref = refs[-2:]
-    weight = turned(weight_ref[0, :, 4 * C :])
+            normed_ref[step] = layer_norm(values, 0).astype(BF16)
+    project_out(
+        normed_ref, weight, length, place_ref[0], place_ref[1], spread_ref, stage_ref, out_ref, out_sems
+    )
+
+
+def turn_kernel(pair_ref, *refs):
     for step in range(16):
-        values = jnp.transpose(pair_step(pair_ref, step), (1, 0))
-        pair_out_ref[step] = values
-        gate_ref[step] = jax.nn.sigmoid(dot(weight, layer_norm(values, 0).astype(BF16)))
+        refs[-1][step] = jnp.transpose(pair_step(pair_ref, step), (1, 0))
 
 
 def gate_back_kernel(pair_ref, weight_ref, *refs):
@@ -125,42 +126,77 @@
         gate_ref[:, step] = jnp.transpose(gate, (1, 0)).reshape(2, COLS, C)
 
 
-def product_kernel(recv_ref, *refs, outgoing):
-    out_ref, left_ref, right_ref = refs[-3:]
-    if outgoing:
-        bias_ref = refs[0]
-        for core in range(2):
-            for col in range(8):
-                tile = bias_ref[2 * col + core]
-                out_ref[core, col, :, 16:, :] = jnp.broadcast_to(tile[None], (8, 16, 128))
+def tiles_to_rows(recv_ref, rows, channel, dest):
     for block in range(4):
         lanes = slice(block * 128, (block + 1) * 128)
-        for side, dest_ref in ((0, left_ref), (1, right_ref)):
-            rows = slice(side * 16, side * 16 + 16)
-            for core in range(2):
-                first, second = swap_halves(
-                    recv_ref[core, 2 * block, :, rows, :].astype(F32),
-                    recv_ref[core, 2 * block + 1, :, rows, :].astype(F32),
-                )
-                dest_ref[:, core, 0, :, lanes] = first.astype(BF16)
-                dest_ref[:, core, 1, :, lanes] = second.astype(BF16)
-    left = left_ref[...].reshape(TOK, TOK)
-    right = right_ref[...].reshape(TOK, TOK)
-    for block in range(4):
-        lanes = slice(block * 128, (block + 1) * 128)
-        if outgoing:
-            summed = dot(left, right[lanes], NT)
-        else:
-            summed = dot(left, right[:, lanes], TN)
-        summed = summed.reshape(8, 2, 2, 16, 128)
-        for core in range(2):
-            first, second = swap_halves(summed[:, core, 0], summed[:, core, 1])
-            out_ref[core, 2 * block, :, :16, :] = first.astype(BF16)
-            out_ref[core, 2 * block + 1, :, :16, :] = second.astype(BF16)
+        halves = swap_halves(
+            recv_ref[:, 2 * block, channel, rows, :].astype(F32),
+            recv_ref[:, 2 * block + 1, channel, rows, :].astype(F32),
+        )
+        for half in range(2):
+            ref, index = dest(half, lanes)
+            ref[index] = halves[half].astype(BF16)
+
+
+def outgoing_kernel(place_ref, recv_ref, far_ref, bias_ref, out_ref, left_ref, right_ref):
+    own = place_ref[2]
+    for head in range(2):
+        for col in range(8):
+            tile = bias_ref[2 * col + head]
+            rows = slice(32 + 16 * head, 48 + 16 * head)
+            out_ref[:, col, rows, :] = jnp.broadcast_to(tile[None], (8, 16, 128))
+    for channel in range(2):
+        tiles_to_rows(
+            recv_ref, slice(16), channel,
+            lambda half, lanes: (left_ref, (channel, slice(None), half, slice(None), lanes)),
+        )
+        for core, ref, rows in ((own, recv_ref, slice(16, 32)), (1 - own, far_ref, slice(16))):
+            tiles_to_rows(
+                ref, rows, channel,
+                lambda half, lanes: (right_ref, (channel, slice(None), core, half, slice(None), lanes)),
+            )
+        left = left_ref[channel].reshape(TOK // 2, TOK)
+        right = right_ref[channel].reshape(TOK, TOK)
+        rows = slice(16 * channel, 16 * channel + 16)
+        for block in range(4):
+            summed = dot(left, right[block * 128 : (block + 1) * 128], NT).reshape(8, 2, 16, 128)
+            first, second = swap_halves(summed[:, 0], summed[:, 1])
+            out_ref[:, 2 * block, rows, :] = first.astype(BF16)
+            out_ref[:, 2 * block + 1, rows, :] = second.astype(BF16)
+
+
+def take_right_kernel(recv_ref, bias_ref, out_ref):
+    out_ref[...] = recv_ref[:, :, :, 16:, :]
+
+
+def incoming_kernel(place_ref, recv_ref, token_ref, own_ref, far_ref, left_ref, right_ref):
+    first_core = place_ref[2] == 0
+    for channel in range(2):
+        for ref, rows in ((left_ref, slice(16)), (right_ref, slice(16, 32))):
+            tiles_to_rows(
+                recv_ref, rows, channel,
+                lambda half, lanes: (ref, (channel, slice(None), half, slice(None), lanes)),
+            )
+        left = left_ref[channel].reshape(TOK // 2, TOK)
+        right = right_ref[channel].reshape(TOK // 2, TOK)
+        rows = slice(16 * channel, 16 * channel + 16)
+        for block in range(4):
+            summed = dot(left, right[:, block * 128 : (block + 1) * 128], TN).reshape(8, 2, 2, 16, 128)
+            for out_ref, kept in (
+                (own_ref, jnp.where(first_core, summed[:, 0], summed[:, 1])),
+                (far_ref, jnp.where(first_core, summed[:, 1], summed[:, 0])),
+            ):
+                first, second = swap_halves(kept[:, 0], kept[:, 1])
+                out_ref[:, 2 * block, rows, :] = first.astype(BF16)
+                out_ref[:, 2 * block + 1, rows, :] = second.astype(BF16)
+
+
+def add_kernel(own_ref, far_ref, out_ref):
+    out_ref[...] = (own_ref[...].astype(F32) + far_ref[...].astype(F32)).astype(BF16)
 
 
 def load_summed(recv_ref, recv_f32_ref):
-    recv_f32_ref.reshape(C, RECV_PITCH, 128)[:, :16] = recv_ref[:, :16, :].astype(F32)
+    recv_f32_ref.reshape(C, RECV_PITCH, 128)[:, :16] = recv_ref[:, :32, :].reshape(C, 16, 128).astype(F32)
 
 
 def normed_sum(recv_f32_ref, step):
@@ -168,19 +204,23 @@
 
 
 def finish_project_kernel(
-    place_ref, mask_ref, recv_ref, pair_ref, gate_ref, out_weight_ref, in_weight_ref,
-    pair_out_ref, out_ref, recv_f32_ref, spread_ref, stage_ref, out_sems,
+    place_ref, mask_ref, recv_ref, pair_ref, out_weight_ref, in_weight_ref,
+    pair_out_ref, out_ref, recv_f32_ref, normed_ref, spread_ref, stage_ref, out_sems,
 ):
     length = mask_length(mask_ref)
-    weight = turned(in_weight_ref[1, :, : 4 * C])
+    weight = quarter_weight(in_weight_ref[1, :, : 4 * C])
+    gate_weight = turned(in_weight_ref[0, :, 4 * C :])
     out_weight = turned(out_weight_ref[0])
     load_summed(recv_ref, recv_f32_ref)
     for step in range(16):
-        update = dot(out_weight, normed_sum(recv_f32_ref, step))
-        values = pair_ref[step] + gate_ref[step] * update
+        values = pair_ref[step]
+        gate = jax.nn.sigmoid(dot(gate_weight, layer_norm(values, 0).astype(BF16)))
+        values = values + gate * dot(out_weight, normed_sum(recv_f32_ref, step))
         pair_out_ref[step] = values
-        project_step(values, step, length, place_ref[0], place_ref[1], weight, spread_ref)
-    send_out(spread_ref, stage_ref, out_ref, out_sems)
+        normed_ref[step] = layer_norm(values, 0).astype(BF16)
+    project_out(
+        normed_ref, weight, length, place_ref[0], place_ref[1], spread_ref, stage_ref, out_ref, out_sems
+    )
 
 
 def finish_kernel(recv_ref, pair_ref, gate_ref, out_weight_ref, out_ref, recv_f32_ref, stage_ref, sems):
@@ -271,11 +311,12 @@
     live = lax.broadcasted_iota(jnp.int32, (1, TOK), 1) < mask_length(mask_ref)
     for block in range(4):
         lanes = slice(block * 128, (block + 1) * 128)
-        for head, source_ref, rows in ((own, bias_ref, slice(16, 32)), (1 - own, other_bias_ref, slice(16))):
-            for core in range(2):
+        for core, source_ref, base in ((own, bias_ref, 32), (1 - own, other_bias_ref, 0)):
+            for head in range(2):
+                rows = slice(base + 16 * head, base + 16 * head + 16)
                 first, second = swap_halves(
-                    source_ref[core, 2 * block, :, rows, :].astype(F32),
-                    source_ref[core, 2 * block + 1, :, rows, :].astype(F32),
+                    source_ref[:, 2 * block, rows, :].astype(F32),
+                    source_ref[:, 2 * block + 1, rows, :].astype(F32),
                 )
                 full_bias_ref[head, :, core, 0, :, lanes] = first.astype(BF16)
                 full_bias_ref[head, :, core, 1, :, lanes] = second.astype(BF16)
@@ -353,7 +394,12 @@
     return jax.ShapeDtypeStruct(dims, dtype)
 
 
-ALL = ("core", "col", "z")
+ALL = ("z", "col")
+EARLY, LATE = 4, 6
+
+
+def from_other_core(value):
+    return lax.ppermute(value, "core", [(0, 1), (1, 0)])
 
 
 def exchange(value):
@@ -374,20 +420,13 @@
     place = jnp.stack([(z * 2 + core) * ROWS, col * COLS, core, col, z]).astype(jnp.int32)
     tile = (2, 16, COLS, C)
     send = shape(C, 32, 128, dtype=BF16)
+    normed = pltpu.VMEM((16, C, 128), BF16)
     spread = pltpu.VMEM((C * PITCH, 128), F32)
     stage = pltpu.VMEM((C, 32, 128), BF16)
     received = pltpu.VMEM((C * RECV_PITCH, 128), F32)
-    square = pltpu.VMEM((8, 2, 2, 16, TOK), BF16)
+    half = pltpu.VMEM((2, 8, 2, 16, TOK), BF16)
+    sums = shape(8, 8, 32, 128, dtype=BF16)
     sems = pltpu.SemaphoreType.DMA((4,))
-
-    def product(gathered, outgoing, extra):
-        rows = 32 if outgoing else 16
-        result = call(
-            functools.partial(product_kernel, outgoing=outgoing), "product",
-            shape(2, 8, 8, rows, 128, dtype=BF16), [square, square],
-            gathered.reshape(2, 8, 8, 32, 128), extra, flops=2 * TOK**3, limit=NARROW,
-        )
-        return exchange(result.reshape(C, rows, 128))
 
     turned_tile = shape(16, C, 128)
     token_shape = shape(8, 128)
@@ -397,11 +436,11 @@
         project_kernel, "project", send,
         [
             pltpu.VMEM((1, TOK), jnp.int32), pltpu.VMEM(tile, F32), pltpu.VMEM((2, C, 5 * C), BF16),
-            spread, stage, pltpu.SemaphoreType.DMA((6,)), sems,
+            normed, spread, stage, pltpu.SemaphoreType.DMA((6,)), sems,
         ],
         place, pair_mask, pair0, trunk_in, smem=1, far=(1, 2, 3), far_out=(0,),
     )
-    gathered = exchange(operands)
+    gathered = exchange(operands.reshape(64, 64, 128)).reshape(8, 8, 2, 32, 128)
 
     start, gate2, *parts = call(
         tokens_kernel, "tokens_in",
@@ -413,26 +452,34 @@
         place, diff_tokens[0], atom_feats[0], atom_token, atom_weight, attn_in,
         smem=1, far_out=range(10), after=(operands,),
     )
+    parts = swap(parts, "col")
     bias_here = call(
         bias_kernel, "bias", shape(HEADS, 16, 128, dtype=BF16), [pltpu.VMEM((HEADS * 16, 128), F32)],
-        prev_pair.reshape(tile), jnp.swapaxes(bias_weight, 0, 1), after=(parts[0],),
+        prev_pair.reshape(tile), jnp.swapaxes(bias_weight, 0, 1), after=tuple(parts[1:EARLY]),
     )
     bias_other = lax.ppermute(bias_here, "grp", [(0, 1), (1, 0)])
 
-    summed0 = product(gathered, True, bias_other)
-    parts = swap(parts, "col")
-    pair0, gate0 = call(
-        gate_kernel, "gate", [turned_tile, turned_tile], [], pair0, trunk_in, after=tuple(parts[1:]),
-        limit=MIDDLE,
-    )
+    right = call(
+        take_right_kernel, "take_right", shape(8, 8, 2, 16, 128, dtype=BF16), [],
+        gathered, bias_other, limit=NARROW,
+    )
+    summed0 = call(
+        outgoing_kernel, "outgoing", shape(8, 8, 64, 128, dtype=BF16),
+        [half, pltpu.VMEM((2, 8, 2, 2, 16, TOK), BF16)],
+        place, gathered, from_other_core(right), bias_other,
+        smem=1, flops=2 * TOK**3, limit=NARROW,
+    )
+    summed0 = exchange(summed0.reshape(64, 64, 128))
+    token = call(fence_kernel, "fence", token_shape, [], after=tuple(parts[EARLY:]))
+    pair0 = call(turn_kernel, "turn", turned_tile, [], pair0, after=(token,), limit=NARROW)
 
     pair1, operands = call(
-        finish_project_kernel, "finish_project", (turned_tile, send), [received, spread, stage, sems],
-        place, pair_mask, summed0, pair0, gate0, trunk_out, trunk_in,
-        smem=1, far_out=(1,), limit=NARROW,
-    )
-    gathered = exchange(operands)
-    bias_far = lax.ppermute(summed0[:, 16:, :], "core", [(0, 1), (1, 0)])
+        finish_project_kernel, "finish_project", (turned_tile, send), [received, normed, spread, stage, sems],
+        place, pair_mask, summed0, pair0, trunk_out, trunk_in,
+        smem=1, far_out=(1,), limit=FINISH,
+    )
+    gathered = exchange(operands.reshape(64, 64, 128)).reshape(8, 8, 2, 32, 128)
+    bias_far = from_other_core(summed0[:, 32:, :])
     mixed = call(
         attention_kernel, "attention", [shape(PAIR, 128, dtype=BF16)] * 8,
         [
@@ -444,12 +491,17 @@
             pltpu.VMEM((8, PAIR, 128), BF16),
             pltpu.SemaphoreType.DMA((8,)),
         ],
-        place, diff_mask, summed0.reshape(2, 8, 8, 32, 128), bias_far.reshape(2, 8, 8, 16, 128), *parts,
+        place, diff_mask, summed0.reshape(8, 8, 64, 128), bias_far.reshape(8, 8, 32, 128), *parts,
         smem=1, far=range(4, 12), far_out=range(8),
     )
     mixed = swap(mixed, "col")
-    token = call(fence_kernel, "fence", token_shape, [], after=tuple(mixed[1:]))
-    summed1 = product(gathered, False, token)
+    token = call(fence_kernel, "fence", token_shape, [], after=tuple(mixed[1:LATE]))
+    own, far = call(
+        incoming_kernel, "incoming", [sums, sums], [half, half],
+        place, gathered, token, smem=1, flops=2 * TOK**3, limit=NARROW,
+    )
+    summed1 = call(add_kernel, "add", sums, [], own, from_other_core(far), limit=NARROW)
+    summed1 = exchange(summed1.reshape(64, 32, 128))
     tokens_done = call(
         tokens_out_kernel, "tokens_out", shape(2, 64, WIDTH),
         [

time: 180 us -> 167 us (0.928)
  waiting for transfers between devices: 64.3 us -> 46.5 us
  starting transfers between devices: 66.2 us -> 74.3 us
  local copies, waits for them, and re-layouts: 14.3 us -> 9.61 us
    all_to_all x4, waiting for transfers between devices: 44.6 us -> 11.1 us  [exchange(): return lax.all_to_all(value, ALL, 0, 0, tiled=True)]
    ppermute x14, waiting for transfers between devices: 14.4 us -> 26.7 us  [swap(): lax.ppermute(values[slot], axis, [(at, at ^ slot) for at in range(8)])]
    ppermute x1 -> x3, starting transfers between devices: 0.66 us -> 10.3 us  [from_other_core(): return lax.ppermute(value, 'core', [(0, 1), (1, 0)])]
    unnamed x72 -> x64, local copies, waits for them, and re-layouts: 13.6 us -> 8.89 us
    ppermute x1 -> x3, waiting for transfers between devices: 1.54 us -> 4.61 us  [from_other_core(): return lax.ppermute(value, 'core', [(0, 1), (1, 0)])]
    pallas_call x12 -> x15, Pallas kernels: 33.7 us -> 34.6 us  [call(): pl.pallas_call(kernel, name=name, out_shape=out_shape, in_specs=[scalar i...]
  transfers between devices with their start and end apart: 20 -> 22, of which waited for: 12 -> 19; matrix products, arithmetic and copies ran while one was open for 0% -> 0% of each run, Pallas kernels for 11% -> 12%
where the time goes in v4:
time: 167 us; the launch traced here: 166 us
  starting transfers between devices  74.3 us (44%)
  waiting for transfers between devices  46.5 us (28%)
  Pallas kernels  34.6 us (21%)
  local copies, waits for them, and re-layouts  9.61 us (6%)
    all_to_all x4, starting transfers between devices, exchange(): return lax.all_to_all(value, ALL, 0, 0, tiled=True)  38 us
    pallas_call x15, Pallas kernels, call(): pl.pallas_call(kernel, name=name, out_shape=out_shape, in_specs=[scalar i...  34.6 us
    ppermute x14, waiting for transfers between devices, swap(): lax.ppermute(values[slot], axis, [(at, at ^ slot) for at in range(8)])  26.7 us
    ppermute x14, starting transfers between devices, swap(): lax.ppermute(values[slot], axis, [(at, at ^ slot) for at in range(8)])  25.6 us
    all_to_all x4, waiting for transfers between devices, exchange(): return lax.all_to_all(value, ALL, 0, 0, tiled=True)  11.1 us
    ppermute x3, starting transfers between devices, from_other_core(): return lax.ppermute(value, 'core', [(0, 1), (1, 0)])  10.3 us
    unnamed x64, local copies, waits for them, and re-layouts  8.89 us
    ppermute x3, waiting for transfers between devices, from_other_core(): return lax.ppermute(value, 'core', [(0, 1), (1, 0)])  4.61 us
  transfers between devices with their start and end apart: 22, of which 19 were waited for; matrix products, arithmetic and copies ran while one was open for 0% of the time, Pallas kernels for 12%

profile of v4, /device:TPU:1, one launch (start us, length us, event | category | flops | bytes accessed | tf_op | source)
XLA Modules:
  0.0 166.1 jit_solution(14404722196458241843)
XLA Ops:
  0.6 0.7 stack.23.place_ref
  1.3 4.1 %project.1.refs_0_ = bf16[128,32,128]{2,1,0:T(8,128)(2,1)} custom-call(s32[5]{0:T(128)} %stack.23.place_ref, s32[1,512]{1,0:T(1,128)} %mask_ref.2, f32[2,16,64,128]{3,2,1,0:T(8,128)} %bitcast.23, bf16[2,128,640]{2,1,0:T(8,128)(2,1)} %weight_ref.3), custom_call_target="tpu_custom_call" | custom-call | flops 100000000 | bytes 2426900 | tf_op jit(solution)/shard_map/project/pallas_call | solution.py:377
  5.4 15.1 %all-to-all-start = ((bf16[64,64,128]{2,1,0:T(8,128)(2,1)}), bf16[64,64,128]{2,1,0:T(8,128)(2,1)S(1)}, u32[]{:S(2)}, u32[]{:S(2)}) async-start(bf16[64,64,128]{2,1,0:T(8,128)(2,1)} %bitcast.28), calls=%async_computation | async-start | bytes 2097152 | tf_op jit(solution)/shard_map/all_to_all | solution.py:406
  20.6 5.1 %tokens_in.1 = (f32[128,768]{1,0:T(8,128)}, f32[128,768]{1,0:T(8,128)}, bf16[288,128]{1,0:T(8,128)(2,1)}, bf16[288,128]{1,0:T(8,128)(2,1)}, bf16[288,128]{1,0:T(...) custom-call(s32[5]{0:T(128)} %stack.23.place_ref, ...), custom_call_target="tpu_custom_call" | custom-call | flops 100000000 | bytes 6816788 | tf_op jit(solution)/shard_map/tokens_in/pallas_call | solution.py:377
  25.7 1.1 collective-permute-start
  26.8 2.4 %collective-permute-start.1 = (bf16[288,128]{1,0:T(8,128)(2,1)}, bf16[288,128]{1,0:T(8,128)(2,1)S(1)}, u32[]{:S(2)}, u32[]{:S(2)}) collective-permute-start(bf16[288,128]{1,0:T(8,128)(2,1)} %get-tuple-element.27), channel_id=1, source_target_pairs={{0,2},{1,3},{2,0},{3,1},{4,6},{5,7},{6,4},{7,5},{8,10},{9,11},{10,... | collective-permute-start | bytes 221192 | tf_op jit(solution)/shard_map/ppermute | solution.py:411
  29.2 0.5 collective-permute-start.2
  29.7 1.3 collective-permute-done.refs_0_.refs_1_
  30.9 2.6 %collective-permute-done.1.refs_1_.refs_2_ = bf16[288,128]{1,0:T(8,128)(2,1)S(1)} collective-permute-done((bf16[288,128]{1,0:T(8,128)(2,1)}, bf16[288,128]{1,0:T(8,128)(2,1)S(1)}, u32[]{:S(2)}, u32[]{:S(2)}) %collective-permute-start.1) | collective-permute-done | bytes 73760 | tf_op jit(solution)/shard_map/ppermute | solution.py:411
  33.6 3.2 %collective-permute-done.2.refs_2_.refs_3_ = bf16[288,128]{1,0:T(8,128)(2,1)S(1)} collective-permute-done((bf16[288,128]{1,0:T(8,128)(2,1)}, bf16[288,128]{1,0:T(8,128)(2,1)S(1)}, u32[]{:S(2)}, u32[]{:S(2)}) %collective-permute-start.2) | collective-permute-done | bytes 73760 | tf_op jit(solution)/shard_map/ppermute | solution.py:411
  36.8 0.6 copy-done.16
  37.4 3.4 %bias.1 = bf16[16,16,128]{2,1,0:T(8,128)(2,1)} custom-call(f32[2,16,64,128]{3,2,1,0:T(8,128)} %bitcast.30, bf16[16,128]{1,0:T(8,128)(2,1)} %bitcast.34, bf16[288,128]{1,0:T(8,128)(2,1)} %copy-done.14, bf16[288,128]{1,0:T(8,128)(2,1)} %copy-done.15, bf16[288,128]{1,0:T(8,128)(2,1)} %copy-done.16), custom_call_target="tpu_custom_call" | custom-call | flops 100000000 | bytes 1118208 | tf_op jit(solution)/shard_map/bias/pallas_call | solution.py:377
  40.8 0.4 collective-permute-start.3
  41.2 4.1 %collective-permute-done.3.bias_ref = bf16[16,16,128]{2,1,0:T(8,128)(2,1)S(1)} collective-permute-done((bf16[16,16,128]{2,1,0:T(8,128)(2,1)}, bf16[16,16,128]{2,1,0:T(8,128)(2,1)S(1)}, u32[]{:S(2)}, u32[]{:S(2)}) %collective-permute-start.3) | collective-permute-done | bytes 65568 | tf_op jit(solution)/shard_map/ppermute | solution.py:460
  45.3 1.5 all-to-all-done
  46.8 4.0 %collective-permute-start.4 = (bf16[8,8,2,16,128]{4,3,2,1,0:T(8,128)(2,1)S(1)}, bf16[8,8,2,16,128]{4,3,2,1,0:T(8,128)(2,1)S(1)}, u32[]{:S(2)}, u32[]{:S(2)}) collective-permute-start(bf16[8,8,2,16,128]{4,3,2,1,0:T(8,128)(2,1)S(1)} %take_right.1), channel_id=1, source_target_pairs={{0,8},{8,0},{1,9},{9,1},{2,10},{10,2},{3,11},{11,3},{4,12},{12,4},... | collective-permute-start | bytes 1572872 | tf_op jit(solution)/shard_map/ppermute | solution.py:402
  50.9 1.5 collective-permute-done.4.far_ref
  52.4 2.9 %outgoing.1 = bf16[8,8,64,128]{3,2,1,0:T(8,128)(2,1)} custom-call(s32[5]{0:T(128)S(1)} %copy-done.8, bf16[8,8,2,32,128]{4,3,2,1,0:T(8,128)(2,1)S(1)} %bitcast.22, bf16[8,8,2,16,128]{4,3,2,1,0:T(8,128)(2,1)S(1)} %collective-permute-done.4.far_ref, bf16[16,16,128]{2,1,0:T(8,128)(2,1)S(1)} %collective-permute-done.3.bias_ref), custom_call_target="tpu_custom_call" | custom-call | flops 268435456 | bytes 2686996 | tf_op jit(solution)/shard_map/outgoing/pallas_call | solution.py:377
  55.3 7.2 %all-to-all-start.1 = ((bf16[64,64,128]{2,1,0:T(8,128)(2,1)}), bf16[64,64,128]{2,1,0:T(8,128)(2,1)S(1)}, u32[]{:S(2)}, u32[]{:S(2)}) async-start(bf16[64,64,128]{2,1,0:T(8,128)(2,1)} %bitcast.12), calls=%async_computation.1 | async-start | bytes 2097152 | tf_op jit(solution)/shard_map/all_to_all | solution.py:406
  62.5 2.6 %collective-permute-start.5 = (bf16[288,128]{1,0:T(8,128)(2,1)S(1)}, bf16[288,128]{1,0:T(8,128)(2,1)S(1)}, u32[]{:S(2)}, u32[]{:S(2)}) collective-permute-start(bf16[288,128]{1,0:T(8,128)(2,1)S(1)} %copy-done.31), channel_id=1, source_target_pairs={{0,4},{1,5},{2,6},{3,7},{4,0},{5,1},{6,2},{7,3},{8,12},{9,13},{10,... | collective-permute-start | bytes 221192 | tf_op jit(solution)/shard_map/ppermute | solution.py:411
  65.1 1.2 collective-permute-start.6
  66.3 4.8 %collective-permute-start.7 = (bf16[288,128]{1,0:T(8,128)(2,1)S(1)}, bf16[288,128]{1,0:T(8,128)(2,1)S(1)}, u32[]{:S(2)}, u32[]{:S(2)}) collective-permute-start(bf16[288,128]{1,0:T(8,128)(2,1)S(1)} %copy-done.29), channel_id=1, source_target_pairs={{0,6},{1,7},{2,4},{3,5},{4,2},{5,3},{6,0},{7,1},{8,14},{9,15},{10,... | collective-permute-start | bytes 221192 | tf_op jit(solution)/shard_map/ppermute | solution.py:411
  71.1 0.5 collective-permute-start.8
  71.6 4.9 %collective-permute-done.7.refs_2_.refs_6_ = bf16[288,128]{1,0:T(8,128)(2,1)S(1)} collective-permute-done((bf16[288,128]{1,0:T(8,128)(2,1)S(1)}, bf16[288,128]{1,0:T(8,128)(2,1)S(1)}, u32[]{:S(2)}, u32[]{:S(2)}) %collective-permute-start.7) | collective-permute-done | bytes 73760 | tf_op jit(solution)/shard_map/ppermute | solution.py:411
  76.5 3.1 %collective-permute-done.8.refs_3_.refs_7_ = bf16[288,128]{1,0:T(8,128)(2,1)S(1)} collective-permute-done((bf16[288,128]{1,0:T(8,128)(2,1)S(1)}, bf16[288,128]{1,0:T(8,128)(2,1)S(1)}, u32[]{:S(2)}, u32[]{:S(2)}) %collective-permute-start.8) | collective-permute-done | bytes 73760 | tf_op jit(solution)/shard_map/ppermute | solution.py:411
  79.6 0.6 copy-done.20
  80.3 0.6 fence.2.refs_0_
  80.9 0.7 copy-done.12
  81.5 0.3 turn.1.pair_ref
  81.9 7.2 %all-to-all-done.1.recv_ref = bf16[64,64,128]{2,1,0:T(8,128)(2,1)S(1)} async-done(((bf16[64,64,128]{2,1,0:T(8,128)(2,1)}), bf16[64,64,128]{2,1,0:T(8,128)(2,1)S(1)}, u32[]{:S(2)}, u32[]{:S(2)}) %all-to-all-start.1) | async-done | bytes 1048608 | tf_op jit(solution)/shard_map/all_to_all | solution.py:406
  89.1 3.1 %finish_project.1 = (f32[16,128,128]{2,1,0:T(8,128)S(1)}, bf16[128,32,128]{2,1,0:T(8,128)(2,1)S(1)}) custom-call(s32[5]{0:T(128)S(1)} %copy-done.8, s32[1,512]{1,0:T(1,128)S(1)} %copy-done.10, bf16[64,64,128]{2,1,0:T(8,128)(2,1)S(1)} %all-to-all-done.1.recv_ref, f32[16,128,128]{2,1,0:T(8,128)S(1)} %turn.1.pair_ref, bf16[2,128,128]{2,1,0:T(8,128)(2,1)S(1)} %copy-done.7, ...), custom_call_target="tpu_custom_call" | custom-call | flops 100000000 | bytes 4589588 | tf_op jit(solution)/shard_map/finish_project/pallas_call | solution.py:377
  92.2 1.0 copy-done.4
  93.2 1.0 copy-done.6
  94.2 8.9 %all-to-all-start.2 = ((bf16[64,64,128]{2,1,0:T(8,128)(2,1)}), bf16[64,64,128]{2,1,0:T(8,128)(2,1)S(1)}, u32[]{:S(2)}, u32[]{:S(2)}) async-start(bf16[64,64,128]{2,1,0:T(8,128)(2,1)} %bitcast.27), calls=%async_computation.2 | async-start | bytes 2097152 | tf_op jit(solution)/shard_map/all_to_all | solution.py:406
  103.2 1.8 %collective-permute-start.9 = (bf16[64,32,128]{2,1,0:T(8,128)(2,1)S(1)}, bf16[64,32,128]{2,1,0:T(8,128)(2,1)S(1)}, u32[]{:S(2)}, u32[]{:S(2)}) collective-permute-start(bf16[64,32,128]{2,1,0:T(8,128)(2,1)S(1)} %slice.4), channel_id=1, source_target_pairs={{0,8},{8,0},{1,9},{9,1},{2,10},{10,2},{3,11},{11,3},{4,12},{12,4},... | collective-permute-start | bytes 1572872 | tf_op jit(solution)/shard_map/ppermute | solution.py:402
  104.9 1.5 collective-permute-done.9
  106.5 0.8 copy-done.13
  107.3 5.7 %attention.1 = (bf16[96,128]{1,0:T(8,128)(2,1)}, bf16[96,128]{1,0:T(8,128)(2,1)}, bf16[96,128]{1,0:T(8,128)(2,1)}, bf16[96,128]{1,0:T(8,128)(2,1)}, bf16[96,128]...) custom-call(s32[5]{0:T(128)} %stack.23.place_ref, ...), custom_call_target="tpu_custom_call" | custom-call | flops 100000000 | bytes 2361364 | tf_op jit(solution)/shard_map/attention/pallas_call | solution.py:377
  113.0 1.4 collective-permute-start.10
  114.4 2.4 %collective-permute-start.11 = (bf16[96,128]{1,0:T(8,128)(2,1)}, bf16[96,128]{1,0:T(8,128)(2,1)S(1)}, u32[]{:S(2)}, u32[]{:S(2)}) collective-permute-start(bf16[96,128]{1,0:T(8,128)(2,1)} %get-tuple-element.36), channel_id=1, source_target_pairs={{0,2},{1,3},{2,0},{3,1},{4,6},{5,7},{6,4},{7,5},{8,10},{9,11},{10,... | collective-permute-start | bytes 73736 | tf_op jit(solution)/shard_map/ppermute | solution.py:411
  117.0 2.8 %collective-permute-start.13 = (bf16[96,128]{1,0:T(8,128)(2,1)}, bf16[96,128]{1,0:T(8,128)(2,1)S(1)}, u32[]{:S(2)}, u32[]{:S(2)}) collective-permute-start(bf16[96,128]{1,0:T(8,128)(2,1)} %get-tuple-element.38), channel_id=1, source_target_pairs={{0,4},{1,5},{2,6},{3,7},{4,0},{5,1},{6,2},{7,3},{8,12},{9,13},{10,... | collective-permute-start | bytes 73736 | tf_op jit(solution)/shard_map/ppermute | solution.py:411
  119.8 0.3 collective-permute-done.11.refs_1_.refs_2_
  120.1 1.1 collective-permute-done.12.refs_2_.refs_3_
  121.2 1.7 %collective-permute-done.13.refs_3_.refs_4_ = bf16[96,128]{1,0:T(8,128)(2,1)S(1)} collective-permute-done((bf16[96,128]{1,0:T(8,128)(2,1)}, bf16[96,128]{1,0:T(8,128)(2,1)S(1)}, u32[]{:S(2)}, u32[]{:S(2)}) %collective-permute-start.13) | collective-permute-done | bytes 24608 | tf_op jit(solution)/shard_map/ppermute | solution.py:411
  122.9 2.5 %collective-permute-done.14.refs_4_.refs_5_ = bf16[96,128]{1,0:T(8,128)(2,1)S(1)} collective-permute-done((bf16[96,128]{1,0:T(8,128)(2,1)}, bf16[96,128]{1,0:T(8,128)(2,1)S(1)}, u32[]{:S(2)}, u32[]{:S(2)}) %collective-permute-start.14) | collective-permute-done | bytes 24608 | tf_op jit(solution)/shard_map/ppermute | solution.py:411
  125.4 0.6 copy-done.25
  126.0 0.6 fence.3.token_ref
  126.6 2.4 %all-to-all-done.2 = bf16[64,64,128]{2,1,0:T(8,128)(2,1)S(1)} async-done(((bf16[64,64,128]{2,1,0:T(8,128)(2,1)}), bf16[64,64,128]{2,1,0:T(8,128)(2,1)S(1)}, u32[]{:S(2)}, u32[]{:S(2)}) %all-to-all-start.2) | async-done | bytes 1048608 | tf_op jit(solution)/shard_map/all_to_all | solution.py:406
  129.0 0.7 copy-done.11
  129.7 1.9 %incoming.1 = (bf16[8,8,32,128]{3,2,1,0:T(8,128)(2,1)S(1)}, bf16[8,8,32,128]{3,2,1,0:T(8,128)(2,1)S(1)}) custom-call(s32[5]{0:T(128)S(1)} %copy-done.9, bf16[8,8,2,32,128]{4,3,2,1,0:T(8,128)(2,1)S(1)} %bitcast.25, f32[8,128]{1,0:T(8,128)S(1)} %copy-done.11), custom_call_target="tpu_custom_call" | custom-call | flops 268435456 | bytes 2101268 | tf_op jit(solution)/shard_map/incoming/pallas_call | solution.py:377
  131.6 4.5 %collective-permute-start.15 = (bf16[8,8,32,128]{3,2,1,0:T(8,128)(2,1)S(1)}, bf16[8,8,32,128]{3,2,1,0:T(8,128)(2,1)S(1)}, u32[]{:S(2)}, u32[]{:S(2)}) collective-permute-start(bf16[8,8,32,128]{3,2,1,0:T(8,128)(2,1)S(1)} %get-tuple-element.41), channel_id=1, source_target_pairs={{0,8},{8,0},{1,9},{9,1},{2,10},{10,2},{3,11},{11,3},{4,12},{12,4},... | collective-permute-start | bytes 1572872 | tf_op jit(solution)/shard_map/ppermute | solution.py:402
  136.1 1.5 collective-permute-done.15.far_ref
  137.6 0.9 add.5
  138.5 6.8 %all-to-all-start.3 = ((bf16[64,32,128]{2,1,0:T(8,128)(2,1)}), bf16[64,32,128]{2,1,0:T(8,128)(2,1)S(1)}, u32[]{:S(2)}, u32[]{:S(2)}) async-start(bf16[64,32,128]{2,1,0:T(8,128)(2,1)} %bitcast.17), calls=%async_computation.3 | async-start | bytes 1048576 | tf_op jit(solution)/shard_map/all_to_all | solution.py:406
  145.3 5.0 %collective-permute-start.16 = (bf16[96,128]{1,0:T(8,128)(2,1)}, bf16[96,128]{1,0:T(8,128)(2,1)S(1)}, u32[]{:S(2)}, u32[]{:S(2)}) collective-permute-start(bf16[96,128]{1,0:T(8,128)(2,1)} %get-tuple-element.46), channel_id=1, source_target_pairs={{0,6},{1,7},{2,4},{3,5},{4,2},{5,3},{6,0},{7,1},{8,14},{9,15},{10,... | collective-permute-start | bytes 73736 | tf_op jit(solution)/shard_map/ppermute | solution.py:411
  150.3 0.9 collective-permute-start.17
  151.2 1.3 collective-permute-done.16.refs_6_
  152.5 4.6 %collective-permute-done.17.refs_7_ = bf16[96,128]{1,0:T(8,128)(2,1)S(1)} collective-permute-done((bf16[96,128]{1,0:T(8,128)(2,1)}, bf16[96,128]{1,0:T(8,128)(2,1)S(1)}, u32[]{:S(2)}, u32[]{:S(2)}) %collective-permute-start.17) | collective-permute-done | bytes 24608 | tf_op jit(solution)/shard_map/ppermute | solution.py:411
  157.1 0.6 copy-done.27
  157.7 3.5 %tokens_out.1.refs_0_ = f32[2,64,768]{2,1,0:T(8,128)} custom-call(s32[5]{0:T(128)} %stack.23.place_ref, f32[128,768]{1,0:T(8,128)} %get-tuple-element.43.gate_in, f32[128,768]{1,0:T(8,128)} %get-tuple-element.44.start_in, bf16[768,768]{1,0:T(8,128)(2,1)} %weight_in.3, bf16[96,128]{1,0:T(8,128)(2,1)} %get-tuple-element.45.refs_0_, ...), custom_call_target="tpu_custom_call" | custom-call | flops 100000000 | bytes 2555924 | tf_op jit(solution)/shard_map/tokens_out/pallas_call | solution.py:377
  161.3 1.0 copy-done.3
  162.3 1.2 copy-done.5
  163.5 0.9 gate_back.1
  164.4 1.5 finish.1
  (61 shorter events, 0.5 us)
Async XLA Ops:
  5.4 41.3 %all-to-all-start = ((bf16[64,64,128]{2,1,0:T(8,128)(2,1)}), bf16[64,64,128]{2,1,0:T(8,128)(2,1)S(1)}, u32[]{:S(2)}, u32[]{:S(2)}) async-start(bf16[64,64,128]{2,1,0:T(8,128)(2,1)} %bitcast.28), calls=%async_computation | async-start | bytes 2097152 | tf_op jit(solution)/shard_map/all_to_all | solution.py:406
  20.6 31.8 %copy-start.8 = (s32[5]{0:T(128)S(1)}, s32[5]{0:T(128)}, u32[]{:S(2)}) copy-start(s32[5]{0:T(128)} %stack.23.place_ref) | copy-start | bytes 64
  25.7 36.8 %copy-start.31 = (bf16[288,128]{1,0:T(8,128)(2,1)S(1)}, bf16[288,128]{1,0:T(8,128)(2,1)}, u32[]{:S(2)}) copy-start(bf16[288,128]{1,0:T(8,128)(2,1)} %get-tuple-element.29) | copy-start | bytes 221188
  25.7 39.4 %copy-start.30 = (bf16[288,128]{1,0:T(8,128)(2,1)S(1)}, bf16[288,128]{1,0:T(8,128)(2,1)}, u32[]{:S(2)}) copy-start(bf16[288,128]{1,0:T(8,128)(2,1)} %get-tuple-element.30) | copy-start | bytes 221188
  25.7 40.6 %copy-start.29 = (bf16[288,128]{1,0:T(8,128)(2,1)S(1)}, bf16[288,128]{1,0:T(8,128)(2,1)}, u32[]{:S(2)}) copy-start(bf16[288,128]{1,0:T(8,128)(2,1)} %get-tuple-element.31) | copy-start | bytes 221188
  25.7 45.4 %copy-start.28 = (bf16[288,128]{1,0:T(8,128)(2,1)S(1)}, bf16[288,128]{1,0:T(8,128)(2,1)}, u32[]{:S(2)}) copy-start(bf16[288,128]{1,0:T(8,128)(2,1)} %get-tuple-element.32) | copy-start | bytes 221188
  25.7 55.2 %copy-start.1 = (f32[1,32,64,128]{3,2,1,0:T(8,128)S(1)}, f32[1,32,64,128]{3,2,1,0:T(8,128)}, u32[]{:S(2)}) copy-start(f32[1,32,64,128]{3,2,1,0:T(8,128)} %param.13) | copy-start | bytes 3145732
  25.7 5.2 %collective-permute-start = (bf16[288,128]{1,0:T(8,128)(2,1)}, bf16[288,128]{1,0:T(8,128)(2,1)S(1)}, u32[]{:S(2)}, u32[]{:S(2)}) collective-permute-start(bf16[288,128]{1,0:T(8,128)(2,1)} %get-tuple-element.26), channel_id=1, source_target_pairs={{0,1},{1,0},{2,3},{3,2},{4,5},{5,4},{6,7},{7,6},{8,9},{9,8},{10,11... | collective-permute-start | bytes 221192 | tf_op jit(solution)/shard_map/ppermute | solution.py:411
  26.8 6.8 %collective-permute-start.1 = (bf16[288,128]{1,0:T(8,128)(2,1)}, bf16[288,128]{1,0:T(8,128)(2,1)S(1)}, u32[]{:S(2)}, u32[]{:S(2)}) collective-permute-start(bf16[288,128]{1,0:T(8,128)(2,1)} %get-tuple-element.27), channel_id=1, source_target_pairs={{0,2},{1,3},{2,0},{3,1},{4,6},{5,7},{6,4},{7,5},{8,10},{9,11},{10,... | collective-permute-start | bytes 221192 | tf_op jit(solution)/shard_map/ppermute | solution.py:411
  29.2 7.6 %collective-permute-start.2 = (bf16[288,128]{1,0:T(8,128)(2,1)}, bf16[288,128]{1,0:T(8,128)(2,1)S(1)}, u32[]{:S(2)}, u32[]{:S(2)}) collective-permute-start(bf16[288,128]{1,0:T(8,128)(2,1)} %get-tuple-element.28), channel_id=1, source_target_pairs={{0,3},{1,2},{2,1},{3,0},{4,7},{5,6},{6,5},{7,4},{8,11},{9,10},{10,... | collective-permute-start | bytes 221192 | tf_op jit(solution)/shard_map/ppermute | solution.py:411
  30.9 5.8 %copy-start.14 = (bf16[288,128]{1,0:T(8,128)(2,1)}, bf16[288,128]{1,0:T(8,128)(2,1)S(1)}, u32[]{:S(2)}) copy-start(bf16[288,128]{1,0:T(8,128)(2,1)S(1)} %collective-permute-done.refs_0_.refs_1_) | copy-start | bytes 221188
  33.6 3.2 %copy-start.15 = (bf16[288,128]{1,0:T(8,128)(2,1)}, bf16[288,128]{1,0:T(8,128)(2,1)S(1)}, u32[]{:S(2)}) copy-start(bf16[288,128]{1,0:T(8,128)(2,1)S(1)} %collective-permute-done.1.refs_1_.refs_2_) | copy-start | bytes 221188
  36.8 0.6 copy-start.16
  40.8 48.2 %copy-start.2 = (bf16[2,128,640]{2,1,0:T(8,128)(2,1)S(1)}, bf16[2,128,640]{2,1,0:T(8,128)(2,1)}, u32[]{:S(2)}) copy-start(bf16[2,128,640]{2,1,0:T(8,128)(2,1)} %weight_ref.3) | copy-start | bytes 983044
  40.8 48.2 %copy-start.7 = (bf16[2,128,128]{2,1,0:T(8,128)(2,1)S(1)}, bf16[2,128,128]{2,1,0:T(8,128)(2,1)}, u32[]{:S(2)}) copy-start(bf16[2,128,128]{2,1,0:T(8,128)(2,1)} %out_weight_ref.3) | copy-start | bytes 196612
  40.8 48.2 %copy-start.10 = (s32[1,512]{1,0:T(1,128)S(1)}, s32[1,512]{1,0:T(1,128)}, u32[]{:S(2)}) copy-start(s32[1,512]{1,0:T(1,128)} %mask_ref.2) | copy-start | bytes 6148
  40.8 4.5 %collective-permute-start.3 = (bf16[16,16,128]{2,1,0:T(8,128)(2,1)}, bf16[16,16,128]{2,1,0:T(8,128)(2,1)S(1)}, u32[]{:S(2)}, u32[]{:S(2)}) collective-permute-start(bf16[16,16,128]{2,1,0:T(8,128)(2,1)} %bias.1), channel_id=1, source_target_pairs={{0,128},{128,0},{1,129},{129,1},{2,130},{130,2},{3,131},{131,3},{4... | collective-permute-start | bytes 196616 | tf_op jit(solution)/shard_map/ppermute | solution.py:460
  46.8 5.6 %collective-permute-start.4 = (bf16[8,8,2,16,128]{4,3,2,1,0:T(8,128)(2,1)S(1)}, bf16[8,8,2,16,128]{4,3,2,1,0:T(8,128)(2,1)S(1)}, u32[]{:S(2)}, u32[]{:S(2)}) collective-permute-start(bf16[8,8,2,16,128]{4,3,2,1,0:T(8,128)(2,1)S(1)} %take_right.1), channel_id=1, source_target_pairs={{0,8},{8,0},{1,9},{9,1},{2,10},{10,2},{3,11},{11,3},{4,12},{12,4},... | collective-permute-start | bytes 1572872 | tf_op jit(solution)/shard_map/ppermute | solution.py:402
  55.3 33.8 %all-to-all-start.1 = ((bf16[64,64,128]{2,1,0:T(8,128)(2,1)}), bf16[64,64,128]{2,1,0:T(8,128)(2,1)S(1)}, u32[]{:S(2)}, u32[]{:S(2)}) async-start(bf16[64,64,128]{2,1,0:T(8,128)(2,1)} %bitcast.12), calls=%async_computation.1 | async-start | bytes 2097152 | tf_op jit(solution)/shard_map/all_to_all | solution.py:406
  62.5 9.0 %collective-permute-start.5 = (bf16[288,128]{1,0:T(8,128)(2,1)S(1)}, bf16[288,128]{1,0:T(8,128)(2,1)S(1)}, u32[]{:S(2)}, u32[]{:S(2)}) collective-permute-start(bf16[288,128]{1,0:T(8,128)(2,1)S(1)} %copy-done.31), channel_id=1, source_target_pairs={{0,4},{1,5},{2,6},{3,7},{4,0},{5,1},{6,2},{7,3},{8,12},{9,13},{10,... | collective-permute-start | bytes 221192 | tf_op jit(solution)/shard_map/ppermute | solution.py:411
  65.1 6.5 %collective-permute-start.6 = (bf16[288,128]{1,0:T(8,128)(2,1)S(1)}, bf16[288,128]{1,0:T(8,128)(2,1)S(1)}, u32[]{:S(2)}, u32[]{:S(2)}) collective-permute-start(bf16[288,128]{1,0:T(8,128)(2,1)S(1)} %copy-done.30), channel_id=1, source_target_pairs={{0,5},{1,4},{2,7},{3,6},{4,1},{5,0},{6,3},{7,2},{8,13},{9,12},{10,... | collective-permute-start | bytes 221192 | tf_op jit(solution)/shard_map/ppermute | solution.py:411
  66.3 10.2 %collective-permute-start.7 = (bf16[288,128]{1,0:T(8,128)(2,1)S(1)}, bf16[288,128]{1,0:T(8,128)(2,1)S(1)}, u32[]{:S(2)}, u32[]{:S(2)}) collective-permute-start(bf16[288,128]{1,0:T(8,128)(2,1)S(1)} %copy-done.29), channel_id=1, source_target_pairs={{0,6},{1,7},{2,4},{3,5},{4,2},{5,3},{6,0},{7,1},{8,14},{9,15},{10,... | collective-permute-start | bytes 221192 | tf_op jit(solution)/shard_map/ppermute | solution.py:411
  71.1 8.6 %collective-permute-start.8 = (bf16[288,128]{1,0:T(8,128)(2,1)S(1)}, bf16[288,128]{1,0:T(8,128)(2,1)S(1)}, u32[]{:S(2)}, u32[]{:S(2)}) collective-permute-start(bf16[288,128]{1,0:T(8,128)(2,1)S(1)} %copy-done.28), channel_id=1, source_target_pairs={{0,7},{1,6},{2,5},{3,4},{4,3},{5,2},{6,1},{7,0},{8,15},{9,14},{10,... | collective-permute-start | bytes 221192 | tf_op jit(solution)/shard_map/ppermute | solution.py:411
  71.5 8.1 %copy-start.17 = (bf16[288,128]{1,0:T(8,128)(2,1)}, bf16[288,128]{1,0:T(8,128)(2,1)S(1)}, u32[]{:S(2)}) copy-start(bf16[288,128]{1,0:T(8,128)(2,1)S(1)} %collective-permute-done.5.refs_0_.refs_4_) | copy-start | bytes 221188
  71.6 8.0 %copy-start.18 = (bf16[288,128]{1,0:T(8,128)(2,1)}, bf16[288,128]{1,0:T(8,128)(2,1)S(1)}, u32[]{:S(2)}) copy-start(bf16[288,128]{1,0:T(8,128)(2,1)S(1)} %collective-permute-done.6.refs_1_.refs_5_) | copy-start | bytes 221188
  76.5 3.1 %copy-start.19 = (bf16[288,128]{1,0:T(8,128)(2,1)}, bf16[288,128]{1,0:T(8,128)(2,1)S(1)}, u32[]{:S(2)}) copy-start(bf16[288,128]{1,0:T(8,128)(2,1)S(1)} %collective-permute-done.7.refs_2_.refs_6_) | copy-start | bytes 221188
  79.6 0.6 copy-start.20
  80.9 0.7 copy-start.12
  81.5 47.5 %copy-start.9 = (s32[5]{0:T(128)S(1)}, s32[5]{0:T(128)}, u32[]{:S(2)}) copy-start(s32[5]{0:T(128)} %stack.23.place_ref) | copy-start | bytes 64
  89.1 17.4 %copy-start = (bf16[64,64,128]{2,1,0:T(8,128)(2,1)}, bf16[64,64,128]{2,1,0:T(8,128)(2,1)S(1)}, u32[]{:S(2)}) copy-start(bf16[64,64,128]{2,1,0:T(8,128)(2,1)S(1)} %all-to-all-done.1.recv_ref) | copy-start | bytes 3145732
  92.2 1.0 copy-start.4
  93.2 1.0 copy-start.6
  94.2 34.8 %all-to-all-start.2 = ((bf16[64,64,128]{2,1,0:T(8,128)(2,1)}), bf16[64,64,128]{2,1,0:T(8,128)(2,1)S(1)}, u32[]{:S(2)}, u32[]{:S(2)}) async-start(bf16[64,64,128]{2,1,0:T(8,128)(2,1)} %bitcast.27), calls=%async_computation.2 | async-start | bytes 2097152 | tf_op jit(solution)/shard_map/all_to_all | solution.py:406
  103.2 3.3 %collective-permute-start.9 = (bf16[64,32,128]{2,1,0:T(8,128)(2,1)S(1)}, bf16[64,32,128]{2,1,0:T(8,128)(2,1)S(1)}, u32[]{:S(2)}, u32[]{:S(2)}) collective-permute-start(bf16[64,32,128]{2,1,0:T(8,128)(2,1)S(1)} %slice.4), channel_id=1, source_target_pairs={{0,8},{8,0},{1,9},{9,1},{2,10},{10,2},{3,11},{11,3},{4,12},{12,4},... | collective-permute-start | bytes 1572872 | tf_op jit(solution)/shard_map/ppermute | solution.py:402
  106.5 0.8 copy-start.13
  113.0 6.8 %collective-permute-start.10 = (bf16[96,128]{1,0:T(8,128)(2,1)}, bf16[96,128]{1,0:T(8,128)(2,1)S(1)}, u32[]{:S(2)}, u32[]{:S(2)}) collective-permute-start(bf16[96,128]{1,0:T(8,128)(2,1)} %get-tuple-element.35), channel_id=1, source_target_pairs={{0,1},{1,0},{2,3},{3,2},{4,5},{5,4},{6,7},{7,6},{8,9},{9,8},{10,11... | collective-permute-start | bytes 73736 | tf_op jit(solution)/shard_map/ppermute | solution.py:411
  114.4 5.7 %collective-permute-start.11 = (bf16[96,128]{1,0:T(8,128)(2,1)}, bf16[96,128]{1,0:T(8,128)(2,1)S(1)}, u32[]{:S(2)}, u32[]{:S(2)}) collective-permute-start(bf16[96,128]{1,0:T(8,128)(2,1)} %get-tuple-element.36), channel_id=1, source_target_pairs={{0,2},{1,3},{2,0},{3,1},{4,6},{5,7},{6,4},{7,5},{8,10},{9,11},{10,... | collective-permute-start | bytes 73736 | tf_op jit(solution)/shard_map/ppermute | solution.py:411
  116.8 4.4 %collective-permute-start.12 = (bf16[96,128]{1,0:T(8,128)(2,1)}, bf16[96,128]{1,0:T(8,128)(2,1)S(1)}, u32[]{:S(2)}, u32[]{:S(2)}) collective-permute-start(bf16[96,128]{1,0:T(8,128)(2,1)} %get-tuple-element.37), channel_id=1, source_target_pairs={{0,3},{1,2},{2,1},{3,0},{4,7},{5,6},{6,5},{7,4},{8,11},{9,10},{10,... | collective-permute-start | bytes 73736 | tf_op jit(solution)/shard_map/ppermute | solution.py:411
  117.0 5.9 %collective-permute-start.13 = (bf16[96,128]{1,0:T(8,128)(2,1)}, bf16[96,128]{1,0:T(8,128)(2,1)S(1)}, u32[]{:S(2)}, u32[]{:S(2)}) collective-permute-start(bf16[96,128]{1,0:T(8,128)(2,1)} %get-tuple-element.38), channel_id=1, source_target_pairs={{0,4},{1,5},{2,6},{3,7},{4,0},{5,1},{6,2},{7,3},{8,12},{9,13},{10,... | collective-permute-start | bytes 73736 | tf_op jit(solution)/shard_map/ppermute | solution.py:411
  119.8 5.6 %collective-permute-start.14 = (bf16[96,128]{1,0:T(8,128)(2,1)}, bf16[96,128]{1,0:T(8,128)(2,1)S(1)}, u32[]{:S(2)}, u32[]{:S(2)}) collective-permute-start(bf16[96,128]{1,0:T(8,128)(2,1)} %get-tuple-element.39), channel_id=1, source_target_pairs={{0,5},{1,4},{2,7},{3,6},{4,1},{5,0},{6,3},{7,2},{8,13},{9,12},{10,... | collective-permute-start | bytes 73736 | tf_op jit(solution)/shard_map/ppermute | solution.py:411
  119.8 5.6 %copy-start.21 = (bf16[96,128]{1,0:T(8,128)(2,1)}, bf16[96,128]{1,0:T(8,128)(2,1)S(1)}, u32[]{:S(2)}) copy-start(bf16[96,128]{1,0:T(8,128)(2,1)S(1)} %collective-permute-done.10.refs_0_.refs_1_) | copy-start | bytes 73732
  120.1 5.3 %copy-start.22 = (bf16[96,128]{1,0:T(8,128)(2,1)}, bf16[96,128]{1,0:T(8,128)(2,1)S(1)}, u32[]{:S(2)}) copy-start(bf16[96,128]{1,0:T(8,128)(2,1)S(1)} %collective-permute-done.11.refs_1_.refs_2_) | copy-start | bytes 73732
  121.2 4.2 %copy-start.23 = (bf16[96,128]{1,0:T(8,128)(2,1)}, bf16[96,128]{1,0:T(8,128)(2,1)S(1)}, u32[]{:S(2)}) copy-start(bf16[96,128]{1,0:T(8,128)(2,1)S(1)} %collective-permute-done.12.refs_2_.refs_3_) | copy-start | bytes 73732
  122.9 2.5 %copy-start.24 = (bf16[96,128]{1,0:T(8,128)(2,1)}, bf16[96,128]{1,0:T(8,128)(2,1)S(1)}, u32[]{:S(2)}) copy-start(bf16[96,128]{1,0:T(8,128)(2,1)S(1)} %collective-permute-done.13.refs_3_.refs_4_) | copy-start | bytes 73732
  125.4 0.6 copy-start.25
  129.0 0.7 copy-start.11
  131.6 6.0 %collective-permute-start.15 = (bf16[8,8,32,128]{3,2,1,0:T(8,128)(2,1)S(1)}, bf16[8,8,32,128]{3,2,1,0:T(8,128)(2,1)S(1)}, u32[]{:S(2)}, u32[]{:S(2)}) collective-permute-start(bf16[8,8,32,128]{3,2,1,0:T(8,128)(2,1)S(1)} %get-tuple-element.41), channel_id=1, source_target_pairs={{0,8},{8,0},{1,9},{9,1},{2,10},{10,2},{3,11},{11,3},{4,12},{12,4},... | collective-permute-start | bytes 1572872 | tf_op jit(solution)/shard_map/ppermute | solution.py:402
  138.5 25.9 %all-to-all-start.3 = ((bf16[64,32,128]{2,1,0:T(8,128)(2,1)}), bf16[64,32,128]{2,1,0:T(8,128)(2,1)S(1)}, u32[]{:S(2)}, u32[]{:S(2)}) async-start(bf16[64,32,128]{2,1,0:T(8,128)(2,1)} %bitcast.17), calls=%async_computation.3 | async-start | bytes 1048576 | tf_op jit(solution)/shard_map/all_to_all | solution.py:406
  145.3 7.2 %collective-permute-start.16 = (bf16[96,128]{1,0:T(8,128)(2,1)}, bf16[96,128]{1,0:T(8,128)(2,1)S(1)}, u32[]{:S(2)}, u32[]{:S(2)}) collective-permute-start(bf16[96,128]{1,0:T(8,128)(2,1)} %get-tuple-element.46), channel_id=1, source_target_pairs={{0,6},{1,7},{2,4},{3,5},{4,2},{5,3},{6,0},{7,1},{8,14},{9,15},{10,... | collective-permute-start | bytes 73736 | tf_op jit(solution)/shard_map/ppermute | solution.py:411
  150.3 6.8 %collective-permute-start.17 = (bf16[96,128]{1,0:T(8,128)(2,1)}, bf16[96,128]{1,0:T(8,128)(2,1)S(1)}, u32[]{:S(2)}, u32[]{:S(2)}) collective-permute-start(bf16[96,128]{1,0:T(8,128)(2,1)} %get-tuple-element.47), channel_id=1, source_target_pairs={{0,7},{1,6},{2,5},{3,4},{4,3},{5,2},{6,1},{7,0},{8,15},{9,14},{10,... | collective-permute-start | bytes 73736 | tf_op jit(solution)/shard_map/ppermute | solution.py:411
  152.5 4.6 %copy-start.26 = (bf16[96,128]{1,0:T(8,128)(2,1)}, bf16[96,128]{1,0:T(8,128)(2,1)S(1)}, u32[]{:S(2)}) copy-start(bf16[96,128]{1,0:T(8,128)(2,1)S(1)} %collective-permute-done.16.refs_6_) | copy-start | bytes 73732
  157.1 0.6 copy-start.27
  161.3 1.0 copy-start.3
  162.3 1.2 copy-start.5

commit v5 on v4

--- a/solution.py
+++ b/solution.py
@@ -395,7 +395,7 @@
 
 
 ALL = ("z", "col")
-EARLY, LATE = 4, 6
+EARLY, LATE = 1, 6
 
 
 def from_other_core(value):
@@ -455,7 +455,7 @@
     parts = swap(parts, "col")
     bias_here = call(
         bias_kernel, "bias", shape(HEADS, 16, 128, dtype=BF16), [pltpu.VMEM((HEADS * 16, 128), F32)],
-        prev_pair.reshape(tile), jnp.swapaxes(bias_weight, 0, 1), after=tuple(parts[1:EARLY]),
+        prev_pair.reshape(tile), jnp.swapaxes(bias_weight, 0, 1), after=(parts[0],),
     )
     bias_other = lax.ppermute(bias_here, "grp", [(0, 1), (1, 0)])
 
@@ -512,7 +512,7 @@
     )
     pair1, gate1 = call(
         gate_back_kernel, "gate_back", [shape(*tile), shape(*tile)], [], pair1, trunk_in,
-        after=(tokens_done,), limit=MIDDLE,
+        limit=MIDDLE,
     )
     pair2 = call(
         finish_kernel, "finish", shape(*tile), [received, pltpu.VMEM(tile, F32), sems],

time: 167 us -> 165 us (0.988)
    ppermute x14, waiting for transfers between devices: 26.7 us -> 17.6 us  [swap(): lax.ppermute(values[slot], axis, [(at, at ^ slot) for at in range(8)])]
    all_to_all x4, waiting for transfers between devices: 11.1 us -> 19.3 us  [exchange(): return lax.all_to_all(value, ALL, 0, 0, tiled=True)]
    unnamed x64 -> x68, local copies, waits for them, and re-layouts: 8.89 us -> 7.31 us
  transfers between devices with their start and end apart: 22 -> 22, of which waited for: 19 -> 16; matrix products, arithmetic and copies ran while one was open for 0% -> 0% of each run, Pallas kernels for 12% -> 12%
where the time goes in v5:
time: 165 us; the launch traced here: 163 us
  starting transfers between devices  74.1 us (45%)
  waiting for transfers between devices  44.9 us (27%)
  Pallas kernels  34.8 us (21%)
  local copies, waits for them, and re-layouts  7.98 us (5%)
    all_to_all x4, starting transfers between devices, exchange(): return lax.all_to_all(value, ALL, 0, 0, tiled=True)  37.6 us
    pallas_call x15, Pallas kernels, call(): pl.pallas_call(kernel, name=name, out_shape=out_shape, in_specs=[scalar i...  34.8 us
    ppermute x14, starting transfers between devices, swap(): lax.ppermute(values[slot], axis, [(at, at ^ slot) for at in range(8)])  25.9 us
    all_to_all x4, waiting for transfers between devices, exchange(): return lax.all_to_all(value, ALL, 0, 0, tiled=True)  19.3 us
    ppermute x14, waiting for transfers between devices, swap(): lax.ppermute(values[slot], axis, [(at, at ^ slot) for at in range(8)])  17.6 us
    ppermute x3, starting transfers between devices, from_other_core(): return lax.ppermute(value, 'core', [(0, 1), (1, 0)])  10.3 us
    unnamed x68, local copies, waits for them, and re-layouts  7.31 us
    ppermute x3, waiting for transfers between devices, from_other_core(): return lax.ppermute(value, 'core', [(0, 1), (1, 0)])  4.61 us
  transfers between devices with their start and end apart: 22, of which 16 were waited for; matrix products, arithmetic and copies ran while one was open for 0% of the time, Pallas kernels for 12%

profile of v5, /device:TPU:1, one launch (start us, length us, event | category | flops | bytes accessed | tf_op | source)
XLA Modules:
  0.0 162.9 jit_solution(61430102378728501)
XLA Ops:
  0.6 0.6 stack.23.place_ref
  1.3 4.1 %project.1.refs_0_ = bf16[128,32,128]{2,1,0:T(8,128)(2,1)} custom-call(s32[5]{0:T(128)} %stack.23.place_ref, s32[1,512]{1,0:T(1,128)} %mask_ref.2, f32[2,16,64,128]{3,2,1,0:T(8,128)} %bitcast.23, bf16[2,128,640]{2,1,0:T(8,128)(2,1)} %weight_ref.3), custom_call_target="tpu_custom_call" | custom-call | flops 100000000 | bytes 2426900 | tf_op jit(solution)/shard_map/project/pallas_call | solution.py:377
  5.4 15.1 %all-to-all-start = ((bf16[64,64,128]{2,1,0:T(8,128)(2,1)}), bf16[64,64,128]{2,1,0:T(8,128)(2,1)S(1)}, u32[]{:S(2)}, u32[]{:S(2)}) async-start(bf16[64,64,128]{2,1,0:T(8,128)(2,1)} %bitcast.27), calls=%async_computation | async-start | bytes 2097152 | tf_op jit(solution)/shard_map/all_to_all | solution.py:406
  20.5 5.1 %tokens_in.1 = (f32[128,768]{1,0:T(8,128)}, f32[128,768]{1,0:T(8,128)}, bf16[288,128]{1,0:T(8,128)(2,1)}, bf16[288,128]{1,0:T(8,128)(2,1)}, bf16[288,128]{1,0:T(...) custom-call(s32[5]{0:T(128)} %stack.23.place_ref, ...), custom_call_target="tpu_custom_call" | custom-call | flops 100000000 | bytes 6816788 | tf_op jit(solution)/shard_map/tokens_in/pallas_call | solution.py:377
  25.7 0.0 copy-start.1
  25.7 3.5 %bias.1 = bf16[16,16,128]{2,1,0:T(8,128)(2,1)} custom-call(f32[2,16,64,128]{3,2,1,0:T(8,128)} %bitcast.29, bf16[16,128]{1,0:T(8,128)(2,1)} %bitcast.34, bf16[288,128]{1,0:T(8,128)(2,1)} %get-tuple-element.26.refs_0_), custom_call_target="tpu_custom_call" | custom-call | flops 100000000 | bytes 1118208 | tf_op jit(solution)/shard_map/bias/pallas_call | solution.py:377
  29.2 0.4 collective-permute-start
  29.6 3.5 %collective-permute-done.bias_ref = bf16[16,16,128]{2,1,0:T(8,128)(2,1)S(1)} collective-permute-done((bf16[16,16,128]{2,1,0:T(8,128)(2,1)}, bf16[16,16,128]{2,1,0:T(8,128)(2,1)S(1)}, u32[]{:S(2)}, u32[]{:S(2)}) %collective-permute-start) | collective-permute-done | bytes 65568 | tf_op jit(solution)/shard_map/ppermute | solution.py:460
  33.1 13.6 %all-to-all-done = bf16[64,64,128]{2,1,0:T(8,128)(2,1)S(1)} async-done(((bf16[64,64,128]{2,1,0:T(8,128)(2,1)}), bf16[64,64,128]{2,1,0:T(8,128)(2,1)S(1)}, u32[]{:S(2)}, u32[]{:S(2)}) %all-to-all-start) | async-done | bytes 1048608 | tf_op jit(solution)/shard_map/all_to_all | solution.py:406
  46.8 4.0 %collective-permute-start.1 = (bf16[8,8,2,16,128]{4,3,2,1,0:T(8,128)(2,1)S(1)}, bf16[8,8,2,16,128]{4,3,2,1,0:T(8,128)(2,1)S(1)}, u32[]{:S(2)}, u32[]{:S(2)}) collective-permute-start(bf16[8,8,2,16,128]{4,3,2,1,0:T(8,128)(2,1)S(1)} %take_right.1), channel_id=1, source_target_pairs={{0,8},{8,0},{1,9},{9,1},{2,10},{10,2},{3,11},{11,3},{4,12},{12,4},... | collective-permute-start | bytes 1572872 | tf_op jit(solution)/shard_map/ppermute | solution.py:402
  50.8 1.5 collective-permute-done.1.far_ref
  52.3 2.9 %outgoing.1 = bf16[8,8,64,128]{3,2,1,0:T(8,128)(2,1)} custom-call(s32[5]{0:T(128)S(1)} %copy-done.7, bf16[8,8,2,32,128]{4,3,2,1,0:T(8,128)(2,1)S(1)} %bitcast.22, bf16[8,8,2,16,128]{4,3,2,1,0:T(8,128)(2,1)S(1)} %collective-permute-done.1.far_ref, bf16[16,16,128]{2,1,0:T(8,128)(2,1)S(1)} %collective-permute-done.bias_ref), custom_call_target="tpu_custom_call" | custom-call | flops 268435456 | bytes 2686996 | tf_op jit(solution)/shard_map/outgoing/pallas_call | solution.py:377
  55.2 6.8 %all-to-all-start.1 = ((bf16[64,64,128]{2,1,0:T(8,128)(2,1)}), bf16[64,64,128]{2,1,0:T(8,128)(2,1)S(1)}, u32[]{:S(2)}, u32[]{:S(2)}) async-start(bf16[64,64,128]{2,1,0:T(8,128)(2,1)} %bitcast.12), calls=%async_computation.1 | async-start | bytes 2097152 | tf_op jit(solution)/shard_map/all_to_all | solution.py:406
  62.0 1.1 collective-permute-start.2
  63.1 2.4 %collective-permute-start.3 = (bf16[288,128]{1,0:T(8,128)(2,1)S(1)}, bf16[288,128]{1,0:T(8,128)(2,1)S(1)}, u32[]{:S(2)}, u32[]{:S(2)}) collective-permute-start(bf16[288,128]{1,0:T(8,128)(2,1)S(1)} %copy-done.32), channel_id=1, source_target_pairs={{0,2},{1,3},{2,0},{3,1},{4,6},{5,7},{6,4},{7,5},{8,10},{9,11},{10,... | collective-permute-start | bytes 221192 | tf_op jit(solution)/shard_map/ppermute | solution.py:411
  65.5 0.5 collective-permute-start.4
  66.0 2.5 %collective-permute-start.5 = (bf16[288,128]{1,0:T(8,128)(2,1)S(1)}, bf16[288,128]{1,0:T(8,128)(2,1)S(1)}, u32[]{:S(2)}, u32[]{:S(2)}) collective-permute-start(bf16[288,128]{1,0:T(8,128)(2,1)S(1)} %copy-done.30), channel_id=1, source_target_pairs={{0,4},{1,5},{2,6},{3,7},{4,0},{5,1},{6,2},{7,3},{8,12},{9,13},{10,... | collective-permute-start | bytes 221192 | tf_op jit(solution)/shard_map/ppermute | solution.py:411
  68.5 6.0 %collective-permute-start.7 = (bf16[288,128]{1,0:T(8,128)(2,1)S(1)}, bf16[288,128]{1,0:T(8,128)(2,1)S(1)}, u32[]{:S(2)}, u32[]{:S(2)}) collective-permute-start(bf16[288,128]{1,0:T(8,128)(2,1)S(1)} %copy-done.28), channel_id=1, source_target_pairs={{0,6},{1,7},{2,4},{3,5},{4,2},{5,3},{6,0},{7,1},{8,14},{9,15},{10,... | collective-permute-start | bytes 221192 | tf_op jit(solution)/shard_map/ppermute | solution.py:411
  74.6 0.7 collective-permute-start.8
  75.3 0.0 collective-permute-done.4.refs_2_.refs_3_
  75.3 0.4 collective-permute-done.6.refs_4_.refs_5_
  75.7 2.8 %collective-permute-done.7.refs_5_.refs_6_ = bf16[288,128]{1,0:T(8,128)(2,1)S(1)} collective-permute-done((bf16[288,128]{1,0:T(8,128)(2,1)S(1)}, bf16[288,128]{1,0:T(8,128)(2,1)S(1)}, u32[]{:S(2)}, u32[]{:S(2)}) %collective-permute-start.7) | collective-permute-done | bytes 73760 | tf_op jit(solution)/shard_map/ppermute | solution.py:411
  78.5 4.9 %collective-permute-done.8.refs_6_.refs_7_ = bf16[288,128]{1,0:T(8,128)(2,1)S(1)} collective-permute-done((bf16[288,128]{1,0:T(8,128)(2,1)S(1)}, bf16[288,128]{1,0:T(8,128)(2,1)S(1)}, u32[]{:S(2)}, u32[]{:S(2)}) %collective-permute-start.8) | collective-permute-done | bytes 73760 | tf_op jit(solution)/shard_map/ppermute | solution.py:411
  83.5 0.6 copy-done.19
  84.1 0.6 fence.2.refs_0_
  84.7 0.7 copy-done.9
  85.4 0.3 turn.1.pair_ref
  85.7 2.9 %all-to-all-done.1.recv_ref = bf16[64,64,128]{2,1,0:T(8,128)(2,1)S(1)} async-done(((bf16[64,64,128]{2,1,0:T(8,128)(2,1)}), bf16[64,64,128]{2,1,0:T(8,128)(2,1)S(1)}, u32[]{:S(2)}, u32[]{:S(2)}) %all-to-all-start.1) | async-done | bytes 1048608 | tf_op jit(solution)/shard_map/all_to_all | solution.py:406
  88.7 3.1 %finish_project.1 = (f32[16,128,128]{2,1,0:T(8,128)S(1)}, bf16[128,32,128]{2,1,0:T(8,128)(2,1)S(1)}) custom-call(s32[5]{0:T(128)S(1)} %copy-done.7, s32[1,512]{1,0:T(1,128)S(1)} %copy-done.10, bf16[64,64,128]{2,1,0:T(8,128)(2,1)S(1)} %all-to-all-done.1.recv_ref, f32[16,128,128]{2,1,0:T(8,128)S(1)} %turn.1.pair_ref, bf16[2,128,128]{2,1,0:T(8,128)(2,1)S(1)} %copy-done.6, ...), custom_call_target="tpu_custom_call" | custom-call | flops 100000000 | bytes 4589588 | tf_op jit(solution)/shard_map/finish_project/pallas_call | solution.py:377
  91.8 1.0 copy-done.3
  92.8 1.0 copy-done.5
  93.8 8.9 %all-to-all-start.2 = ((bf16[64,64,128]{2,1,0:T(8,128)(2,1)}), bf16[64,64,128]{2,1,0:T(8,128)(2,1)S(1)}, u32[]{:S(2)}, u32[]{:S(2)}) async-start(bf16[64,64,128]{2,1,0:T(8,128)(2,1)} %bitcast.26), calls=%async_computation.2 | async-start | bytes 2097152 | tf_op jit(solution)/shard_map/all_to_all | solution.py:406
  102.7 1.8 %collective-permute-start.9 = (bf16[64,32,128]{2,1,0:T(8,128)(2,1)S(1)}, bf16[64,32,128]{2,1,0:T(8,128)(2,1)S(1)}, u32[]{:S(2)}, u32[]{:S(2)}) collective-permute-start(bf16[64,32,128]{2,1,0:T(8,128)(2,1)S(1)} %slice.4), channel_id=1, source_target_pairs={{0,8},{8,0},{1,9},{9,1},{2,10},{10,2},{3,11},{11,3},{4,12},{12,4},... | collective-permute-start | bytes 1572872 | tf_op jit(solution)/shard_map/ppermute | solution.py:402
  104.5 1.5 collective-permute-done.9
  106.1 0.8 copy-done.12
  106.8 5.8 %attention.1 = (bf16[96,128]{1,0:T(8,128)(2,1)}, bf16[96,128]{1,0:T(8,128)(2,1)}, bf16[96,128]{1,0:T(8,128)(2,1)}, bf16[96,128]{1,0:T(8,128)(2,1)}, bf16[96,128]...) custom-call(s32[5]{0:T(128)} %stack.23.place_ref, ...), custom_call_target="tpu_custom_call" | custom-call | flops 100000000 | bytes 2361364 | tf_op jit(solution)/shard_map/attention/pallas_call | solution.py:377
  112.6 1.4 collective-permute-start.10
  114.0 2.4 %collective-permute-start.11 = (bf16[96,128]{1,0:T(8,128)(2,1)}, bf16[96,128]{1,0:T(8,128)(2,1)S(1)}, u32[]{:S(2)}, u32[]{:S(2)}) collective-permute-start(bf16[96,128]{1,0:T(8,128)(2,1)} %get-tuple-element.36), channel_id=1, source_target_pairs={{0,2},{1,3},{2,0},{3,1},{4,6},{5,7},{6,4},{7,5},{8,10},{9,11},{10,... | collective-permute-start | bytes 73736 | tf_op jit(solution)/shard_map/ppermute | solution.py:411
  116.4 0.2 collective-permute-start.12
  116.6 2.8 %collective-permute-start.13 = (bf16[96,128]{1,0:T(8,128)(2,1)}, bf16[96,128]{1,0:T(8,128)(2,1)S(1)}, u32[]{:S(2)}, u32[]{:S(2)}) collective-permute-start(bf16[96,128]{1,0:T(8,128)(2,1)} %get-tuple-element.38), channel_id=1, source_target_pairs={{0,4},{1,5},{2,6},{3,7},{4,0},{5,1},{6,2},{7,3},{8,12},{9,13},{10,... | collective-permute-start | bytes 73736 | tf_op jit(solution)/shard_map/ppermute | solution.py:411
  119.3 0.0 collective-permute-start.14
  119.4 0.0 collective-permute-done.10.refs_0_.refs_1_
  119.4 0.3 collective-permute-done.11.refs_1_.refs_2_
  119.7 1.1 collective-permute-done.12.refs_2_.refs_3_
  120.8 1.7 %collective-permute-done.13.refs_3_.refs_4_ = bf16[96,128]{1,0:T(8,128)(2,1)S(1)} collective-permute-done((bf16[96,128]{1,0:T(8,128)(2,1)}, bf16[96,128]{1,0:T(8,128)(2,1)S(1)}, u32[]{:S(2)}, u32[]{:S(2)}) %collective-permute-start.13) | collective-permute-done | bytes 24608 | tf_op jit(solution)/shard_map/ppermute | solution.py:411
  122.5 2.5 %collective-permute-done.14.refs_4_.refs_5_ = bf16[96,128]{1,0:T(8,128)(2,1)S(1)} collective-permute-done((bf16[96,128]{1,0:T(8,128)(2,1)}, bf16[96,128]{1,0:T(8,128)(2,1)S(1)}, u32[]{:S(2)}, u32[]{:S(2)}) %collective-permute-start.14) | collective-permute-done | bytes 24608 | tf_op jit(solution)/shard_map/ppermute | solution.py:411
  125.0 0.6 copy-done.24
  125.6 0.6 fence.3.token_ref
  126.2 2.3 %all-to-all-done.2 = bf16[64,64,128]{2,1,0:T(8,128)(2,1)S(1)} async-done(((bf16[64,64,128]{2,1,0:T(8,128)(2,1)}), bf16[64,64,128]{2,1,0:T(8,128)(2,1)S(1)}, u32[]{:S(2)}, u32[]{:S(2)}) %all-to-all-start.2) | async-done | bytes 1048608 | tf_op jit(solution)/shard_map/all_to_all | solution.py:406
  128.5 0.7 copy-done.11
  129.2 1.9 %incoming.1 = (bf16[8,8,32,128]{3,2,1,0:T(8,128)(2,1)S(1)}, bf16[8,8,32,128]{3,2,1,0:T(8,128)(2,1)S(1)}) custom-call(s32[5]{0:T(128)S(1)} %copy-done.8, bf16[8,8,2,32,128]{4,3,2,1,0:T(8,128)(2,1)S(1)} %bitcast.25, f32[8,128]{1,0:T(8,128)S(1)} %copy-done.11), custom_call_target="tpu_custom_call" | custom-call | flops 268435456 | bytes 2101268 | tf_op jit(solution)/shard_map/incoming/pallas_call | solution.py:377
  131.1 4.5 %collective-permute-start.15 = (bf16[8,8,32,128]{3,2,1,0:T(8,128)(2,1)S(1)}, bf16[8,8,32,128]{3,2,1,0:T(8,128)(2,1)S(1)}, u32[]{:S(2)}, u32[]{:S(2)}) collective-permute-start(bf16[8,8,32,128]{3,2,1,0:T(8,128)(2,1)S(1)} %get-tuple-element.41), channel_id=1, source_target_pairs={{0,8},{8,0},{1,9},{9,1},{2,10},{10,2},{3,11},{11,3},{4,12},{12,4},... | collective-permute-start | bytes 1572872 | tf_op jit(solution)/shard_map/ppermute | solution.py:402
  135.6 1.5 collective-permute-done.15.far_ref
  137.2 0.9 add.5
  138.1 6.7 %all-to-all-start.3 = ((bf16[64,32,128]{2,1,0:T(8,128)(2,1)}), bf16[64,32,128]{2,1,0:T(8,128)(2,1)S(1)}, u32[]{:S(2)}, u32[]{:S(2)}) async-start(bf16[64,32,128]{2,1,0:T(8,128)(2,1)} %bitcast.17), calls=%async_computation.3 | async-start | bytes 1048576 | tf_op jit(solution)/shard_map/all_to_all | solution.py:406
  144.8 5.0 %collective-permute-start.16 = (bf16[96,128]{1,0:T(8,128)(2,1)}, bf16[96,128]{1,0:T(8,128)(2,1)S(1)}, u32[]{:S(2)}, u32[]{:S(2)}) collective-permute-start(bf16[96,128]{1,0:T(8,128)(2,1)} %get-tuple-element.48), channel_id=1, source_target_pairs={{0,6},{1,7},{2,4},{3,5},{4,2},{5,3},{6,0},{7,1},{8,14},{9,15},{10,... | collective-permute-start | bytes 73736 | tf_op jit(solution)/shard_map/ppermute | solution.py:411
  149.8 0.9 collective-permute-start.17
  150.7 1.2 copy-done.4
  151.9 0.9 gate_back.1
  152.8 3.8 %collective-permute-done.17.refs_7_ = bf16[96,128]{1,0:T(8,128)(2,1)S(1)} collective-permute-done((bf16[96,128]{1,0:T(8,128)(2,1)}, bf16[96,128]{1,0:T(8,128)(2,1)S(1)}, u32[]{:S(2)}, u32[]{:S(2)}) %collective-permute-start.17) | collective-permute-done | bytes 24608 | tf_op jit(solution)/shard_map/ppermute | solution.py:411
  156.7 0.6 copy-done.26
  157.3 3.5 %tokens_out.1 = f32[2,64,768]{2,1,0:T(8,128)} custom-call(s32[5]{0:T(128)} %stack.23.place_ref, f32[128,768]{1,0:T(8,128)} %get-tuple-element.45.gate_in, f32[128,768]{1,0:T(8,128)} %get-tuple-element.46.start_in, bf16[768,768]{1,0:T(8,128)(2,1)} %weight_in.3, bf16[96,128]{1,0:T(8,128)(2,1)} %get-tuple-element.47.refs_0_, bf16[96,128]{1,0:T(8,128)(2,1)} %copy-done.20, ...), custom_call_target="tpu_custom_call" | custom-call | flops 100000000 | bytes 2555924 | tf_op jit(solution)/shard_map/tokens_out/pallas_call | solution.py:377
  160.8 0.4 all-to-all-done.3.recv_ref
  161.2 1.5 finish.1
  (65 shorter events, 0.2 us)
Async XLA Ops:
  5.4 41.3 %all-to-all-start = ((bf16[64,64,128]{2,1,0:T(8,128)(2,1)}), bf16[64,64,128]{2,1,0:T(8,128)(2,1)S(1)}, u32[]{:S(2)}, u32[]{:S(2)}) async-start(bf16[64,64,128]{2,1,0:T(8,128)(2,1)} %bitcast.27), calls=%async_computation | async-start | bytes 2097152 | tf_op jit(solution)/shard_map/all_to_all | solution.py:406
  20.5 31.8 %copy-start.7 = (s32[5]{0:T(128)S(1)}, s32[5]{0:T(128)}, u32[]{:S(2)}) copy-start(s32[5]{0:T(128)} %stack.23.place_ref) | copy-start | bytes 64
  25.6 36.4 %copy-start.33 = (bf16[288,128]{1,0:T(8,128)(2,1)S(1)}, bf16[288,128]{1,0:T(8,128)(2,1)}, u32[]{:S(2)}) copy-start(bf16[288,128]{1,0:T(8,128)(2,1)} %get-tuple-element.27) | copy-start | bytes 221188
  25.6 37.5 %copy-start.32 = (bf16[288,128]{1,0:T(8,128)(2,1)S(1)}, bf16[288,128]{1,0:T(8,128)(2,1)}, u32[]{:S(2)}) copy-start(bf16[288,128]{1,0:T(8,128)(2,1)} %get-tuple-element.28) | copy-start | bytes 221188
  25.6 39.9 %copy-start.31 = (bf16[288,128]{1,0:T(8,128)(2,1)S(1)}, bf16[288,128]{1,0:T(8,128)(2,1)}, u32[]{:S(2)}) copy-start(bf16[288,128]{1,0:T(8,128)(2,1)} %get-tuple-element.29) | copy-start | bytes 221188
  25.6 40.4 %copy-start.30 = (bf16[288,128]{1,0:T(8,128)(2,1)S(1)}, bf16[288,128]{1,0:T(8,128)(2,1)}, u32[]{:S(2)}) copy-start(bf16[288,128]{1,0:T(8,128)(2,1)} %get-tuple-element.30) | copy-start | bytes 221188
  25.6 42.9 %copy-start.29 = (bf16[288,128]{1,0:T(8,128)(2,1)S(1)}, bf16[288,128]{1,0:T(8,128)(2,1)}, u32[]{:S(2)}) copy-start(bf16[288,128]{1,0:T(8,128)(2,1)} %get-tuple-element.31) | copy-start | bytes 221188
  25.7 42.9 %copy-start.28 = (bf16[288,128]{1,0:T(8,128)(2,1)S(1)}, bf16[288,128]{1,0:T(8,128)(2,1)}, u32[]{:S(2)}) copy-start(bf16[288,128]{1,0:T(8,128)(2,1)} %get-tuple-element.32) | copy-start | bytes 221188
  25.7 48.9 %copy-start.27 = (bf16[288,128]{1,0:T(8,128)(2,1)S(1)}, bf16[288,128]{1,0:T(8,128)(2,1)}, u32[]{:S(2)}) copy-start(bf16[288,128]{1,0:T(8,128)(2,1)} %get-tuple-element.33) | copy-start | bytes 221188
  25.7 59.0 %copy-start.1 = (f32[1,32,64,128]{3,2,1,0:T(8,128)S(1)}, f32[1,32,64,128]{3,2,1,0:T(8,128)}, u32[]{:S(2)}) copy-start(f32[1,32,64,128]{3,2,1,0:T(8,128)} %param.13) | copy-start | bytes 3145732
  29.2 59.4 %copy-start.2 = (bf16[2,128,640]{2,1,0:T(8,128)(2,1)S(1)}, bf16[2,128,640]{2,1,0:T(8,128)(2,1)}, u32[]{:S(2)}) copy-start(bf16[2,128,640]{2,1,0:T(8,128)(2,1)} %weight_ref.3) | copy-start | bytes 983044
  29.2 59.4 %copy-start.6 = (bf16[2,128,128]{2,1,0:T(8,128)(2,1)S(1)}, bf16[2,128,128]{2,1,0:T(8,128)(2,1)}, u32[]{:S(2)}) copy-start(bf16[2,128,128]{2,1,0:T(8,128)(2,1)} %out_weight_ref.3) | copy-start | bytes 196612
  29.2 59.4 %copy-start.10 = (s32[1,512]{1,0:T(1,128)S(1)}, s32[1,512]{1,0:T(1,128)}, u32[]{:S(2)}) copy-start(s32[1,512]{1,0:T(1,128)} %mask_ref.2) | copy-start | bytes 6148
  29.2 3.9 %collective-permute-start = (bf16[16,16,128]{2,1,0:T(8,128)(2,1)}, bf16[16,16,128]{2,1,0:T(8,128)(2,1)S(1)}, u32[]{:S(2)}, u32[]{:S(2)}) collective-permute-start(bf16[16,16,128]{2,1,0:T(8,128)(2,1)} %bias.1), channel_id=1, source_target_pairs={{0,128},{128,0},{1,129},{129,1},{2,130},{130,2},{3,131},{131,3},{4... | collective-permute-start | bytes 196616 | tf_op jit(solution)/shard_map/ppermute | solution.py:460
  46.8 5.6 %collective-permute-start.1 = (bf16[8,8,2,16,128]{4,3,2,1,0:T(8,128)(2,1)S(1)}, bf16[8,8,2,16,128]{4,3,2,1,0:T(8,128)(2,1)S(1)}, u32[]{:S(2)}, u32[]{:S(2)}) collective-permute-start(bf16[8,8,2,16,128]{4,3,2,1,0:T(8,128)(2,1)S(1)} %take_right.1), channel_id=1, source_target_pairs={{0,8},{8,0},{1,9},{9,1},{2,10},{10,2},{3,11},{11,3},{4,12},{12,4},... | collective-permute-start | bytes 1572872 | tf_op jit(solution)/shard_map/ppermute | solution.py:402
  55.2 33.4 %all-to-all-start.1 = ((bf16[64,64,128]{2,1,0:T(8,128)(2,1)}), bf16[64,64,128]{2,1,0:T(8,128)(2,1)S(1)}, u32[]{:S(2)}, u32[]{:S(2)}) async-start(bf16[64,64,128]{2,1,0:T(8,128)(2,1)} %bitcast.12), calls=%async_computation.1 | async-start | bytes 2097152 | tf_op jit(solution)/shard_map/all_to_all | solution.py:406
  62.0 6.5 %collective-permute-start.2 = (bf16[288,128]{1,0:T(8,128)(2,1)S(1)}, bf16[288,128]{1,0:T(8,128)(2,1)S(1)}, u32[]{:S(2)}, u32[]{:S(2)}) collective-permute-start(bf16[288,128]{1,0:T(8,128)(2,1)S(1)} %copy-done.33), channel_id=1, source_target_pairs={{0,1},{1,0},{2,3},{3,2},{4,5},{5,4},{6,7},{7,6},{8,9},{9,8},{10,11... | collective-permute-start | bytes 221192 | tf_op jit(solution)/shard_map/ppermute | solution.py:411
  63.1 11.4 %collective-permute-start.3 = (bf16[288,128]{1,0:T(8,128)(2,1)S(1)}, bf16[288,128]{1,0:T(8,128)(2,1)S(1)}, u32[]{:S(2)}, u32[]{:S(2)}) collective-permute-start(bf16[288,128]{1,0:T(8,128)(2,1)S(1)} %copy-done.32), channel_id=1, source_target_pairs={{0,2},{1,3},{2,0},{3,1},{4,6},{5,7},{6,4},{7,5},{8,10},{9,11},{10,... | collective-permute-start | bytes 221192 | tf_op jit(solution)/shard_map/ppermute | solution.py:411
  65.5 9.8 %collective-permute-start.4 = (bf16[288,128]{1,0:T(8,128)(2,1)S(1)}, bf16[288,128]{1,0:T(8,128)(2,1)S(1)}, u32[]{:S(2)}, u32[]{:S(2)}) collective-permute-start(bf16[288,128]{1,0:T(8,128)(2,1)S(1)} %copy-done.31), channel_id=1, source_target_pairs={{0,3},{1,2},{2,1},{3,0},{4,7},{5,6},{6,5},{7,4},{8,11},{9,10},{10,... | collective-permute-start | bytes 221192 | tf_op jit(solution)/shard_map/ppermute | solution.py:411
  66.0 9.3 %collective-permute-start.5 = (bf16[288,128]{1,0:T(8,128)(2,1)S(1)}, bf16[288,128]{1,0:T(8,128)(2,1)S(1)}, u32[]{:S(2)}, u32[]{:S(2)}) collective-permute-start(bf16[288,128]{1,0:T(8,128)(2,1)S(1)} %copy-done.30), channel_id=1, source_target_pairs={{0,4},{1,5},{2,6},{3,7},{4,0},{5,1},{6,2},{7,3},{8,12},{9,13},{10,... | collective-permute-start | bytes 221192 | tf_op jit(solution)/shard_map/ppermute | solution.py:411
  68.5 7.2 %collective-permute-start.6 = (bf16[288,128]{1,0:T(8,128)(2,1)S(1)}, bf16[288,128]{1,0:T(8,128)(2,1)S(1)}, u32[]{:S(2)}, u32[]{:S(2)}) collective-permute-start(bf16[288,128]{1,0:T(8,128)(2,1)S(1)} %copy-done.29), channel_id=1, source_target_pairs={{0,5},{1,4},{2,7},{3,6},{4,1},{5,0},{6,3},{7,2},{8,13},{9,12},{10,... | collective-permute-start | bytes 221192 | tf_op jit(solution)/shard_map/ppermute | solution.py:411
  68.5 14.9 %copy-start.13 = (bf16[288,128]{1,0:T(8,128)(2,1)}, bf16[288,128]{1,0:T(8,128)(2,1)S(1)}, u32[]{:S(2)}) copy-start(bf16[288,128]{1,0:T(8,128)(2,1)S(1)} %collective-permute-done.2.refs_0_.refs_1_) | copy-start | bytes 221188
  68.5 10.0 %collective-permute-start.7 = (bf16[288,128]{1,0:T(8,128)(2,1)S(1)}, bf16[288,128]{1,0:T(8,128)(2,1)S(1)}, u32[]{:S(2)}, u32[]{:S(2)}) collective-permute-start(bf16[288,128]{1,0:T(8,128)(2,1)S(1)} %copy-done.28), channel_id=1, source_target_pairs={{0,6},{1,7},{2,4},{3,5},{4,2},{5,3},{6,0},{7,1},{8,14},{9,15},{10,... | collective-permute-start | bytes 221192 | tf_op jit(solution)/shard_map/ppermute | solution.py:411
  74.6 8.9 %copy-start.14 = (bf16[288,128]{1,0:T(8,128)(2,1)}, bf16[288,128]{1,0:T(8,128)(2,1)S(1)}, u32[]{:S(2)}) copy-start(bf16[288,128]{1,0:T(8,128)(2,1)S(1)} %collective-permute-done.3.refs_1_.refs_2_) | copy-start | bytes 221188
  74.6 8.9 %collective-permute-start.8 = (bf16[288,128]{1,0:T(8,128)(2,1)S(1)}, bf16[288,128]{1,0:T(8,128)(2,1)S(1)}, u32[]{:S(2)}, u32[]{:S(2)}) collective-permute-start(bf16[288,128]{1,0:T(8,128)(2,1)S(1)} %copy-done.27), channel_id=1, source_target_pairs={{0,7},{1,6},{2,5},{3,4},{4,3},{5,2},{6,1},{7,0},{8,15},{9,14},{10,... | collective-permute-start | bytes 221192 | tf_op jit(solution)/shard_map/ppermute | solution.py:411
  75.3 8.1 %copy-start.15 = (bf16[288,128]{1,0:T(8,128)(2,1)}, bf16[288,128]{1,0:T(8,128)(2,1)S(1)}, u32[]{:S(2)}) copy-start(bf16[288,128]{1,0:T(8,128)(2,1)S(1)} %collective-permute-done.4.refs_2_.refs_3_) | copy-start | bytes 221188
  75.3 8.1 %copy-start.16 = (bf16[288,128]{1,0:T(8,128)(2,1)}, bf16[288,128]{1,0:T(8,128)(2,1)S(1)}, u32[]{:S(2)}) copy-start(bf16[288,128]{1,0:T(8,128)(2,1)S(1)} %collective-permute-done.5.refs_3_.refs_4_) | copy-start | bytes 221188
  75.7 7.8 %copy-start.17 = (bf16[288,128]{1,0:T(8,128)(2,1)}, bf16[288,128]{1,0:T(8,128)(2,1)S(1)}, u32[]{:S(2)}) copy-start(bf16[288,128]{1,0:T(8,128)(2,1)S(1)} %collective-permute-done.6.refs_4_.refs_5_) | copy-start | bytes 221188
  78.5 5.0 %copy-start.18 = (bf16[288,128]{1,0:T(8,128)(2,1)}, bf16[288,128]{1,0:T(8,128)(2,1)S(1)}, u32[]{:S(2)}) copy-start(bf16[288,128]{1,0:T(8,128)(2,1)S(1)} %collective-permute-done.7.refs_5_.refs_6_) | copy-start | bytes 221188
  83.5 0.6 copy-start.19
  84.7 0.7 copy-start.9
  85.4 43.1 %copy-start.8 = (s32[5]{0:T(128)S(1)}, s32[5]{0:T(128)}, u32[]{:S(2)}) copy-start(s32[5]{0:T(128)} %stack.23.place_ref) | copy-start | bytes 64
  88.7 17.4 %copy-start = (bf16[64,64,128]{2,1,0:T(8,128)(2,1)}, bf16[64,64,128]{2,1,0:T(8,128)(2,1)S(1)}, u32[]{:S(2)}) copy-start(bf16[64,64,128]{2,1,0:T(8,128)(2,1)S(1)} %all-to-all-done.1.recv_ref) | copy-start | bytes 3145732
  91.8 1.0 copy-start.3
  92.8 1.0 copy-start.5
  93.8 34.8 %all-to-all-start.2 = ((bf16[64,64,128]{2,1,0:T(8,128)(2,1)}), bf16[64,64,128]{2,1,0:T(8,128)(2,1)S(1)}, u32[]{:S(2)}, u32[]{:S(2)}) async-start(bf16[64,64,128]{2,1,0:T(8,128)(2,1)} %bitcast.26), calls=%async_computation.2 | async-start | bytes 2097152 | tf_op jit(solution)/shard_map/all_to_all | solution.py:406
  102.7 3.3 %collective-permute-start.9 = (bf16[64,32,128]{2,1,0:T(8,128)(2,1)S(1)}, bf16[64,32,128]{2,1,0:T(8,128)(2,1)S(1)}, u32[]{:S(2)}, u32[]{:S(2)}) collective-permute-start(bf16[64,32,128]{2,1,0:T(8,128)(2,1)S(1)} %slice.4), channel_id=1, source_target_pairs={{0,8},{8,0},{1,9},{9,1},{2,10},{10,2},{3,11},{11,3},{4,12},{12,4},... | collective-permute-start | bytes 1572872 | tf_op jit(solution)/shard_map/ppermute | solution.py:402
  106.1 0.8 copy-start.12
  112.6 6.8 %collective-permute-start.10 = (bf16[96,128]{1,0:T(8,128)(2,1)}, bf16[96,128]{1,0:T(8,128)(2,1)S(1)}, u32[]{:S(2)}, u32[]{:S(2)}) collective-permute-start(bf16[96,128]{1,0:T(8,128)(2,1)} %get-tuple-element.35), channel_id=1, source_target_pairs={{0,1},{1,0},{2,3},{3,2},{4,5},{5,4},{6,7},{7,6},{8,9},{9,8},{10,11... | collective-permute-start | bytes 73736 | tf_op jit(solution)/shard_map/ppermute | solution.py:411
  114.0 5.7 %collective-permute-start.11 = (bf16[96,128]{1,0:T(8,128)(2,1)}, bf16[96,128]{1,0:T(8,128)(2,1)S(1)}, u32[]{:S(2)}, u32[]{:S(2)}) collective-permute-start(bf16[96,128]{1,0:T(8,128)(2,1)} %get-tuple-element.36), channel_id=1, source_target_pairs={{0,2},{1,3},{2,0},{3,1},{4,6},{5,7},{6,4},{7,5},{8,10},{9,11},{10,... | collective-permute-start | bytes 73736 | tf_op jit(solution)/shard_map/ppermute | solution.py:411
  116.4 4.4 %collective-permute-start.12 = (bf16[96,128]{1,0:T(8,128)(2,1)}, bf16[96,128]{1,0:T(8,128)(2,1)S(1)}, u32[]{:S(2)}, u32[]{:S(2)}) collective-permute-start(bf16[96,128]{1,0:T(8,128)(2,1)} %get-tuple-element.37), channel_id=1, source_target_pairs={{0,3},{1,2},{2,1},{3,0},{4,7},{5,6},{6,5},{7,4},{8,11},{9,10},{10,... | collective-permute-start | bytes 73736 | tf_op jit(solution)/shard_map/ppermute | solution.py:411
  116.6 5.9 %collective-permute-start.13 = (bf16[96,128]{1,0:T(8,128)(2,1)}, bf16[96,128]{1,0:T(8,128)(2,1)S(1)}, u32[]{:S(2)}, u32[]{:S(2)}) collective-permute-start(bf16[96,128]{1,0:T(8,128)(2,1)} %get-tuple-element.38), channel_id=1, source_target_pairs={{0,4},{1,5},{2,6},{3,7},{4,0},{5,1},{6,2},{7,3},{8,12},{9,13},{10,... | collective-permute-start | bytes 73736 | tf_op jit(solution)/shard_map/ppermute | solution.py:411
  119.3 5.6 %collective-permute-start.14 = (bf16[96,128]{1,0:T(8,128)(2,1)}, bf16[96,128]{1,0:T(8,128)(2,1)S(1)}, u32[]{:S(2)}, u32[]{:S(2)}) collective-permute-start(bf16[96,128]{1,0:T(8,128)(2,1)} %get-tuple-element.39), channel_id=1, source_target_pairs={{0,5},{1,4},{2,7},{3,6},{4,1},{5,0},{6,3},{7,2},{8,13},{9,12},{10,... | collective-permute-start | bytes 73736 | tf_op jit(solution)/shard_map/ppermute | solution.py:411
  119.4 5.6 %copy-start.20 = (bf16[96,128]{1,0:T(8,128)(2,1)}, bf16[96,128]{1,0:T(8,128)(2,1)S(1)}, u32[]{:S(2)}) copy-start(bf16[96,128]{1,0:T(8,128)(2,1)S(1)} %collective-permute-done.10.refs_0_.refs_1_) | copy-start | bytes 73732
  119.7 5.3 %copy-start.21 = (bf16[96,128]{1,0:T(8,128)(2,1)}, bf16[96,128]{1,0:T(8,128)(2,1)S(1)}, u32[]{:S(2)}) copy-start(bf16[96,128]{1,0:T(8,128)(2,1)S(1)} %collective-permute-done.11.refs_1_.refs_2_) | copy-start | bytes 73732
  120.8 4.2 %copy-start.22 = (bf16[96,128]{1,0:T(8,128)(2,1)}, bf16[96,128]{1,0:T(8,128)(2,1)S(1)}, u32[]{:S(2)}) copy-start(bf16[96,128]{1,0:T(8,128)(2,1)S(1)} %collective-permute-done.12.refs_2_.refs_3_) | copy-start | bytes 73732
  122.5 2.5 %copy-start.23 = (bf16[96,128]{1,0:T(8,128)(2,1)}, bf16[96,128]{1,0:T(8,128)(2,1)S(1)}, u32[]{:S(2)}) copy-start(bf16[96,128]{1,0:T(8,128)(2,1)S(1)} %collective-permute-done.13.refs_3_.refs_4_) | copy-start | bytes 73732
  125.0 0.6 copy-start.24
  128.5 0.7 copy-start.11
  131.1 6.0 %collective-permute-start.15 = (bf16[8,8,32,128]{3,2,1,0:T(8,128)(2,1)S(1)}, bf16[8,8,32,128]{3,2,1,0:T(8,128)(2,1)S(1)}, u32[]{:S(2)}, u32[]{:S(2)}) collective-permute-start(bf16[8,8,32,128]{3,2,1,0:T(8,128)(2,1)S(1)} %get-tuple-element.41), channel_id=1, source_target_pairs={{0,8},{8,0},{1,9},{9,1},{2,10},{10,2},{3,11},{11,3},{4,12},{12,4},... | collective-permute-start | bytes 1572872 | tf_op jit(solution)/shard_map/ppermute | solution.py:402
  138.1 23.1 %all-to-all-start.3 = ((bf16[64,32,128]{2,1,0:T(8,128)(2,1)}), bf16[64,32,128]{2,1,0:T(8,128)(2,1)S(1)}, u32[]{:S(2)}, u32[]{:S(2)}) async-start(bf16[64,32,128]{2,1,0:T(8,128)(2,1)} %bitcast.17), calls=%async_computation.3 | async-start | bytes 1048576 | tf_op jit(solution)/shard_map/all_to_all | solution.py:406
  144.8 8.0 %collective-permute-start.16 = (bf16[96,128]{1,0:T(8,128)(2,1)}, bf16[96,128]{1,0:T(8,128)(2,1)S(1)}, u32[]{:S(2)}, u32[]{:S(2)}) collective-permute-start(bf16[96,128]{1,0:T(8,128)(2,1)} %get-tuple-element.48), channel_id=1, source_target_pairs={{0,6},{1,7},{2,4},{3,5},{4,2},{5,3},{6,0},{7,1},{8,14},{9,15},{10,... | collective-permute-start | bytes 73736 | tf_op jit(solution)/shard_map/ppermute | solution.py:411
  149.8 6.8 %collective-permute-start.17 = (bf16[96,128]{1,0:T(8,128)(2,1)}, bf16[96,128]{1,0:T(8,128)(2,1)S(1)}, u32[]{:S(2)}, u32[]{:S(2)}) collective-permute-start(bf16[96,128]{1,0:T(8,128)(2,1)} %get-tuple-element.49), channel_id=1, source_target_pairs={{0,7},{1,6},{2,5},{3,4},{4,3},{5,2},{6,1},{7,0},{8,15},{9,14},{10,... | collective-permute-start | bytes 73736 | tf_op jit(solution)/shard_map/ppermute | solution.py:411
  150.7 1.2 copy-start.4
  152.8 3.8 %copy-start.25 = (bf16[96,128]{1,0:T(8,128)(2,1)}, bf16[96,128]{1,0:T(8,128)(2,1)S(1)}, u32[]{:S(2)}) copy-start(bf16[96,128]{1,0:T(8,128)(2,1)S(1)} %collective-permute-done.16.refs_6_) | copy-start | bytes 73732
  156.6 0.6 copy-start.26

commit v6 on v5

--- a/solution.py
+++ b/solution.py
@@ -83,9 +83,11 @@
 
 
 def project_kernel(
-    place_ref, mask_in, pair_in, weight_in, out_ref,
+    mask_in, pair_in, weight_in, out_ref,
     mask_ref, pair_ref, weight_ref, normed_ref, spread_ref, stage_ref, in_sems, out_sems,
 ):
+    row0 = (lax.axis_index("z") * 2 + lax.axis_index("core")) * ROWS
+    col0 = lax.axis_index("col") * COLS
     copies = [
         pltpu.make_async_copy(mask_in, mask_ref, in_sems.at[4]),
         pltpu.make_async_copy(weight_in, weight_ref, in_sems.at[5]),
@@ -107,7 +109,7 @@
             values = jnp.transpose(pair_step(pair_ref, step), (1, 0))
             normed_ref[step] = layer_norm(values, 0).astype(BF16)
     project_out(
-        normed_ref, weight, length, place_ref[0], place_ref[1], spread_ref, stage_ref, out_ref, out_sems
+        normed_ref, weight, length, row0, col0, spread_ref, stage_ref, out_ref, out_sems
     )
 
 
@@ -438,7 +440,7 @@
             pltpu.VMEM((1, TOK), jnp.int32), pltpu.VMEM(tile, F32), pltpu.VMEM((2, C, 5 * C), BF16),
             normed, spread, stage, pltpu.SemaphoreType.DMA((6,)), sems,
         ],
-        place, pair_mask, pair0, trunk_in, smem=1, far=(1, 2, 3), far_out=(0,),
+        pair_mask, pair0, trunk_in, far=(0, 1, 2), far_out=(0,),
     )
     gathered = exchange(operands.reshape(64, 64, 128)).reshape(8, 8, 2, 32, 128)
 

time: 165 us -> 164 us (level)
  transfers between devices with their start and end apart: 22 -> 22, of which waited for: 16 -> 16; matrix products, arithmetic and copies ran while one was open for 0% -> 0% of each run, Pallas kernels for 12% -> 13%
where the time goes in v6:
time: 164 us; the launch traced here: 162 us
  starting transfers between devices  74.2 us (45%)
  waiting for transfers between devices  44.3 us (27%)
  Pallas kernels  34.1 us (21%)
  local copies, waits for them, and re-layouts  7.98 us (5%)
    all_to_all x4, starting transfers between devices, exchange(): return lax.all_to_all(value, ALL, 0, 0, tiled=True)  37.6 us
    pallas_call x15, Pallas kernels, call(): pl.pallas_call(kernel, name=name, out_shape=out_shape, in_specs=[scalar i...  34.1 us
    ppermute x14, starting transfers between devices, swap(): lax.ppermute(values[slot], axis, [(at, at ^ slot) for at in range(8)])  25.9 us
    all_to_all x4, waiting for transfers between devices, exchange(): return lax.all_to_all(value, ALL, 0, 0, tiled=True)  18.8 us
    ppermute x14, waiting for transfers between devices, swap(): lax.ppermute(values[slot], axis, [(at, at ^ slot) for at in range(8)])  17.5 us
    ppermute x3, starting transfers between devices, from_other_core(): return lax.ppermute(value, 'core', [(0, 1), (1, 0)])  10.3 us
    unnamed x68, local copies, waits for them, and re-layouts  7.31 us
    ppermute x3, waiting for transfers between devices, from_other_core(): return lax.ppermute(value, 'core', [(0, 1), (1, 0)])  4.61 us
  transfers between devices with their start and end apart: 22, of which 16 were waited for; matrix products, arithmetic and copies ran while one was open for 0% of the time, Pallas kernels for 13%

profile of v6, /device:TPU:1, one launch (start us, length us, event | category | flops | bytes accessed | tf_op | source)
XLA Modules:
  0.0 161.6 jit_solution(14357807519834224305)
XLA Ops:
  0.6 3.4 %project.1.refs_0_ = bf16[128,32,128]{2,1,0:T(8,128)(2,1)} custom-call(s32[1,512]{1,0:T(1,128)} %mask_ref.2, f32[2,16,64,128]{3,2,1,0:T(8,128)} %bitcast.23, bf16[2,128,640]{2,1,0:T(8,128)(2,1)} %weight_ref.3), custom_call_target="tpu_custom_call" | custom-call | flops 100000000 | bytes 2426880 | tf_op jit(solution)/shard_map/project/pallas_call | solution.py:379
  4.1 15.2 %all-to-all-start = ((bf16[64,64,128]{2,1,0:T(8,128)(2,1)}), bf16[64,64,128]{2,1,0:T(8,128)(2,1)S(1)}, u32[]{:S(2)}, u32[]{:S(2)}) async-start(bf16[64,64,128]{2,1,0:T(8,128)(2,1)} %bitcast.27), calls=%async_computation | async-start | bytes 2097152 | tf_op jit(solution)/shard_map/all_to_all | solution.py:408
  19.2 0.6 stack.23.place_ref
  19.9 5.0 %tokens_in.1 = (f32[128,768]{1,0:T(8,128)}, f32[128,768]{1,0:T(8,128)}, bf16[288,128]{1,0:T(8,128)(2,1)}, bf16[288,128]{1,0:T(8,128)(2,1)}, bf16[288,128]{1,0:T(...) custom-call(s32[5]{0:T(128)} %stack.23.place_ref, ...), custom_call_target="tpu_custom_call" | custom-call | flops 100000000 | bytes 6816788 | tf_op jit(solution)/shard_map/tokens_in/pallas_call | solution.py:379
  25.0 0.0 copy-start.1
  25.0 3.5 %bias.1 = bf16[16,16,128]{2,1,0:T(8,128)(2,1)} custom-call(f32[2,16,64,128]{3,2,1,0:T(8,128)} %bitcast.29, bf16[16,128]{1,0:T(8,128)(2,1)} %bitcast.34, bf16[288,128]{1,0:T(8,128)(2,1)} %get-tuple-element.26.refs_0_), custom_call_target="tpu_custom_call" | custom-call | flops 100000000 | bytes 1118208 | tf_op jit(solution)/shard_map/bias/pallas_call | solution.py:379
  28.6 0.4 collective-permute-start
  29.0 3.3 %collective-permute-done.bias_ref = bf16[16,16,128]{2,1,0:T(8,128)(2,1)S(1)} collective-permute-done((bf16[16,16,128]{2,1,0:T(8,128)(2,1)}, bf16[16,16,128]{2,1,0:T(8,128)(2,1)S(1)}, u32[]{:S(2)}, u32[]{:S(2)}) %collective-permute-start) | collective-permute-done | bytes 65568 | tf_op jit(solution)/shard_map/ppermute | solution.py:462
  32.3 13.1 %all-to-all-done = bf16[64,64,128]{2,1,0:T(8,128)(2,1)S(1)} async-done(((bf16[64,64,128]{2,1,0:T(8,128)(2,1)}), bf16[64,64,128]{2,1,0:T(8,128)(2,1)S(1)}, u32[]{:S(2)}, u32[]{:S(2)}) %all-to-all-start) | async-done | bytes 1048608 | tf_op jit(solution)/shard_map/all_to_all | solution.py:408
  45.5 4.0 %collective-permute-start.1 = (bf16[8,8,2,16,128]{4,3,2,1,0:T(8,128)(2,1)S(1)}, bf16[8,8,2,16,128]{4,3,2,1,0:T(8,128)(2,1)S(1)}, u32[]{:S(2)}, u32[]{:S(2)}) collective-permute-start(bf16[8,8,2,16,128]{4,3,2,1,0:T(8,128)(2,1)S(1)} %take_right.1), channel_id=1, source_target_pairs={{0,8},{8,0},{1,9},{9,1},{2,10},{10,2},{3,11},{11,3},{4,12},{12,4},... | collective-permute-start | bytes 1572872 | tf_op jit(solution)/shard_map/ppermute | solution.py:404
  49.5 1.5 collective-permute-done.1.far_ref
  51.0 2.9 %outgoing.1 = bf16[8,8,64,128]{3,2,1,0:T(8,128)(2,1)} custom-call(s32[5]{0:T(128)S(1)} %copy-done.7, bf16[8,8,2,32,128]{4,3,2,1,0:T(8,128)(2,1)S(1)} %bitcast.22, bf16[8,8,2,16,128]{4,3,2,1,0:T(8,128)(2,1)S(1)} %collective-permute-done.1.far_ref, bf16[16,16,128]{2,1,0:T(8,128)(2,1)S(1)} %collective-permute-done.bias_ref), custom_call_target="tpu_custom_call" | custom-call | flops 268435456 | bytes 2686996 | tf_op jit(solution)/shard_map/outgoing/pallas_call | solution.py:379
  53.9 6.8 %all-to-all-start.1 = ((bf16[64,64,128]{2,1,0:T(8,128)(2,1)}), bf16[64,64,128]{2,1,0:T(8,128)(2,1)S(1)}, u32[]{:S(2)}, u32[]{:S(2)}) async-start(bf16[64,64,128]{2,1,0:T(8,128)(2,1)} %bitcast.12), calls=%async_computation.1 | async-start | bytes 2097152 | tf_op jit(solution)/shard_map/all_to_all | solution.py:408
  60.7 1.1 collective-permute-start.2
  61.8 2.4 %collective-permute-start.3 = (bf16[288,128]{1,0:T(8,128)(2,1)S(1)}, bf16[288,128]{1,0:T(8,128)(2,1)S(1)}, u32[]{:S(2)}, u32[]{:S(2)}) collective-permute-start(bf16[288,128]{1,0:T(8,128)(2,1)S(1)} %copy-done.32), channel_id=1, source_target_pairs={{0,2},{1,3},{2,0},{3,1},{4,6},{5,7},{6,4},{7,5},{8,10},{9,11},{10,... | collective-permute-start | bytes 221192 | tf_op jit(solution)/shard_map/ppermute | solution.py:413
  64.2 0.5 collective-permute-start.4
  64.7 2.5 %collective-permute-start.5 = (bf16[288,128]{1,0:T(8,128)(2,1)S(1)}, bf16[288,128]{1,0:T(8,128)(2,1)S(1)}, u32[]{:S(2)}, u32[]{:S(2)}) collective-permute-start(bf16[288,128]{1,0:T(8,128)(2,1)S(1)} %copy-done.30), channel_id=1, source_target_pairs={{0,4},{1,5},{2,6},{3,7},{4,0},{5,1},{6,2},{7,3},{8,12},{9,13},{10,... | collective-permute-start | bytes 221192 | tf_op jit(solution)/shard_map/ppermute | solution.py:413
  67.2 0.0 collective-permute-start.6
  67.2 6.0 %collective-permute-start.7 = (bf16[288,128]{1,0:T(8,128)(2,1)S(1)}, bf16[288,128]{1,0:T(8,128)(2,1)S(1)}, u32[]{:S(2)}, u32[]{:S(2)}) collective-permute-start(bf16[288,128]{1,0:T(8,128)(2,1)S(1)} %copy-done.28), channel_id=1, source_target_pairs={{0,6},{1,7},{2,4},{3,5},{4,2},{5,3},{6,0},{7,1},{8,14},{9,15},{10,... | collective-permute-start | bytes 221192 | tf_op jit(solution)/shard_map/ppermute | solution.py:413
  73.3 0.7 collective-permute-start.8
  74.0 0.0 collective-permute-done.4.refs_2_.refs_3_
  74.0 0.4 collective-permute-done.6.refs_4_.refs_5_
  74.4 2.8 %collective-permute-done.7.refs_5_.refs_6_ = bf16[288,128]{1,0:T(8,128)(2,1)S(1)} collective-permute-done((bf16[288,128]{1,0:T(8,128)(2,1)S(1)}, bf16[288,128]{1,0:T(8,128)(2,1)S(1)}, u32[]{:S(2)}, u32[]{:S(2)}) %collective-permute-start.7) | collective-permute-done | bytes 73760 | tf_op jit(solution)/shard_map/ppermute | solution.py:413
  77.2 4.9 %collective-permute-done.8.refs_6_.refs_7_ = bf16[288,128]{1,0:T(8,128)(2,1)S(1)} collective-permute-done((bf16[288,128]{1,0:T(8,128)(2,1)S(1)}, bf16[288,128]{1,0:T(8,128)(2,1)S(1)}, u32[]{:S(2)}, u32[]{:S(2)}) %collective-permute-start.8) | collective-permute-done | bytes 73760 | tf_op jit(solution)/shard_map/ppermute | solution.py:413
  82.2 0.6 copy-done.19
  82.8 0.6 fence.2.refs_0_
  83.4 0.7 copy-done.9
  84.1 0.3 turn.1.pair_ref
  84.4 2.9 %all-to-all-done.1.recv_ref = bf16[64,64,128]{2,1,0:T(8,128)(2,1)S(1)} async-done(((bf16[64,64,128]{2,1,0:T(8,128)(2,1)}), bf16[64,64,128]{2,1,0:T(8,128)(2,1)S(1)}, u32[]{:S(2)}, u32[]{:S(2)}) %all-to-all-start.1) | async-done | bytes 1048608 | tf_op jit(solution)/shard_map/all_to_all | solution.py:408
  87.4 3.1 %finish_project.1 = (f32[16,128,128]{2,1,0:T(8,128)S(1)}, bf16[128,32,128]{2,1,0:T(8,128)(2,1)S(1)}) custom-call(s32[5]{0:T(128)S(1)} %copy-done.7, s32[1,512]{1,0:T(1,128)S(1)} %copy-done.10, bf16[64,64,128]{2,1,0:T(8,128)(2,1)S(1)} %all-to-all-done.1.recv_ref, f32[16,128,128]{2,1,0:T(8,128)S(1)} %turn.1.pair_ref, bf16[2,128,128]{2,1,0:T(8,128)(2,1)S(1)} %copy-done.6, ...), custom_call_target="tpu_custom_call" | custom-call | flops 100000000 | bytes 4589588 | tf_op jit(solution)/shard_map/finish_project/pallas_call | solution.py:379
  90.5 1.0 copy-done.3
  91.5 1.0 copy-done.5
  92.5 8.9 %all-to-all-start.2 = ((bf16[64,64,128]{2,1,0:T(8,128)(2,1)}), bf16[64,64,128]{2,1,0:T(8,128)(2,1)S(1)}, u32[]{:S(2)}, u32[]{:S(2)}) async-start(bf16[64,64,128]{2,1,0:T(8,128)(2,1)} %bitcast.26), calls=%async_computation.2 | async-start | bytes 2097152 | tf_op jit(solution)/shard_map/all_to_all | solution.py:408
  101.4 1.8 %collective-permute-start.9 = (bf16[64,32,128]{2,1,0:T(8,128)(2,1)S(1)}, bf16[64,32,128]{2,1,0:T(8,128)(2,1)S(1)}, u32[]{:S(2)}, u32[]{:S(2)}) collective-permute-start(bf16[64,32,128]{2,1,0:T(8,128)(2,1)S(1)} %slice.4), channel_id=1, source_target_pairs={{0,8},{8,0},{1,9},{9,1},{2,10},{10,2},{3,11},{11,3},{4,12},{12,4},... | collective-permute-start | bytes 1572872 | tf_op jit(solution)/shard_map/ppermute | solution.py:404
  103.2 1.5 collective-permute-done.9
  104.8 0.8 copy-done.12
  105.5 5.8 %attention.1 = (bf16[96,128]{1,0:T(8,128)(2,1)}, bf16[96,128]{1,0:T(8,128)(2,1)}, bf16[96,128]{1,0:T(8,128)(2,1)}, bf16[96,128]{1,0:T(8,128)(2,1)}, bf16[96,128]...) custom-call(s32[5]{0:T(128)} %stack.23.place_ref, ...), custom_call_target="tpu_custom_call" | custom-call | flops 100000000 | bytes 2361364 | tf_op jit(solution)/shard_map/attention/pallas_call | solution.py:379
  111.3 1.4 collective-permute-start.10
  112.7 2.4 %collective-permute-start.11 = (bf16[96,128]{1,0:T(8,128)(2,1)}, bf16[96,128]{1,0:T(8,128)(2,1)S(1)}, u32[]{:S(2)}, u32[]{:S(2)}) collective-permute-start(bf16[96,128]{1,0:T(8,128)(2,1)} %get-tuple-element.36), channel_id=1, source_target_pairs={{0,2},{1,3},{2,0},{3,1},{4,6},{5,7},{6,4},{7,5},{8,10},{9,11},{10,... | collective-permute-start | bytes 73736 | tf_op jit(solution)/shard_map/ppermute | solution.py:413
  115.1 0.2 collective-permute-start.12
  115.3 2.8 %collective-permute-start.13 = (bf16[96,128]{1,0:T(8,128)(2,1)}, bf16[96,128]{1,0:T(8,128)(2,1)S(1)}, u32[]{:S(2)}, u32[]{:S(2)}) collective-permute-start(bf16[96,128]{1,0:T(8,128)(2,1)} %get-tuple-element.38), channel_id=1, source_target_pairs={{0,4},{1,5},{2,6},{3,7},{4,0},{5,1},{6,2},{7,3},{8,12},{9,13},{10,... | collective-permute-start | bytes 73736 | tf_op jit(solution)/shard_map/ppermute | solution.py:413
  118.1 0.0 collective-permute-start.14
  118.1 0.3 collective-permute-done.11.refs_1_.refs_2_
  118.4 1.1 collective-permute-done.12.refs_2_.refs_3_
  119.5 1.7 %collective-permute-done.13.refs_3_.refs_4_ = bf16[96,128]{1,0:T(8,128)(2,1)S(1)} collective-permute-done((bf16[96,128]{1,0:T(8,128)(2,1)}, bf16[96,128]{1,0:T(8,128)(2,1)S(1)}, u32[]{:S(2)}, u32[]{:S(2)}) %collective-permute-start.13) | collective-permute-done | bytes 24608 | tf_op jit(solution)/shard_map/ppermute | solution.py:413
  121.2 2.5 %collective-permute-done.14.refs_4_.refs_5_ = bf16[96,128]{1,0:T(8,128)(2,1)S(1)} collective-permute-done((bf16[96,128]{1,0:T(8,128)(2,1)}, bf16[96,128]{1,0:T(8,128)(2,1)S(1)}, u32[]{:S(2)}, u32[]{:S(2)}) %collective-permute-start.14) | collective-permute-done | bytes 24608 | tf_op jit(solution)/shard_map/ppermute | solution.py:413
  123.7 0.6 copy-done.24
  124.3 0.6 fence.3.token_ref
  124.9 2.3 %all-to-all-done.2 = bf16[64,64,128]{2,1,0:T(8,128)(2,1)S(1)} async-done(((bf16[64,64,128]{2,1,0:T(8,128)(2,1)}), bf16[64,64,128]{2,1,0:T(8,128)(2,1)S(1)}, u32[]{:S(2)}, u32[]{:S(2)}) %all-to-all-start.2) | async-done | bytes 1048608 | tf_op jit(solution)/shard_map/all_to_all | solution.py:408
  127.2 0.7 copy-done.11
  127.9 1.9 %incoming.1 = (bf16[8,8,32,128]{3,2,1,0:T(8,128)(2,1)S(1)}, bf16[8,8,32,128]{3,2,1,0:T(8,128)(2,1)S(1)}) custom-call(s32[5]{0:T(128)S(1)} %copy-done.8, bf16[8,8,2,32,128]{4,3,2,1,0:T(8,128)(2,1)S(1)} %bitcast.25, f32[8,128]{1,0:T(8,128)S(1)} %copy-done.11), custom_call_target="tpu_custom_call" | custom-call | flops 268435456 | bytes 2101268 | tf_op jit(solution)/shard_map/incoming/pallas_call | solution.py:379
  129.8 4.5 %collective-permute-start.15 = (bf16[8,8,32,128]{3,2,1,0:T(8,128)(2,1)S(1)}, bf16[8,8,32,128]{3,2,1,0:T(8,128)(2,1)S(1)}, u32[]{:S(2)}, u32[]{:S(2)}) collective-permute-start(bf16[8,8,32,128]{3,2,1,0:T(8,128)(2,1)S(1)} %get-tuple-element.41), channel_id=1, source_target_pairs={{0,8},{8,0},{1,9},{9,1},{2,10},{10,2},{3,11},{11,3},{4,12},{12,4},... | collective-permute-start | bytes 1572872 | tf_op jit(solution)/shard_map/ppermute | solution.py:404
  134.3 1.5 collective-permute-done.15.far_ref
  135.8 0.9 add.5
  136.8 6.8 %all-to-all-start.3 = ((bf16[64,32,128]{2,1,0:T(8,128)(2,1)}), bf16[64,32,128]{2,1,0:T(8,128)(2,1)S(1)}, u32[]{:S(2)}, u32[]{:S(2)}) async-start(bf16[64,32,128]{2,1,0:T(8,128)(2,1)} %bitcast.17), calls=%async_computation.3 | async-start | bytes 1048576 | tf_op jit(solution)/shard_map/all_to_all | solution.py:408
  143.5 5.0 %collective-permute-start.16 = (bf16[96,128]{1,0:T(8,128)(2,1)}, bf16[96,128]{1,0:T(8,128)(2,1)S(1)}, u32[]{:S(2)}, u32[]{:S(2)}) collective-permute-start(bf16[96,128]{1,0:T(8,128)(2,1)} %get-tuple-element.48), channel_id=1, source_target_pairs={{0,6},{1,7},{2,4},{3,5},{4,2},{5,3},{6,0},{7,1},{8,14},{9,15},{10,... | collective-permute-start | bytes 73736 | tf_op jit(solution)/shard_map/ppermute | solution.py:413
  148.5 0.9 collective-permute-start.17
  149.4 1.2 copy-done.4
  150.6 0.9 gate_back.1
  151.5 3.8 %collective-permute-done.17.refs_7_ = bf16[96,128]{1,0:T(8,128)(2,1)S(1)} collective-permute-done((bf16[96,128]{1,0:T(8,128)(2,1)}, bf16[96,128]{1,0:T(8,128)(2,1)S(1)}, u32[]{:S(2)}, u32[]{:S(2)}) %collective-permute-start.17) | collective-permute-done | bytes 24608 | tf_op jit(solution)/shard_map/ppermute | solution.py:413
  155.4 0.6 copy-done.26
  156.0 3.5 %tokens_out.1 = f32[2,64,768]{2,1,0:T(8,128)} custom-call(s32[5]{0:T(128)} %stack.23.place_ref, f32[128,768]{1,0:T(8,128)} %get-tuple-element.45.gate_in, f32[128,768]{1,0:T(8,128)} %get-tuple-element.46.start_in, bf16[768,768]{1,0:T(8,128)(2,1)} %weight_in.3, bf16[96,128]{1,0:T(8,128)(2,1)} %get-tuple-element.47.refs_0_, bf16[96,128]{1,0:T(8,128)(2,1)} %copy-done.20, ...), custom_call_target="tpu_custom_call" | custom-call | flops 100000000 | bytes 2555924 | tf_op jit(solution)/shard_map/tokens_out/pallas_call | solution.py:379
  159.5 0.4 all-to-all-done.3.recv_ref
  159.9 1.5 finish.1
  (65 shorter events, 0.2 us)
Async XLA Ops:
  4.1 41.4 %all-to-all-start = ((bf16[64,64,128]{2,1,0:T(8,128)(2,1)}), bf16[64,64,128]{2,1,0:T(8,128)(2,1)S(1)}, u32[]{:S(2)}, u32[]{:S(2)}) async-start(bf16[64,64,128]{2,1,0:T(8,128)(2,1)} %bitcast.27), calls=%async_computation | async-start | bytes 2097152 | tf_op jit(solution)/shard_map/all_to_all | solution.py:408
  19.9 31.2 %copy-start.7 = (s32[5]{0:T(128)S(1)}, s32[5]{0:T(128)}, u32[]{:S(2)}) copy-start(s32[5]{0:T(128)} %stack.23.place_ref) | copy-start | bytes 64
  24.9 35.8 %copy-start.33 = (bf16[288,128]{1,0:T(8,128)(2,1)S(1)}, bf16[288,128]{1,0:T(8,128)(2,1)}, u32[]{:S(2)}) copy-start(bf16[288,128]{1,0:T(8,128)(2,1)} %get-tuple-element.27) | copy-start | bytes 221188
  24.9 36.9 %copy-start.32 = (bf16[288,128]{1,0:T(8,128)(2,1)S(1)}, bf16[288,128]{1,0:T(8,128)(2,1)}, u32[]{:S(2)}) copy-start(bf16[288,128]{1,0:T(8,128)(2,1)} %get-tuple-element.28) | copy-start | bytes 221188
  25.0 39.3 %copy-start.31 = (bf16[288,128]{1,0:T(8,128)(2,1)S(1)}, bf16[288,128]{1,0:T(8,128)(2,1)}, u32[]{:S(2)}) copy-start(bf16[288,128]{1,0:T(8,128)(2,1)} %get-tuple-element.29) | copy-start | bytes 221188
  25.0 39.7 %copy-start.30 = (bf16[288,128]{1,0:T(8,128)(2,1)S(1)}, bf16[288,128]{1,0:T(8,128)(2,1)}, u32[]{:S(2)}) copy-start(bf16[288,128]{1,0:T(8,128)(2,1)} %get-tuple-element.30) | copy-start | bytes 221188
  25.0 42.2 %copy-start.29 = (bf16[288,128]{1,0:T(8,128)(2,1)S(1)}, bf16[288,128]{1,0:T(8,128)(2,1)}, u32[]{:S(2)}) copy-start(bf16[288,128]{1,0:T(8,128)(2,1)} %get-tuple-element.31) | copy-start | bytes 221188
  25.0 42.3 %copy-start.28 = (bf16[288,128]{1,0:T(8,128)(2,1)S(1)}, bf16[288,128]{1,0:T(8,128)(2,1)}, u32[]{:S(2)}) copy-start(bf16[288,128]{1,0:T(8,128)(2,1)} %get-tuple-element.32) | copy-start | bytes 221188
  25.0 48.3 %copy-start.27 = (bf16[288,128]{1,0:T(8,128)(2,1)S(1)}, bf16[288,128]{1,0:T(8,128)(2,1)}, u32[]{:S(2)}) copy-start(bf16[288,128]{1,0:T(8,128)(2,1)} %get-tuple-element.33) | copy-start | bytes 221188
  25.0 58.4 %copy-start.1 = (f32[1,32,64,128]{3,2,1,0:T(8,128)S(1)}, f32[1,32,64,128]{3,2,1,0:T(8,128)}, u32[]{:S(2)}) copy-start(f32[1,32,64,128]{3,2,1,0:T(8,128)} %param.13) | copy-start | bytes 3145732
  28.6 58.8 %copy-start.2 = (bf16[2,128,640]{2,1,0:T(8,128)(2,1)S(1)}, bf16[2,128,640]{2,1,0:T(8,128)(2,1)}, u32[]{:S(2)}) copy-start(bf16[2,128,640]{2,1,0:T(8,128)(2,1)} %weight_ref.3) | copy-start | bytes 983044
  28.6 58.8 %copy-start.6 = (bf16[2,128,128]{2,1,0:T(8,128)(2,1)S(1)}, bf16[2,128,128]{2,1,0:T(8,128)(2,1)}, u32[]{:S(2)}) copy-start(bf16[2,128,128]{2,1,0:T(8,128)(2,1)} %out_weight_ref.3) | copy-start | bytes 196612
  28.6 58.8 %copy-start.10 = (s32[1,512]{1,0:T(1,128)S(1)}, s32[1,512]{1,0:T(1,128)}, u32[]{:S(2)}) copy-start(s32[1,512]{1,0:T(1,128)} %mask_ref.2) | copy-start | bytes 6148
  28.6 3.7 %collective-permute-start = (bf16[16,16,128]{2,1,0:T(8,128)(2,1)}, bf16[16,16,128]{2,1,0:T(8,128)(2,1)S(1)}, u32[]{:S(2)}, u32[]{:S(2)}) collective-permute-start(bf16[16,16,128]{2,1,0:T(8,128)(2,1)} %bias.1), channel_id=1, source_target_pairs={{0,128},{128,0},{1,129},{129,1},{2,130},{130,2},{3,131},{131,3},{4... | collective-permute-start | bytes 196616 | tf_op jit(solution)/shard_map/ppermute | solution.py:462
  45.5 5.6 %collective-permute-start.1 = (bf16[8,8,2,16,128]{4,3,2,1,0:T(8,128)(2,1)S(1)}, bf16[8,8,2,16,128]{4,3,2,1,0:T(8,128)(2,1)S(1)}, u32[]{:S(2)}, u32[]{:S(2)}) collective-permute-start(bf16[8,8,2,16,128]{4,3,2,1,0:T(8,128)(2,1)S(1)} %take_right.1), channel_id=1, source_target_pairs={{0,8},{8,0},{1,9},{9,1},{2,10},{10,2},{3,11},{11,3},{4,12},{12,4},... | collective-permute-start | bytes 1572872 | tf_op jit(solution)/shard_map/ppermute | solution.py:404
  53.9 33.4 %all-to-all-start.1 = ((bf16[64,64,128]{2,1,0:T(8,128)(2,1)}), bf16[64,64,128]{2,1,0:T(8,128)(2,1)S(1)}, u32[]{:S(2)}, u32[]{:S(2)}) async-start(bf16[64,64,128]{2,1,0:T(8,128)(2,1)} %bitcast.12), calls=%async_computation.1 | async-start | bytes 2097152 | tf_op jit(solution)/shard_map/all_to_all | solution.py:408
  60.7 6.5 %collective-permute-start.2 = (bf16[288,128]{1,0:T(8,128)(2,1)S(1)}, bf16[288,128]{1,0:T(8,128)(2,1)S(1)}, u32[]{:S(2)}, u32[]{:S(2)}) collective-permute-start(bf16[288,128]{1,0:T(8,128)(2,1)S(1)} %copy-done.33), channel_id=1, source_target_pairs={{0,1},{1,0},{2,3},{3,2},{4,5},{5,4},{6,7},{7,6},{8,9},{9,8},{10,11... | collective-permute-start | bytes 221192 | tf_op jit(solution)/shard_map/ppermute | solution.py:413
  61.8 11.4 %collective-permute-start.3 = (bf16[288,128]{1,0:T(8,128)(2,1)S(1)}, bf16[288,128]{1,0:T(8,128)(2,1)S(1)}, u32[]{:S(2)}, u32[]{:S(2)}) collective-permute-start(bf16[288,128]{1,0:T(8,128)(2,1)S(1)} %copy-done.32), channel_id=1, source_target_pairs={{0,2},{1,3},{2,0},{3,1},{4,6},{5,7},{6,4},{7,5},{8,10},{9,11},{10,... | collective-permute-start | bytes 221192 | tf_op jit(solution)/shard_map/ppermute | solution.py:413
  64.2 9.8 %collective-permute-start.4 = (bf16[288,128]{1,0:T(8,128)(2,1)S(1)}, bf16[288,128]{1,0:T(8,128)(2,1)S(1)}, u32[]{:S(2)}, u32[]{:S(2)}) collective-permute-start(bf16[288,128]{1,0:T(8,128)(2,1)S(1)} %copy-done.31), channel_id=1, source_target_pairs={{0,3},{1,2},{2,1},{3,0},{4,7},{5,6},{6,5},{7,4},{8,11},{9,10},{10,... | collective-permute-start | bytes 221192 | tf_op jit(solution)/shard_map/ppermute | solution.py:413
  64.7 9.3 %collective-permute-start.5 = (bf16[288,128]{1,0:T(8,128)(2,1)S(1)}, bf16[288,128]{1,0:T(8,128)(2,1)S(1)}, u32[]{:S(2)}, u32[]{:S(2)}) collective-permute-start(bf16[288,128]{1,0:T(8,128)(2,1)S(1)} %copy-done.30), channel_id=1, source_target_pairs={{0,4},{1,5},{2,6},{3,7},{4,0},{5,1},{6,2},{7,3},{8,12},{9,13},{10,... | collective-permute-start | bytes 221192 | tf_op jit(solution)/shard_map/ppermute | solution.py:413
  67.2 7.2 %collective-permute-start.6 = (bf16[288,128]{1,0:T(8,128)(2,1)S(1)}, bf16[288,128]{1,0:T(8,128)(2,1)S(1)}, u32[]{:S(2)}, u32[]{:S(2)}) collective-permute-start(bf16[288,128]{1,0:T(8,128)(2,1)S(1)} %copy-done.29), channel_id=1, source_target_pairs={{0,5},{1,4},{2,7},{3,6},{4,1},{5,0},{6,3},{7,2},{8,13},{9,12},{10,... | collective-permute-start | bytes 221192 | tf_op jit(solution)/shard_map/ppermute | solution.py:413
  67.2 14.9 %copy-start.13 = (bf16[288,128]{1,0:T(8,128)(2,1)}, bf16[288,128]{1,0:T(8,128)(2,1)S(1)}, u32[]{:S(2)}) copy-start(bf16[288,128]{1,0:T(8,128)(2,1)S(1)} %collective-permute-done.2.refs_0_.refs_1_) | copy-start | bytes 221188
  67.2 9.9 %collective-permute-start.7 = (bf16[288,128]{1,0:T(8,128)(2,1)S(1)}, bf16[288,128]{1,0:T(8,128)(2,1)S(1)}, u32[]{:S(2)}, u32[]{:S(2)}) collective-permute-start(bf16[288,128]{1,0:T(8,128)(2,1)S(1)} %copy-done.28), channel_id=1, source_target_pairs={{0,6},{1,7},{2,4},{3,5},{4,2},{5,3},{6,0},{7,1},{8,14},{9,15},{10,... | collective-permute-start | bytes 221192 | tf_op jit(solution)/shard_map/ppermute | solution.py:413
  73.3 8.8 %copy-start.14 = (bf16[288,128]{1,0:T(8,128)(2,1)}, bf16[288,128]{1,0:T(8,128)(2,1)S(1)}, u32[]{:S(2)}) copy-start(bf16[288,128]{1,0:T(8,128)(2,1)S(1)} %collective-permute-done.3.refs_1_.refs_2_) | copy-start | bytes 221188
  73.3 8.8 %collective-permute-start.8 = (bf16[288,128]{1,0:T(8,128)(2,1)S(1)}, bf16[288,128]{1,0:T(8,128)(2,1)S(1)}, u32[]{:S(2)}, u32[]{:S(2)}) collective-permute-start(bf16[288,128]{1,0:T(8,128)(2,1)S(1)} %copy-done.27), channel_id=1, source_target_pairs={{0,7},{1,6},{2,5},{3,4},{4,3},{5,2},{6,1},{7,0},{8,15},{9,14},{10,... | collective-permute-start | bytes 221192 | tf_op jit(solution)/shard_map/ppermute | solution.py:413
  74.0 8.1 %copy-start.15 = (bf16[288,128]{1,0:T(8,128)(2,1)}, bf16[288,128]{1,0:T(8,128)(2,1)S(1)}, u32[]{:S(2)}) copy-start(bf16[288,128]{1,0:T(8,128)(2,1)S(1)} %collective-permute-done.4.refs_2_.refs_3_) | copy-start | bytes 221188
  74.0 8.1 %copy-start.16 = (bf16[288,128]{1,0:T(8,128)(2,1)}, bf16[288,128]{1,0:T(8,128)(2,1)S(1)}, u32[]{:S(2)}) copy-start(bf16[288,128]{1,0:T(8,128)(2,1)S(1)} %collective-permute-done.5.refs_3_.refs_4_) | copy-start | bytes 221188
  74.4 7.7 %copy-start.17 = (bf16[288,128]{1,0:T(8,128)(2,1)}, bf16[288,128]{1,0:T(8,128)(2,1)S(1)}, u32[]{:S(2)}) copy-start(bf16[288,128]{1,0:T(8,128)(2,1)S(1)} %collective-permute-done.6.refs_4_.refs_5_) | copy-start | bytes 221188
  77.2 5.0 %copy-start.18 = (bf16[288,128]{1,0:T(8,128)(2,1)}, bf16[288,128]{1,0:T(8,128)(2,1)S(1)}, u32[]{:S(2)}) copy-start(bf16[288,128]{1,0:T(8,128)(2,1)S(1)} %collective-permute-done.7.refs_5_.refs_6_) | copy-start | bytes 221188
  82.2 0.6 copy-start.19
  83.4 0.7 copy-start.9
  84.1 43.1 %copy-start.8 = (s32[5]{0:T(128)S(1)}, s32[5]{0:T(128)}, u32[]{:S(2)}) copy-start(s32[5]{0:T(128)} %stack.23.place_ref) | copy-start | bytes 64
  87.4 17.4 %copy-start = (bf16[64,64,128]{2,1,0:T(8,128)(2,1)}, bf16[64,64,128]{2,1,0:T(8,128)(2,1)S(1)}, u32[]{:S(2)}) copy-start(bf16[64,64,128]{2,1,0:T(8,128)(2,1)S(1)} %all-to-all-done.1.recv_ref) | copy-start | bytes 3145732
  90.5 1.0 copy-start.3
  91.5 1.0 copy-start.5
  92.5 34.7 %all-to-all-start.2 = ((bf16[64,64,128]{2,1,0:T(8,128)(2,1)}), bf16[64,64,128]{2,1,0:T(8,128)(2,1)S(1)}, u32[]{:S(2)}, u32[]{:S(2)}) async-start(bf16[64,64,128]{2,1,0:T(8,128)(2,1)} %bitcast.26), calls=%async_computation.2 | async-start | bytes 2097152 | tf_op jit(solution)/shard_map/all_to_all | solution.py:408
  101.4 3.3 %collective-permute-start.9 = (bf16[64,32,128]{2,1,0:T(8,128)(2,1)S(1)}, bf16[64,32,128]{2,1,0:T(8,128)(2,1)S(1)}, u32[]{:S(2)}, u32[]{:S(2)}) collective-permute-start(bf16[64,32,128]{2,1,0:T(8,128)(2,1)S(1)} %slice.4), channel_id=1, source_target_pairs={{0,8},{8,0},{1,9},{9,1},{2,10},{10,2},{3,11},{11,3},{4,12},{12,4},... | collective-permute-start | bytes 1572872 | tf_op jit(solution)/shard_map/ppermute | solution.py:404
  104.8 0.8 copy-start.12
  111.3 6.8 %collective-permute-start.10 = (bf16[96,128]{1,0:T(8,128)(2,1)}, bf16[96,128]{1,0:T(8,128)(2,1)S(1)}, u32[]{:S(2)}, u32[]{:S(2)}) collective-permute-start(bf16[96,128]{1,0:T(8,128)(2,1)} %get-tuple-element.35), channel_id=1, source_target_pairs={{0,1},{1,0},{2,3},{3,2},{4,5},{5,4},{6,7},{7,6},{8,9},{9,8},{10,11... | collective-permute-start | bytes 73736 | tf_op jit(solution)/shard_map/ppermute | solution.py:413
  112.7 5.7 %collective-permute-start.11 = (bf16[96,128]{1,0:T(8,128)(2,1)}, bf16[96,128]{1,0:T(8,128)(2,1)S(1)}, u32[]{:S(2)}, u32[]{:S(2)}) collective-permute-start(bf16[96,128]{1,0:T(8,128)(2,1)} %get-tuple-element.36), channel_id=1, source_target_pairs={{0,2},{1,3},{2,0},{3,1},{4,6},{5,7},{6,4},{7,5},{8,10},{9,11},{10,... | collective-permute-start | bytes 73736 | tf_op jit(solution)/shard_map/ppermute | solution.py:413
  115.1 4.4 %collective-permute-start.12 = (bf16[96,128]{1,0:T(8,128)(2,1)}, bf16[96,128]{1,0:T(8,128)(2,1)S(1)}, u32[]{:S(2)}, u32[]{:S(2)}) collective-permute-start(bf16[96,128]{1,0:T(8,128)(2,1)} %get-tuple-element.37), channel_id=1, source_target_pairs={{0,3},{1,2},{2,1},{3,0},{4,7},{5,6},{6,5},{7,4},{8,11},{9,10},{10,... | collective-permute-start | bytes 73736 | tf_op jit(solution)/shard_map/ppermute | solution.py:413
  115.3 5.9 %collective-permute-start.13 = (bf16[96,128]{1,0:T(8,128)(2,1)}, bf16[96,128]{1,0:T(8,128)(2,1)S(1)}, u32[]{:S(2)}, u32[]{:S(2)}) collective-permute-start(bf16[96,128]{1,0:T(8,128)(2,1)} %get-tuple-element.38), channel_id=1, source_target_pairs={{0,4},{1,5},{2,6},{3,7},{4,0},{5,1},{6,2},{7,3},{8,12},{9,13},{10,... | collective-permute-start | bytes 73736 | tf_op jit(solution)/shard_map/ppermute | solution.py:413
  118.1 5.6 %collective-permute-start.14 = (bf16[96,128]{1,0:T(8,128)(2,1)}, bf16[96,128]{1,0:T(8,128)(2,1)S(1)}, u32[]{:S(2)}, u32[]{:S(2)}) collective-permute-start(bf16[96,128]{1,0:T(8,128)(2,1)} %get-tuple-element.39), channel_id=1, source_target_pairs={{0,5},{1,4},{2,7},{3,6},{4,1},{5,0},{6,3},{7,2},{8,13},{9,12},{10,... | collective-permute-start | bytes 73736 | tf_op jit(solution)/shard_map/ppermute | solution.py:413
  118.1 5.6 %copy-start.20 = (bf16[96,128]{1,0:T(8,128)(2,1)}, bf16[96,128]{1,0:T(8,128)(2,1)S(1)}, u32[]{:S(2)}) copy-start(bf16[96,128]{1,0:T(8,128)(2,1)S(1)} %collective-permute-done.10.refs_0_.refs_1_) | copy-start | bytes 73732
  118.4 5.3 %copy-start.21 = (bf16[96,128]{1,0:T(8,128)(2,1)}, bf16[96,128]{1,0:T(8,128)(2,1)S(1)}, u32[]{:S(2)}) copy-start(bf16[96,128]{1,0:T(8,128)(2,1)S(1)} %collective-permute-done.11.refs_1_.refs_2_) | copy-start | bytes 73732
  119.5 4.2 %copy-start.22 = (bf16[96,128]{1,0:T(8,128)(2,1)}, bf16[96,128]{1,0:T(8,128)(2,1)S(1)}, u32[]{:S(2)}) copy-start(bf16[96,128]{1,0:T(8,128)(2,1)S(1)} %collective-permute-done.12.refs_2_.refs_3_) | copy-start | bytes 73732
  121.2 2.5 %copy-start.23 = (bf16[96,128]{1,0:T(8,128)(2,1)}, bf16[96,128]{1,0:T(8,128)(2,1)S(1)}, u32[]{:S(2)}) copy-start(bf16[96,128]{1,0:T(8,128)(2,1)S(1)} %collective-permute-done.13.refs_3_.refs_4_) | copy-start | bytes 73732
  123.7 0.6 copy-start.24
  127.2 0.7 copy-start.11
  129.8 6.0 %collective-permute-start.15 = (bf16[8,8,32,128]{3,2,1,0:T(8,128)(2,1)S(1)}, bf16[8,8,32,128]{3,2,1,0:T(8,128)(2,1)S(1)}, u32[]{:S(2)}, u32[]{:S(2)}) collective-permute-start(bf16[8,8,32,128]{3,2,1,0:T(8,128)(2,1)S(1)} %get-tuple-element.41), channel_id=1, source_target_pairs={{0,8},{8,0},{1,9},{9,1},{2,10},{10,2},{3,11},{11,3},{4,12},{12,4},... | collective-permute-start | bytes 1572872 | tf_op jit(solution)/shard_map/ppermute | solution.py:404
  136.8 23.2 %all-to-all-start.3 = ((bf16[64,32,128]{2,1,0:T(8,128)(2,1)}), bf16[64,32,128]{2,1,0:T(8,128)(2,1)S(1)}, u32[]{:S(2)}, u32[]{:S(2)}) async-start(bf16[64,32,128]{2,1,0:T(8,128)(2,1)} %bitcast.17), calls=%async_computation.3 | async-start | bytes 1048576 | tf_op jit(solution)/shard_map/all_to_all | solution.py:408
  143.5 8.0 %collective-permute-start.16 = (bf16[96,128]{1,0:T(8,128)(2,1)}, bf16[96,128]{1,0:T(8,128)(2,1)S(1)}, u32[]{:S(2)}, u32[]{:S(2)}) collective-permute-start(bf16[96,128]{1,0:T(8,128)(2,1)} %get-tuple-element.48), channel_id=1, source_target_pairs={{0,6},{1,7},{2,4},{3,5},{4,2},{5,3},{6,0},{7,1},{8,14},{9,15},{10,... | collective-permute-start | bytes 73736 | tf_op jit(solution)/shard_map/ppermute | solution.py:413
  148.5 6.8 %collective-permute-start.17 = (bf16[96,128]{1,0:T(8,128)(2,1)}, bf16[96,128]{1,0:T(8,128)(2,1)S(1)}, u32[]{:S(2)}, u32[]{:S(2)}) collective-permute-start(bf16[96,128]{1,0:T(8,128)(2,1)} %get-tuple-element.49), channel_id=1, source_target_pairs={{0,7},{1,6},{2,5},{3,4},{4,3},{5,2},{6,1},{7,0},{8,15},{9,14},{10,... | collective-permute-start | bytes 73736 | tf_op jit(solution)/shard_map/ppermute | solution.py:413
  149.4 1.2 copy-start.4
  151.5 3.8 %copy-start.25 = (bf16[96,128]{1,0:T(8,128)(2,1)}, bf16[96,128]{1,0:T(8,128)(2,1)S(1)}, u32[]{:S(2)}) copy-start(bf16[96,128]{1,0:T(8,128)(2,1)S(1)} %collective-permute-done.16.refs_6_) | copy-start | bytes 73732
  155.4 0.6 copy-start.26
